TPU v7x, 256 devices: a whole 4x4x8 slice. The times are simulated.
256 devices in a mesh: dp: 4 (over x), section: 4 (over y), tensor: 16 (over z, core).
Axes of the slice: x: 4, y: 4, z: 8, core: 2. Of those that a mesh axis runs over, the one named last changes fastest.
Arguments:
- hidden_in: bfloat16 [2, 128, 8192], P(None, 'dp'), parts along dimension 1, may hold values from -3 to 3
- queries: bfloat16 [4, 2, 128, 8192], P('section', None, 'dp', 'tensor'), parts along dimension 2, may hold values from -16 to 16
- new_keys: bfloat16 [4, 2, 128, 2048], P('section', None, 'dp', 'tensor'), parts along dimension 2, may hold values from -6 to 6, as said below
- new_values: bfloat16 [4, 2, 128, 2048], P('section', None, 'dp', 'tensor'), parts along dimension 2, may hold values from -6 to 6, as said below
- cache_keys: bfloat16 [4, 128, 384, 2048], P('section', 'dp', None, 'tensor'), parts along dimension 1, may hold values from -12 to 12, as said below
- cache_values: bfloat16 [4, 128, 384, 2048], P('section', 'dp', None, 'tensor'), parts along dimension 1, may hold values from -6 to 6, as said below
- out_weight: bfloat16 [4, 8192, 8192], P('section', 'tensor'), may hold values from -0.75 to 0.75
- cache_lengths: int32 [128], P('dp'), parts along dimension 0, may hold values from 2 to 384, as said below
- positions: int32 [128], P('dp'), parts along dimension 0, may hold values from 2 to 767, as said below
Outputs:
- section_states: bfloat16 [4, 2, 128, 8192], P('section', None, 'dp'), parts along dimension 2
There are 4 independent parts, one for each index of `dp`. A program takes and returns all parts, laid end to end along the dimension named above; an argument that names none is the same for every part. Nothing has to cross between parts.
Inputs may be any that keep to these rules, and one draw needn't show every extreme that they name: `cache_keys`: column blocks 2 t and 2 t + 1 of 128 entries are equal: two devices hold copies of one key-value head. `cache_values`: column blocks 2 t and 2 t + 1 of 128 entries are equal. `new_keys`: column blocks 2 t and 2 t + 1 of 128 entries are equal. `new_values`: column blocks 2 t and 2 t + 1 of 128 entries are equal. `cache_lengths`: some sequence fills all 384 slots. `positions`: each sequence's position is at least its cache length.
All inputs are finite; a program needn't handle non-finite values. Where the computation divides by a largest or mean magnitude, that divisor is 1e-20 or more.
Results may differ from a plain program's by a relative error of at most 0.02.
Values may be sent and summed in bfloat16 or wider, within the bound.
No kernel may reach another device: no remote copies, remote signals or barrier semaphores. Data moves between devices by JAX's collectives and lax.ppermute only.
A program may use at most 128 MiB of HBM per device.

v0:
```python
import jax
import jax.numpy as jnp
from jax import lax
from jax.sharding import PartitionSpec as P

BLOCK = 128


def from_behind(array, axis, by):
    size = lax.axis_size(axis)
    pairs = [(i, i + by) for i in range(size) if 0 <= i + by < size]
    return lax.ppermute(array, axis, pairs)


def rotate(values, where_at):
    half = values.shape[-1] // 2
    rates = 500000.0 ** (-jnp.arange(half, dtype=jnp.float32) * 2.0 / values.shape[-1])
    angles = where_at[..., None] * rates
    cosine = jnp.cos(angles)
    sine = jnp.sin(angles)
    first = values[..., :half]
    second = values[..., half:]
    return jnp.concatenate(
        [first * cosine - second * sine, second * cosine + first * sine], axis=-1
    )


def encode_blocks(blocks):
    block_scale = (jnp.max(jnp.abs(blocks), axis=-1) + 1e-06).astype(jnp.bfloat16)
    code_words = (blocks / block_scale.astype(jnp.float32)[..., None]).astype(jnp.bfloat16)
    return (code_words, block_scale)


def decode_blocks(code_words, block_scale):
    return code_words.astype(jnp.float32) * block_scale.astype(jnp.float32)[..., None]


def per_device(
    hidden_in,
    queries,
    new_keys,
    new_values,
    cache_keys,
    cache_values,
    out_weight,
    cache_lengths,
    positions,
):
    parts = lax.axis_size("tensor")
    section_count = lax.axis_size("section")
    step_count, row_count, model_width = hidden_in.shape
    head_size = cache_keys.shape[3]
    group_size = queries.shape[3] // head_size
    length = cache_keys.shape[2]
    share = model_width // parts
    block_count = share // BLOCK
    flat_rows = step_count * row_count
    angle_rows = (
        positions.astype(jnp.float32)[None, :] + jnp.arange(step_count, dtype=jnp.float32)[:, None]
    )
    query_rot = rotate(
        queries[0].astype(jnp.float32).reshape(step_count, row_count, group_size, head_size),
        angle_rows[:, :, None],
    ).astype(jnp.bfloat16)
    key_rot = rotate(new_keys[0].astype(jnp.float32), angle_rows).astype(jnp.bfloat16)
    factor = head_size ** (-0.5)
    past_scores = (
        jnp.einsum("srgd,rld->srgl", query_rot, cache_keys[0], preferred_element_type=jnp.float32)
        * factor
    )
    visible = jnp.arange(length, dtype=jnp.int32)[None, :] < cache_lengths[:, None]
    past_scores = jnp.where(visible[None, :, None, :], past_scores, -jnp.inf)
    fresh_scores = (
        jnp.einsum("srgd,mrd->srgm", query_rot, key_rot, preferred_element_type=jnp.float32)
        * factor
    )
    causal = (
        jnp.arange(step_count, dtype=jnp.int32)[:, None]
        >= jnp.arange(step_count, dtype=jnp.int32)[None, :]
    )
    fresh_scores = jnp.where(causal[:, None, None, :], fresh_scores, -jnp.inf)
    highest = jnp.maximum(past_scores.max(-1), fresh_scores.max(-1))[..., None]
    past_exp = jnp.exp(past_scores - highest)
    fresh_exp = jnp.exp(fresh_scores - highest)
    total = past_exp.sum(-1, keepdims=True) + fresh_exp.sum(-1, keepdims=True)
    past_weights = (past_exp / total).astype(jnp.bfloat16)
    fresh_weights = (fresh_exp / total).astype(jnp.bfloat16)
    attended = jnp.einsum(
        "srgl,rld->srgd", past_weights, cache_values[0], preferred_element_type=jnp.float32
    )
    attended = attended + jnp.einsum(
        "srgm,mrd->srgd", fresh_weights, new_values[0], preferred_element_type=jnp.float32
    )
    attended = attended.astype(jnp.bfloat16).reshape(flat_rows, group_size * head_size)
    partial_value = jnp.dot(attended, out_weight[0], preferred_element_type=jnp.float32)
    code_words, block_scale = encode_blocks(
        partial_value.reshape(flat_rows, model_width // BLOCK, BLOCK)
    )
    got_codes, got_scale = (
        lax.all_to_all(
            code_words.reshape(flat_rows, parts, block_count, BLOCK),
            "tensor",
            split_axis=1,
            concat_axis=1,
            tiled=True,
        ),
        lax.all_to_all(
            block_scale.reshape(flat_rows, parts, block_count),
            "tensor",
            split_axis=1,
            concat_axis=1,
            tiled=True,
        ),
    )
    summed = jnp.sum(decode_blocks(got_codes, got_scale), axis=1)
    sum_codes, sum_scale = encode_blocks(summed)
    section_index = lax.axis_index("section")
    all_codes, all_scale = (
        lax.all_gather(sum_codes, "tensor", axis=1, tiled=True),
        lax.all_gather(sum_scale, "tensor", axis=1, tiled=True),
    )
    update = decode_blocks(all_codes, all_scale).reshape(step_count, row_count, model_width)
    current = (hidden_in.astype(jnp.float32) + update).astype(jnp.bfloat16)
    for handed in range(1, section_count):
        incoming = from_behind(current, "section", 1)
        current = jnp.where(
            section_index == handed,
            (incoming.astype(jnp.float32) + update).astype(jnp.bfloat16),
            current,
        )
    return current[None]


def solution(mesh):
    placed = (
        P(None, "dp", None),
        P("section", None, "dp", "tensor"),
        P("section", None, "dp", "tensor"),
        P("section", None, "dp", "tensor"),
        P("section", "dp", None, "tensor"),
        P("section", "dp", None, "tensor"),
        P("section", "tensor", None),
        P("dp"),
        P("dp"),
    )
    return jax.shard_map(
        per_device,
        mesh=mesh,
        in_specs=placed,
        out_specs=P("section", None, "dp", None),
        check_vma=False,
    )
```

profile of v0, /device:TPU:1, one launch (start us, length us, event | category | flops | bytes accessed | tf_op | source)
XLA Modules:
  0.0 227.6 jit_solution(9940766607748301929)
XLA Ops:
  11.2 1.4 fusion.39
  14.2 12.0 %copy.58 = bf16[8192,512]{1,0:T(8,128)(2,1)} copy(bf16[8192,512]{0,1:T(8,128)(2,1)} %bitcast.66) | data formatting | bytes 16777216 | tf_op jit(solution)/shard_map/dot_general | solution.py:95
  26.2 7.4 %abs_reduce_fusion = (f32[64,64]{0,1:T(8,128)S(1)}, f32[64,64,128]{2,0,1:T(8,128)}) fusion(bf16[64,512,1]{1,0,2:T(8,128)(2,1)S(1)} %reshape.142, bf16[64,128,512]{2,1,0:T(8,128)(2,1)} %bitcast.65), kind=kOutput, calls=%fused_computation.11 | convolution fusion | flops 537915392 | bytes 10567680 | tf_op jit(solution)/shard_map/dot_general | solution.py:95
  34.3 10.0 %all-to-all-start.1 = ((bf16[16,2,128]{2,1,0:T(2,128)(2,1)}), bf16[16,2,128]{2,1,0:T(2,128)(2,1)S(1)}, u32[]{:S(2)}, u32[]{:S(2)}) async-start(bf16[16,2,128]{2,1,0:T(2,128)(2,1)} %reshape.145), calls=%async_computation.1 | async-start | bytes 16384 | tf_op jit(solution)/shard_map/all_to_all | solution.py:107
  44.3 2.7 %divide_convert_fusion = bf16[64,64,128]{2,0,1:T(8,128)(2,1)} fusion(f32[64,64,128]{2,0,1:T(8,128)} %get-tuple-element.24, f32[64,64]{0,1:T(8,128)S(1)} %get-tuple-element.5), kind=kLoop, calls=%fused_computation.10 | loop fusion | flops 1048576 | bytes 3162112 | tf_op jit(solution)/shard_map/convert_element_type | solution.py:30
  47.0 4.3 %all-to-all-done.1 = bf16[16,2,128]{2,1,0:T(2,128)(2,1)S(1)} async-done(((bf16[16,2,128]{2,1,0:T(2,128)(2,1)}), bf16[16,2,128]{2,1,0:T(2,128)(2,1)S(1)}, u32[]{:S(2)}, u32[]{:S(2)}) %all-to-all-start.1) | async-done | bytes 8224 | tf_op jit(solution)/shard_map/all_to_all | solution.py:107
  51.3 4.7 %all-to-all-start = ((bf16[64,16,4,128]{3,0,2,1:T(8,128)(2,1)}), bf16[64,16,4,128]{3,0,2,1:T(8,128)(2,1)}, u32[]{:S(2)}, u32[]{:S(2)}) async-start(bf16[64,16,4,128]{3,0,2,1:T(8,128)(2,1)} %bitcast.67), calls=%async_computation | async-start | bytes 2097152 | tf_op jit(solution)/shard_map/all_to_all | solution.py:100
  56.2 27.9 %all-to-all-done = bf16[64,16,4,128]{3,0,2,1:T(8,128)(2,1)} async-done(((bf16[64,16,4,128]{3,0,2,1:T(8,128)(2,1)}), bf16[64,16,4,128]{3,0,2,1:T(8,128)(2,1)}, u32[]{:S(2)}, u32[]{:S(2)}) %all-to-all-start) | async-done | bytes 1048608 | tf_op jit(solution)/shard_map/all_to_all | solution.py:100
  84.1 1.7 multiply_reduce_fusion
  86.8 14.5 %all-gather = bf16[16,4,64]{2,1,0:T(4,128)(2,1)S(1)} all-gather(bf16[1,4,64]{2,1,0:T(4,128)(2,1)S(1)} %get-tuple-element.13), channel_id=1, replica_groups=mesh['dp'=4,'section'=4,'tensor'=16] {'tensor'}, dimensions={0}, use_global_device_ids=true | all-gather | bytes 8704 | tf_op jit(solution)/shard_map/all_gather | solution.py:120
  101.2 22.0 %all-gather.3.cloned.1.call-done = bf16[64,64,128]{2,0,1:T(8,128)(2,1)} async-done(((bf16[64,4,128]{2,0,1:T(8,128)(2,1)}), bf16[64,64,128]{2,0,1:T(8,128)(2,1)}) %all-gather.3.cloned.1.call-update) | async-done | bytes 1048592 | tf_op jit(solution)/shard_map/all_gather | solution.py:119
  123.3 1.8 convert_multiply_fusion
  125.1 2.5 %copy.48 = f32[64,64,128]{2,1,0:T(8,128)} copy(f32[64,64,128]{2,0,1:T(8,128)S(1)} %convert_multiply_fusion) | data formatting | bytes 4194304 | tf_op jit(solution)/shard_map/mul | solution.py:35
  127.6 2.8 %reshape.132 = f32[2,32,8192]{2,1,0:T(8,128)} reshape(f32[64,64,128]{2,1,0:T(8,128)} %copy.48) | data formatting | bytes 4194304 | tf_op jit(solution)/shard_map/reshape | solution.py:122
  130.4 3.0 %add_convert_fusion.3 = bf16[2,32,8192]{2,1,0:T(8,128)(2,1)} fusion(f32[2,32,8192]{2,1,0:T(8,128)} %reshape.132, bf16[2,32,8192]{2,1,0:T(8,128)(2,1)} %param.9), kind=kLoop, calls=%fused_computation.7 | loop fusion | flops 1572864 | bytes 4194304 | tf_op jit(solution)/shard_map/convert_element_type | solution.py:123
  133.4 4.1 %collective-permute-start = (bf16[2,32,8192]{2,1,0:T(8,128)(2,1)}, bf16[2,32,8192]{2,1,0:T(8,128)(2,1)}, u32[]{:S(2)}, u32[]{:S(2)}) collective-permute-start(bf16[2,32,8192]{2,1,0:T(8,128)(2,1)} %add_convert_fusion.3), channel_id=1, source_target_pairs={{0,16},{16,32},{32,48},{1,17},{17,33},{33,49},{2,18},{18,34},{34,5... | collective-permute-start | bytes 3145736 | tf_op jit(solution)/shard_map/ppermute | solution.py:12
  137.5 21.6 %collective-permute-done = bf16[2,32,8192]{2,1,0:T(8,128)(2,1)} collective-permute-done((bf16[2,32,8192]{2,1,0:T(8,128)(2,1)}, bf16[2,32,8192]{2,1,0:T(8,128)(2,1)}, u32[]{:S(2)}, u32[]{:S(2)}) %collective-permute-start) | collective-permute-done | bytes 1048608 | tf_op jit(solution)/shard_map/ppermute | solution.py:12
  159.1 3.5 %fusion.24 = bf16[2,32,8192]{2,1,0:T(8,128)(2,1)} fusion(f32[2,32,8192]{2,1,0:T(8,128)} %reshape.132, bf16[2,32,8192]{2,1,0:T(8,128)(2,1)} %collective-permute-done, pred[]{:T(512)S(6)} %eq.11, bf16[2,32,8192]{2,1,0:T(8,128)(2,1)} %param.9), kind=kLoop, calls=%fused_computation.21 | loop fusion | flops 3670016 | bytes 5242881 | tf_op jit(solution)/shard_map/jit(_where)/select_n | solution.py:126
  162.6 5.1 %collective-permute-start.1 = (bf16[2,32,8192]{2,1,0:T(8,128)(2,1)}, bf16[2,32,8192]{2,1,0:T(8,128)(2,1)}, u32[]{:S(2)}, u32[]{:S(2)}) collective-permute-start(bf16[2,32,8192]{2,1,0:T(8,128)(2,1)} %fusion.24), channel_id=1, source_target_pairs={{0,16},{16,32},{32,48},{1,17},{17,33},{33,49},{2,18},{18,34},{34,5... | collective-permute-start | bytes 3145736 | tf_op jit(solution)/shard_map/ppermute | solution.py:12
  167.7 20.7 %collective-permute-done.1 = bf16[2,32,8192]{2,1,0:T(8,128)(2,1)} collective-permute-done((bf16[2,32,8192]{2,1,0:T(8,128)(2,1)}, bf16[2,32,8192]{2,1,0:T(8,128)(2,1)}, u32[]{:S(2)}, u32[]{:S(2)}) %collective-permute-start.1) | collective-permute-done | bytes 1048608 | tf_op jit(solution)/shard_map/ppermute | solution.py:12
  188.4 4.0 %fusion.25 = bf16[2,32,8192]{2,1,0:T(8,128)(2,1)} fusion(f32[2,32,8192]{2,1,0:T(8,128)} %reshape.132, bf16[2,32,8192]{2,1,0:T(8,128)(2,1)} %collective-permute-done.1, pred[]{:T(512)S(6)} %eq.10, bf16[2,32,8192]{2,1,0:T(8,128)(2,1)} %collective-permute-done, pred[]{:T(512)S(6)} %eq.11, bf16[2,32,8192]{2,1,0:T(8,128)(2,1)} %param.9), kind=kLoop, calls=%fused_computation.22 | loop fusion | flops 5767168 | bytes 6291458 | tf_op jit(solution)/shard_map/jit(_where)/select_n | solution.py:126
  192.4 5.1 %collective-permute-start.2 = (bf16[2,32,8192]{2,1,0:T(8,128)(2,1)}, bf16[2,32,8192]{2,1,0:T(8,128)(2,1)}, u32[]{:S(2)}, u32[]{:S(2)}) collective-permute-start(bf16[2,32,8192]{2,1,0:T(8,128)(2,1)} %fusion.25), channel_id=1, source_target_pairs={{0,16},{16,32},{32,48},{1,17},{17,33},{33,49},{2,18},{18,34},{34,5... | collective-permute-start | bytes 3145736 | tf_op jit(solution)/shard_map/ppermute | solution.py:12
  197.5 19.8 %collective-permute-done.2 = bf16[2,32,8192]{2,1,0:T(8,128)(2,1)} collective-permute-done((bf16[2,32,8192]{2,1,0:T(8,128)(2,1)}, bf16[2,32,8192]{2,1,0:T(8,128)(2,1)}, u32[]{:S(2)}, u32[]{:S(2)}) %collective-permute-start.2) | collective-permute-done | bytes 1048608 | tf_op jit(solution)/shard_map/ppermute | solution.py:12
  217.3 3.5 %fusion.27 = bf16[1,2,32,8192]{3,2,1,0:T(8,128)(2,1)} fusion(bf16[2,32,8192]{2,1,0:T(8,128)(2,1)} %fusion.25, f32[2,32,8192]{2,1,0:T(8,128)} %reshape.132, bf16[2,32,8192]{2,1,0:T(8,128)(2,1)} %collective-permute-done.2, pred[]{:T(512)S(6)} %eq.9), kind=kLoop, calls=%fused_computation.24 | loop fusion | flops 2097152 | bytes 5242881 | tf_op jit(solution)/shard_map/broadcast_in_dim | solution.py:131
  (38 shorter events, 7.9 us)
Async XLA Ops:
  6.5 4.6 %copy-start = (bf16[1,32,384,128]{3,2,1,0:T(8,128)(2,1)S(1)}, bf16[1,32,384,128]{3,2,1,0:T(8,128)(2,1)}, u32[]{:S(2)}) copy-start(bf16[1,32,384,128]{3,2,1,0:T(8,128)(2,1)} %param.13) | copy-start | bytes 9437188
  11.2 1.9 copy-start.2
  11.2 2.2 copy-start.1
  34.3 17.0 %all-to-all-start.1 = ((bf16[16,2,128]{2,1,0:T(2,128)(2,1)}), bf16[16,2,128]{2,1,0:T(2,128)(2,1)S(1)}, u32[]{:S(2)}, u32[]{:S(2)}) async-start(bf16[16,2,128]{2,1,0:T(2,128)(2,1)} %reshape.145), calls=%async_computation.1 | async-start | bytes 16384 | tf_op jit(solution)/shard_map/all_to_all | solution.py:107
  51.3 32.8 %all-to-all-start = ((bf16[64,16,4,128]{3,0,2,1:T(8,128)(2,1)}), bf16[64,16,4,128]{3,0,2,1:T(8,128)(2,1)}, u32[]{:S(2)}, u32[]{:S(2)}) async-start(bf16[64,16,4,128]{3,0,2,1:T(8,128)(2,1)} %bitcast.67), calls=%async_computation | async-start | bytes 2097152 | tf_op jit(solution)/shard_map/all_to_all | solution.py:100
  56.1 67.2 %all-gather.3.cloned.1.call-start = ((), (), s32[]{:S(2)}) async-start(), calls=%async_computation.2 | async-start | bytes 1114112 | tf_op jit(solution)/shard_map/all_gather | solution.py:119
  133.4 25.7 %collective-permute-start = (bf16[2,32,8192]{2,1,0:T(8,128)(2,1)}, bf16[2,32,8192]{2,1,0:T(8,128)(2,1)}, u32[]{:S(2)}, u32[]{:S(2)}) collective-permute-start(bf16[2,32,8192]{2,1,0:T(8,128)(2,1)} %add_convert_fusion.3), channel_id=1, source_target_pairs={{0,16},{16,32},{32,48},{1,17},{17,33},{33,49},{2,18},{18,34},{34,5... | collective-permute-start | bytes 3145736 | tf_op jit(solution)/shard_map/ppermute | solution.py:12
  162.6 25.8 %collective-permute-start.1 = (bf16[2,32,8192]{2,1,0:T(8,128)(2,1)}, bf16[2,32,8192]{2,1,0:T(8,128)(2,1)}, u32[]{:S(2)}, u32[]{:S(2)}) collective-permute-start(bf16[2,32,8192]{2,1,0:T(8,128)(2,1)} %fusion.24), channel_id=1, source_target_pairs={{0,16},{16,32},{32,48},{1,17},{17,33},{33,49},{2,18},{18,34},{34,5... | collective-permute-start | bytes 3145736 | tf_op jit(solution)/shard_map/ppermute | solution.py:12
  192.4 24.9 %collective-permute-start.2 = (bf16[2,32,8192]{2,1,0:T(8,128)(2,1)}, bf16[2,32,8192]{2,1,0:T(8,128)(2,1)}, u32[]{:S(2)}, u32[]{:S(2)}) collective-permute-start(bf16[2,32,8192]{2,1,0:T(8,128)(2,1)} %fusion.25), channel_id=1, source_target_pairs={{0,16},{16,32},{32,48},{1,17},{17,33},{33,49},{2,18},{18,34},{34,5... | collective-permute-start | bytes 3145736 | tf_op jit(solution)/shard_map/ppermute | solution.py:12
Sparse Core Ops, SparseCore 0:
  86.9 36.3 all-gather.2
where the time goes:
time: 231 us; the launch traced here: 228 us
  waiting for transfers between devices  116 us (50%)
  starting transfers between devices  29 us (13%)
  other arithmetic  24.4 us (11%)
  local copies, waits for them, and re-layouts  19.2 us (8%)
  blocking collectives  14.5 us (6%)
  between operations  13.6 us (6%)
  matrix products  10.6 us (5%)
    ppermute x3, waiting for transfers between devices, from_behind(): return lax.ppermute(array, axis, pairs)  62.1 us
    all_to_all x1, waiting for transfers between devices, per_device(): lax.all_to_all(code_words.reshape(flat_rows, parts, block_count, BLOCK),...  27.9 us
    all_gather x1, waiting for transfers between devices, per_device(): lax.all_gather(sum_codes, 'tensor', axis=1, tiled=True)  22 us
    all_gather x1, blocking collectives, per_device(): lax.all_gather(sum_scale, 'tensor', axis=1, tiled=True)  14.5 us
    ppermute x3, starting transfers between devices, from_behind(): return lax.ppermute(array, axis, pairs)  14.3 us
    dot_general x1, local copies, waits for them, and re-layouts, per_device(): jnp.dot(attended, out_weight[0], preferred_element_type=jnp.float32)  12 us
    all_to_all x1, starting transfers between devices, per_device(): lax.all_to_all(block_scale.reshape(flat_rows, parts, block_count), 'tenso...  9.98 us
    select_n x2, other arithmetic, per_device(): jnp.where(section_index == handed, (incoming.astype(jnp.float32) + update...  7.55 us
  transfers between devices with their start and end apart: 6, of which 6 were waited for; matrix products, arithmetic and copies ran while one was open for 1% of the time, Pallas kernels for 0%

commit v1 on v0

v1 whole, which is shorter than its diff:
```python
import jax
import jax.numpy as jnp
import numpy as np
from jax import lax
from jax.experimental import pallas as pl
from jax.experimental.pallas import tpu as pltpu
from jax.sharding import Mesh
from jax.sharding import PartitionSpec as P

CHUNK = 8


def attend_project(
    core_ref,
    length_ref,
    position_ref,
    rate_ref,
    query_ref,
    new_key_ref,
    new_value_ref,
    key_ref,
    value_ref,
    weight_ref,
    send_ref,
    keep_ref,
    angle,
    rotated,
    fresh0,
    fresh1,
    value0,
    value1,
    attended,
    weight,
    weight_sem,
):
    step = pl.program_id(0)
    steps, rows, _ = new_key_ref.shape[1:]
    head = new_key_ref.shape[3]
    group = query_ref.shape[3] // head
    per_row = steps * group
    blocks, _, width = send_ref.shape
    factor = head**-0.5
    core = core_ref[0]

    def fetch(side, block):
        half = (1 - core) if side == 0 else core
        column = pl.multiple_of((half * blocks + block) * width, width)
        return pltpu.make_async_copy(
            weight_ref.at[0, :, pl.ds(column, width)],
            weight.at[side * blocks + block],
            weight_sem.at[side * blocks + block],
        )

    @pl.when(step == 0)
    def _():
        for side in range(2):
            for block in range(blocks):
                fetch(side, block).start()
        rate = rate_ref[0:1, :]
        for row in range(rows):
            angle[row : row + 1, :] = position_ref[row].astype(jnp.float32) * jnp.ones_like(rate)
        sign = jnp.where(lax.broadcasted_iota(jnp.int32, (1, head), 1) < head // 2, -1.0, 1.0)
        cosines, sines = [], []
        for s in range(steps):
            turn = (angle[...] + float(s)) * rate
            cosines.append(jnp.cos(turn))
            sines.append(jnp.sin(turn) * sign)

        def rot(v, s):
            v = v.astype(jnp.float32)
            out = v * cosines[s] + pltpu.roll(v, head // 2, 1) * sines[s]
            return out.astype(jnp.bfloat16).astype(jnp.float32)

        keys = [rot(new_key_ref[0, s], s) for s in range(steps)]
        fresh = (fresh0, fresh1)
        fresh_values = (value0, value1)
        for s in range(steps):
            for g in range(group):
                k = s * group + g
                q = rot(query_ref[0, s, :, g * head : (g + 1) * head], s)
                at = pl.ds(k, rows, stride=per_row)
                rotated[at, :] = q
                for m in range(steps):
                    if m <= s:
                        score = jnp.sum(q * keys[m], axis=-1, keepdims=True) * factor
                        fresh[m][at, :] = jnp.broadcast_to(score, (rows, head))
                    else:
                        fresh[m][at, :] = jnp.full((rows, head), -jnp.inf, jnp.float32)
                    fresh_values[m][at, :] = new_value_ref[0, m].astype(jnp.float32)

    length = key_ref.shape[2]
    lane = lax.broadcasted_iota(jnp.int32, (per_row, length), 1)
    base = pl.multiple_of(step * (CHUNK * per_row), CHUNK * per_row)
    here = pl.ds(base, CHUNK * per_row)
    q_all = rotated[here, :].astype(jnp.bfloat16)
    scores = []
    for i in range(CHUNK):
        q = q_all[i * per_row : (i + 1) * per_row]
        score = lax.dot_general(
            q, key_ref[0, i], (((1,), (1,)), ((), ())), preferred_element_type=jnp.float32
        )
        visible = lane < length_ref[step * CHUNK + i]
        scores.append(jnp.where(visible, score * factor, -jnp.inf))
    scores = jnp.concatenate(scores, axis=0)
    new0 = fresh0[here, :]
    new1 = fresh1[here, :]
    highest = jnp.maximum(
        jnp.max(scores, axis=-1, keepdims=True), jnp.maximum(new0, new1)[:, 0:1]
    )
    past = jnp.exp(scores - highest)
    new0 = jnp.exp(new0 - highest)
    new1 = jnp.exp(new1 - highest)
    total = jnp.sum(past, axis=-1, keepdims=True) + (new0 + new1)[:, 0:1]
    past = (past / total).astype(jnp.bfloat16)
    new0 = (new0 / total).astype(jnp.bfloat16).astype(jnp.float32)
    new1 = (new1 / total).astype(jnp.bfloat16).astype(jnp.float32)
    results = []
    for i in range(CHUNK):
        results.append(
            jnp.dot(
                past[i * per_row : (i + 1) * per_row],
                value_ref[0, i],
                preferred_element_type=jnp.float32,
            )
        )
    attended[here, :] = (
        jnp.concatenate(results, axis=0) + new0 * value0[here, :] + new1 * value1[here, :]
    )

    @pl.when(step == pl.num_programs(0) - 1)
    def _():
        per_step = []
        for s in range(steps):
            per_step.append(
                jnp.concatenate(
                    [attended[pl.ds(s * group + g, rows, stride=per_row), :] for g in range(group)],
                    axis=1,
                )
            )
        left = jnp.concatenate(per_step, axis=0).astype(jnp.bfloat16)
        for block in range(blocks):
            fetch(0, block).wait()
            send_ref[block] = jnp.dot(
                left, weight[block], preferred_element_type=jnp.float32
            ).astype(send_ref.dtype)
        for block in range(blocks):
            fetch(1, block).wait()
            keep_ref[block] = jnp.dot(
                left, weight[blocks + block], preferred_element_type=jnp.float32
            )


def sum_blocks(got_ref, out_ref):
    total = got_ref[0].astype(jnp.float32)
    for i in range(1, got_ref.shape[0]):
        total = total + got_ref[i].astype(jnp.float32)
    out_ref[...] = total.astype(out_ref.dtype)


def add_sections(place_ref, hidden_ref, *refs):
    out_ref = refs[-1]
    rows = out_ref.shape[1]
    current = hidden_ref[...].reshape(rows, out_ref.shape[2]).astype(jnp.float32)
    for update in refs[:-1]:
        current = (current + update[...].astype(jnp.float32)).astype(jnp.bfloat16)
        current = current.astype(jnp.float32)
    current = current.astype(out_ref.dtype)
    for i in range(out_ref.shape[0]):
        out_ref[i] = current


def assemble(core_ref, own_ref, other_ref, out_ref):
    core = core_ref[0]
    blocks, _, width = own_ref.shape
    _, steps, rows, _ = out_ref.shape
    for block in range(blocks):
        at = pl.ds(pl.multiple_of((core * blocks + block) * width, width), width)
        out_ref[0, :, :, at] = own_ref[block].reshape(steps, rows, width)
        at = pl.ds(pl.multiple_of(((1 - core) * blocks + block) * width, width), width)
        out_ref[0, :, :, at] = other_ref[block].reshape(steps, rows, width)


VMEM = pl.BlockSpec(memory_space=pltpu.VMEM)
SMEM = pl.BlockSpec(memory_space=pltpu.SMEM)
SWAP = [(0, 1), (1, 0)]


def per_device(
    hidden_in,
    queries,
    new_keys,
    new_values,
    cache_keys,
    cache_values,
    out_weight,
    cache_lengths,
    positions,
):
    cores = lax.axis_size("core")
    chips = lax.axis_size("z")
    sections = lax.axis_size("section")
    steps, rows, model = hidden_in.shape
    length, head = cache_keys.shape[2:]
    group = queries.shape[3] // head
    depth = group * head
    share = model // (cores * chips)
    flat = steps * rows
    pairs = rows * steps * group
    core = lax.axis_index("core").astype(jnp.int32).reshape(1)
    half = head // 2
    rates = np.float32(500000.0) ** (-np.arange(half, dtype=np.float32) * np.float32(2.0 / head))
    rates = np.broadcast_to(np.concatenate([rates, rates]).astype(np.float32), (8, head))

    whole = lambda *shape: pl.BlockSpec(shape, lambda i: (0,) * len(shape))
    send, keep = pl.pallas_call(
        attend_project,
        grid=(rows // CHUNK,),
        out_shape=(
            jax.ShapeDtypeStruct((chips, flat, share), jnp.bfloat16),
            jax.ShapeDtypeStruct((chips, flat, share), jnp.float32),
        ),
        in_specs=[
            SMEM,
            SMEM,
            SMEM,
            whole(8, head),
            whole(1, steps, rows, depth),
            whole(1, steps, rows, head),
            whole(1, steps, rows, head),
            pl.BlockSpec((1, CHUNK, length, head), lambda i: (0, i, 0, 0)),
            pl.BlockSpec((1, CHUNK, length, head), lambda i: (0, i, 0, 0)),
            pl.BlockSpec(memory_space=pl.ANY),
        ],
        out_specs=(whole(chips, flat, share), whole(chips, flat, share)),
        scratch_shapes=[
            pltpu.VMEM((rows, head), jnp.float32),
            pltpu.VMEM((pairs, head), jnp.float32),
            pltpu.VMEM((pairs, head), jnp.float32),
            pltpu.VMEM((pairs, head), jnp.float32),
            pltpu.VMEM((pairs, head), jnp.float32),
            pltpu.VMEM((pairs, head), jnp.float32),
            pltpu.VMEM((pairs, head), jnp.float32),
            pltpu.VMEM((cores * chips, depth, share), jnp.bfloat16),
            pltpu.SemaphoreType.DMA((cores * chips,)),
        ],
        compiler_params=pltpu.CompilerParams(vmem_limit_bytes=40 * 2**20),
        name="attend_project",
    )(
        core,
        cache_lengths,
        positions,
        jnp.asarray(rates),
        queries,
        new_keys,
        new_values,
        cache_keys,
        cache_values,
        out_weight,
    )
    got = lax.ppermute(send, "core", SWAP)
    paired = (keep + got.astype(jnp.float32)).astype(jnp.bfloat16)
    parts = lax.all_to_all(paired, "z", 0, 0, tiled=True)
    update = pl.pallas_call(
        sum_blocks,
        out_shape=jax.ShapeDtypeStruct((flat, share), jnp.bfloat16),
        in_specs=[VMEM],
        out_specs=VMEM,
        name="sum_blocks",
    )(parts)
    updates = [
        lax.ppermute(update, "section", [(i, i + by) for i in range(sections - by)])
        for by in range(sections - 1, 0, -1)
    ] + [update]
    place = (core[0] * chips + lax.axis_index("z").astype(jnp.int32)).reshape(1)
    part = lambda: pl.BlockSpec((flat, share), lambda i, at: (0, 0))
    state = pl.pallas_call(
        add_sections,
        grid_spec=pltpu.PrefetchScalarGridSpec(
            num_scalar_prefetch=1,
            grid=(1,),
            in_specs=[pl.BlockSpec((steps, rows, share), lambda i, at: (0, 0, at[0]))]
            + [part() for _ in updates],
            out_specs=pl.BlockSpec((chips, flat, share), lambda i, at: (0, 0, 0)),
        ),
        out_shape=jax.ShapeDtypeStruct((chips, flat, share), jnp.bfloat16),
        name="add_sections",
    )(place, hidden_in, *updates)
    own = lax.all_to_all(state, "z", 0, 0, tiled=True)
    other = lax.ppermute(own, "core", SWAP)
    return pl.pallas_call(
        assemble,
        out_shape=jax.ShapeDtypeStruct((1, steps, rows, model), jnp.bfloat16),
        in_specs=[SMEM, VMEM, VMEM],
        out_specs=VMEM,
        name="assemble",
    )(core, own, other)


def solution(mesh):
    sizes = dict(mesh.shape)
    split = Mesh(
        mesh.devices.reshape(sizes["dp"], sizes["section"], sizes["tensor"] // 2, 2),
        ("dp", "section", "z", "core"),
    )
    tensor = ("z", "core")
    placed = (
        P(None, "dp", None),
        P("section", None, "dp", tensor),
        P("section", None, "dp", tensor),
        P("section", None, "dp", tensor),
        P("section", "dp", None, tensor),
        P("section", "dp", None, tensor),
        P("section", tensor, None),
        P("dp"),
        P("dp"),
    )
    return jax.shard_map(
        per_device,
        mesh=split,
        in_specs=placed,
        out_specs=P("section", None, "dp", None),
        check_vma=False,
    )
```

time: 231 us -> 86.1 us (0.37); the launches traced: 228 us -> 85.5 us
  waiting for transfers between devices: 116 us -> 4.69 us
  blocking collectives: 14.5 us -> 40.7 us
  other arithmetic: 24.4 us -> 0.16 us
  Pallas kernels: 0 us -> 13.9 us
  between operations: 13.6 us -> 0.08 us
  starting transfers between devices: 29 us -> 16.6 us
  matrix products: 10.6 us -> 0 us
  local copies, waits for them, and re-layouts: 19.2 us -> 9.46 us
    ppermute x3 -> x5, waiting for transfers between devices: 62.1 us -> 4.69 us  [the longest x3 1.61 us: per_device(): lax.ppermute(update, 'section', [(i, i + by) for i in range(sections - by)])]
    all_to_all x0 -> x2, blocking collectives: none -> 40.7 us  [the longest x1 23.1 us: per_device(): parts = lax.all_to_all(paired, 'z', 0, 0, tiled=True)]
    all_to_all x2 -> x0, waiting for transfers between devices: 32.2 us -> none  [the longest x1 27.9 us: per_device(): lax.all_to_all(code_words.reshape(flat_rows, parts, block_count, BLOCK),...]
    all_gather x1 -> x0, waiting for transfers between devices: 22 us -> none  [per_device(): lax.all_gather(sum_codes, 'tensor', axis=1, tiled=True)]
    all_to_all x2 -> x0, starting transfers between devices: 14.7 us -> none  [the longest x1 9.98 us: per_device(): lax.all_to_all(block_scale.reshape(flat_rows, parts, block_count), 'tenso...]
    all_gather x1 -> x0, blocking collectives: 14.5 us -> none  [per_device(): lax.all_gather(sum_scale, 'tensor', axis=1, tiled=True)]
    pallas_call x0 -> x4, Pallas kernels: none -> 13.9 us  [the longest x1 8.06 us: per_device(): pl.pallas_call(attend_project, grid=(rows // CHUNK,), out_shape=(jax.Shap...]
    dot_general x1 -> x0, local copies, waits for them, and re-layouts: 12 us -> none  [per_device(): jnp.dot(attended, out_weight[0], preferred_element_type=jnp.float32)]
  transfers between devices with their start and end apart: 6 -> 5, of which waited for: 6 -> 4; matrix products, arithmetic and copies ran while one was open for 1% -> 0% of each run, Pallas kernels for 0% -> 0%
where the time goes in v1:
time: 86.1 us; the launch traced here: 85.5 us
  blocking collectives  40.7 us (47%)
  starting transfers between devices  16.6 us (19%)
  Pallas kernels  13.9 us (16%)
  local copies, waits for them, and re-layouts  9.46 us (11%)
  waiting for transfers between devices  4.69 us (5%)
    all_to_all x1, blocking collectives, per_device(): parts = lax.all_to_all(paired, 'z', 0, 0, tiled=True)  23.1 us
    all_to_all x1, blocking collectives, per_device(): own = lax.all_to_all(state, 'z', 0, 0, tiled=True)  17.6 us
    ppermute x3, starting transfers between devices, per_device(): lax.ppermute(update, 'section', [(i, i + by) for i in range(sections - by)])  9.01 us
    unnamed x24, local copies, waits for them, and re-layouts  8.8 us
    pallas_call x1, Pallas kernels, per_device(): pl.pallas_call(attend_project, grid=(rows // CHUNK,), out_shape=(jax.Shap...  8.06 us
    ppermute x1, starting transfers between devices, per_device(): other = lax.ppermute(own, 'core', SWAP)  4.21 us
    ppermute x1, starting transfers between devices, per_device(): got = lax.ppermute(send, 'core', SWAP)  3.33 us
    pallas_call x1, Pallas kernels, per_device(): pl.pallas_call(assemble, out_shape=jax.ShapeDtypeStruct((1, steps, rows,...  2.24 us
  transfers between devices with their start and end apart: 5, of which 4 were waited for; matrix products, arithmetic and copies ran while one was open for 0% of the time, Pallas kernels for 0%

profile of v1, /device:TPU:1, one launch (start us, length us, event | category | flops | bytes accessed | tf_op | source)
XLA Modules:
  0.0 85.5 jit_solution(11663065934764933487)
XLA Ops:
  0.0 0.7 jit_solution_.3.rate_ref
  0.7 1.9 %copy-done = bf16[1,32,384,128]{3,2,1,0:T(8,128)(2,1)S(1)} copy-done((bf16[1,32,384,128]{3,2,1,0:T(8,128)(2,1)S(1)}, bf16[1,32,384,128]{3,2,1,0:T(8,128)(2,1)}, u32[]{:S(2)}) %copy-start) | copy-done | bytes 3145752
  2.5 1.9 %copy-done.1 = bf16[1,32,384,128]{3,2,1,0:T(8,128)(2,1)S(1)} copy-done((bf16[1,32,384,128]{3,2,1,0:T(8,128)(2,1)S(1)}, bf16[1,32,384,128]{3,2,1,0:T(8,128)(2,1)}, u32[]{:S(2)}) %copy-start.1) | copy-done | bytes 3145752
  4.4 0.8 copy-done.2
  5.3 0.7 copy-done.3
  6.0 0.7 copy-done.4
  6.7 0.7 copy-done.5
  7.4 0.7 copy-done.6
  8.0 8.1 %attend_project.1 = (bf16[8,64,512]{2,1,0:T(8,128)(2,1)S(1)}, f32[8,64,512]{2,1,0:T(8,128)S(1)}) custom-call(s32[1]{0:T(128)} %bitcast.core_ref, s32[32]{0:T(128)S(1)} %copy-done.5, s32[32]{0:T(128)S(1)} %copy-done.6, f32[8,128]{1,0:T(8,128)S(1)} %jit_solution_.3.rate_ref, bf16[1,2,32,512]{3,2,1,0:T(8,128)(2,1)S(1)} %copy-done.2, ...), custom_call_target="tpu_custom_call" | custom-call | tf_op jit(solution)/shard_map/attend_project/pallas_call | solution.py:215
  16.1 3.3 %collective-permute-start = (bf16[8,64,512]{2,1,0:T(8,128)(2,1)S(1)}, bf16[8,64,512]{2,1,0:T(8,128)(2,1)S(1)}, u32[]{:S(2)}, u32[]{:S(2)}) collective-permute-start(bf16[8,64,512]{2,1,0:T(8,128)(2,1)S(1)} %get-tuple-element.8), channel_id=1, source_target_pairs={{0,1},{1,0},{2,3},{3,2},{4,5},{5,4},{6,7},{7,6},{8,9},{9,8},{10,11... | collective-permute-start | bytes 1572872 | tf_op jit(solution)/shard_map/ppermute | solution.py:260
  19.4 1.5 %collective-permute-done = bf16[8,64,512]{2,1,0:T(8,128)(2,1)S(1)} collective-permute-done((bf16[8,64,512]{2,1,0:T(8,128)(2,1)S(1)}, bf16[8,64,512]{2,1,0:T(8,128)(2,1)S(1)}, u32[]{:S(2)}, u32[]{:S(2)}) %collective-permute-start) | collective-permute-done | bytes 524320 | tf_op jit(solution)/shard_map/ppermute | solution.py:260
  21.1 23.1 %all_to_all.10.got_ref = bf16[8,64,512]{2,1,0:T(8,128)(2,1)} all-to-all(bf16[8,64,512]{2,1,0:T(8,128)(2,1)S(1)} %add_convert_fusion), channel_id=1, replica_groups=mesh['dp'=4,'section'=4,'z'=8,'core'=2] {'z'}, dimensions={0} | all-to-all | bytes 1048576 | tf_op jit(solution)/shard_map/all_to_all | solution.py:262
  44.2 1.7 %sum_blocks.1.refs_3_ = bf16[64,512]{1,0:T(8,128)(2,1)} custom-call(bf16[8,64,512]{2,1,0:T(8,128)(2,1)} %all_to_all.10.got_ref), custom_call_target="tpu_custom_call" | custom-call | tf_op jit(solution)/shard_map/sum_blocks/pallas_call | solution.py:263
  45.9 3.2 %collective-permute-start.3 = (bf16[64,512]{1,0:T(8,128)(2,1)}, bf16[64,512]{1,0:T(8,128)(2,1)S(1)}, u32[]{:S(2)}, u32[]{:S(2)}) collective-permute-start(bf16[64,512]{1,0:T(8,128)(2,1)} %sum_blocks.1.refs_3_), channel_id=1, source_target_pairs={{0,16},{16,32},{32,48},{1,17},{17,33},{33,49},{2,18},{18,34},{34,5... | collective-permute-start | bytes 196616 | tf_op jit(solution)/shard_map/ppermute | solution.py:271
  49.1 4.5 %collective-permute-start.2 = (bf16[64,512]{1,0:T(8,128)(2,1)}, bf16[64,512]{1,0:T(8,128)(2,1)S(1)}, u32[]{:S(2)}, u32[]{:S(2)}) collective-permute-start(bf16[64,512]{1,0:T(8,128)(2,1)} %sum_blocks.1.refs_3_), channel_id=1, source_target_pairs={{0,32},{16,48},{1,33},{17,49},{2,34},{18,50},{3,35},{19,51},{4,36}... | collective-permute-start | bytes 196616 | tf_op jit(solution)/shard_map/ppermute | solution.py:271
  53.6 1.3 %collective-permute-start.1 = (bf16[64,512]{1,0:T(8,128)(2,1)}, bf16[64,512]{1,0:T(8,128)(2,1)S(1)}, u32[]{:S(2)}, u32[]{:S(2)}) collective-permute-start(bf16[64,512]{1,0:T(8,128)(2,1)} %sum_blocks.1.refs_3_), channel_id=1, source_target_pairs={{0,48},{1,49},{2,50},{3,51},{4,52},{5,53},{6,54},{7,55},{8,56},{9,... | collective-permute-start | bytes 196616 | tf_op jit(solution)/shard_map/ppermute | solution.py:271
  55.3 1.3 %collective-permute-done.1.refs_0_ = bf16[64,512]{1,0:T(8,128)(2,1)S(1)} collective-permute-done((bf16[64,512]{1,0:T(8,128)(2,1)}, bf16[64,512]{1,0:T(8,128)(2,1)S(1)}, u32[]{:S(2)}, u32[]{:S(2)}) %collective-permute-start.1) | collective-permute-done | bytes 65568 | tf_op jit(solution)/shard_map/ppermute | solution.py:271
  56.6 0.6 copy-done.11
  57.2 1.8 %add_sections.1 = bf16[8,64,512]{2,1,0:T(8,128)(2,1)} custom-call(s32[1]{0:T(128)} %bitcast.1.place_ref, bf16[2,32,8192]{2,1,0:T(8,128)(2,1)} %hidden_ref.1, bf16[64,512]{1,0:T(8,128)(2,1)} %copy-done.11, bf16[64,512]{1,0:T(8,128)(2,1)} %copy-done.10, bf16[64,512]{1,0:T(8,128)(2,1)} %copy-done.9, bf16[64,512]{1,0:T(8,128)(2,1)} %sum_blocks.1.refs_3_), custom_call_target="tpu_custom_call" | custom-call | tf_op jit(solution)/shard_map/add_sections/pallas_call | solution.py:276
  59.0 17.6 %all_to_all.11.own_ref = bf16[8,64,512]{2,1,0:T(8,128)(2,1)S(1)} all-to-all(bf16[8,64,512]{2,1,0:T(8,128)(2,1)} %add_sections.1), channel_id=1, replica_groups=mesh['dp'=4,'section'=4,'z'=8,'core'=2] {'z'}, dimensions={0} | all-to-all | bytes 1048576 | tf_op jit(solution)/shard_map/all_to_all | solution.py:288
  76.7 4.2 %collective-permute-start.4 = (bf16[8,64,512]{2,1,0:T(8,128)(2,1)S(1)}, bf16[8,64,512]{2,1,0:T(8,128)(2,1)S(1)}, u32[]{:S(2)}, u32[]{:S(2)}) collective-permute-start(bf16[8,64,512]{2,1,0:T(8,128)(2,1)S(1)} %all_to_all.11.own_ref), channel_id=1, source_target_pairs={{0,1},{1,0},{2,3},{3,2},{4,5},{5,4},{6,7},{7,6},{8,9},{9,8},{10,11... | collective-permute-start | bytes 1572872 | tf_op jit(solution)/shard_map/ppermute | solution.py:289
  80.9 1.5 %collective-permute-done.4.other_ref = bf16[8,64,512]{2,1,0:T(8,128)(2,1)S(1)} collective-permute-done((bf16[8,64,512]{2,1,0:T(8,128)(2,1)S(1)}, bf16[8,64,512]{2,1,0:T(8,128)(2,1)S(1)}, u32[]{:S(2)}, u32[]{:S(2)}) %collective-permute-start.4) | collective-permute-done | bytes 524320 | tf_op jit(solution)/shard_map/ppermute | solution.py:289
  82.4 0.8 copy-done.8
  83.2 2.2 %assemble.1 = bf16[1,2,32,8192]{3,2,1,0:T(8,128)(2,1)} custom-call(s32[1]{0:T(128)} %bitcast.core_ref, bf16[8,64,512]{2,1,0:T(8,128)(2,1)} %copy-done.7, bf16[8,64,512]{2,1,0:T(8,128)(2,1)} %copy-done.8), custom_call_target="tpu_custom_call" | custom-call | tf_op jit(solution)/shard_map/assemble/pallas_call | solution.py:290
  (18 shorter events, 0.5 us)
Async XLA Ops:
  0.7 1.9 %copy-start = (bf16[1,32,384,128]{3,2,1,0:T(8,128)(2,1)S(1)}, bf16[1,32,384,128]{3,2,1,0:T(8,128)(2,1)}, u32[]{:S(2)}) copy-start(bf16[1,32,384,128]{3,2,1,0:T(8,128)(2,1)} %key_ref.1) | copy-start | bytes 9437188
  2.5 1.9 %copy-start.1 = (bf16[1,32,384,128]{3,2,1,0:T(8,128)(2,1)S(1)}, bf16[1,32,384,128]{3,2,1,0:T(8,128)(2,1)}, u32[]{:S(2)}) copy-start(bf16[1,32,384,128]{3,2,1,0:T(8,128)(2,1)} %value_ref.1) | copy-start | bytes 9437188
  4.4 0.8 copy-start.2
  5.3 0.7 copy-start.3
  6.0 0.7 copy-start.4
  6.7 0.7 copy-start.5
  7.4 0.7 copy-start.6
  16.1 4.9 %collective-permute-start = (bf16[8,64,512]{2,1,0:T(8,128)(2,1)S(1)}, bf16[8,64,512]{2,1,0:T(8,128)(2,1)S(1)}, u32[]{:S(2)}, u32[]{:S(2)}) collective-permute-start(bf16[8,64,512]{2,1,0:T(8,128)(2,1)S(1)} %get-tuple-element.8), channel_id=1, source_target_pairs={{0,1},{1,0},{2,3},{3,2},{4,5},{5,4},{6,7},{7,6},{8,9},{9,8},{10,11... | collective-permute-start | bytes 1572872 | tf_op jit(solution)/shard_map/ppermute | solution.py:260
  45.9 9.0 %collective-permute-start.3 = (bf16[64,512]{1,0:T(8,128)(2,1)}, bf16[64,512]{1,0:T(8,128)(2,1)S(1)}, u32[]{:S(2)}, u32[]{:S(2)}) collective-permute-start(bf16[64,512]{1,0:T(8,128)(2,1)} %sum_blocks.1.refs_3_), channel_id=1, source_target_pairs={{0,16},{16,32},{32,48},{1,17},{17,33},{33,49},{2,18},{18,34},{34,5... | collective-permute-start | bytes 196616 | tf_op jit(solution)/shard_map/ppermute | solution.py:271
  49.1 6.2 %collective-permute-start.2 = (bf16[64,512]{1,0:T(8,128)(2,1)}, bf16[64,512]{1,0:T(8,128)(2,1)S(1)}, u32[]{:S(2)}, u32[]{:S(2)}) collective-permute-start(bf16[64,512]{1,0:T(8,128)(2,1)} %sum_blocks.1.refs_3_), channel_id=1, source_target_pairs={{0,32},{16,48},{1,33},{17,49},{2,34},{18,50},{3,35},{19,51},{4,36}... | collective-permute-start | bytes 196616 | tf_op jit(solution)/shard_map/ppermute | solution.py:271
  53.6 2.9 %collective-permute-start.1 = (bf16[64,512]{1,0:T(8,128)(2,1)}, bf16[64,512]{1,0:T(8,128)(2,1)S(1)}, u32[]{:S(2)}, u32[]{:S(2)}) collective-permute-start(bf16[64,512]{1,0:T(8,128)(2,1)} %sum_blocks.1.refs_3_), channel_id=1, source_target_pairs={{0,48},{1,49},{2,50},{3,51},{4,52},{5,53},{6,54},{7,55},{8,56},{9,... | collective-permute-start | bytes 196616 | tf_op jit(solution)/shard_map/ppermute | solution.py:271
  55.0 1.6 %copy-start.9 = (bf16[64,512]{1,0:T(8,128)(2,1)}, bf16[64,512]{1,0:T(8,128)(2,1)S(1)}, u32[]{:S(2)}) copy-start(bf16[64,512]{1,0:T(8,128)(2,1)S(1)} %collective-permute-done.3.refs_2_) | copy-start | bytes 196612
  55.3 1.3 %copy-start.10 = (bf16[64,512]{1,0:T(8,128)(2,1)}, bf16[64,512]{1,0:T(8,128)(2,1)S(1)}, u32[]{:S(2)}) copy-start(bf16[64,512]{1,0:T(8,128)(2,1)S(1)} %collective-permute-done.2.refs_1_) | copy-start | bytes 196612
  56.6 0.6 copy-start.11
  76.7 5.8 %copy-start.7 = (bf16[8,64,512]{2,1,0:T(8,128)(2,1)}, bf16[8,64,512]{2,1,0:T(8,128)(2,1)S(1)}, u32[]{:S(2)}) copy-start(bf16[8,64,512]{2,1,0:T(8,128)(2,1)S(1)} %all_to_all.11.own_ref) | copy-start | bytes 1572868
  76.7 5.8 %collective-permute-start.4 = (bf16[8,64,512]{2,1,0:T(8,128)(2,1)S(1)}, bf16[8,64,512]{2,1,0:T(8,128)(2,1)S(1)}, u32[]{:S(2)}, u32[]{:S(2)}) collective-permute-start(bf16[8,64,512]{2,1,0:T(8,128)(2,1)S(1)} %all_to_all.11.own_ref), channel_id=1, source_target_pairs={{0,1},{1,0},{2,3},{3,2},{4,5},{5,4},{6,7},{7,6},{8,9},{9,8},{10,11... | collective-permute-start | bytes 1572872 | tf_op jit(solution)/shard_map/ppermute | solution.py:289
  82.4 0.8 copy-start.8

commit v2 on v1

v2 whole, which is shorter than its diff:
```python
import jax
import jax.numpy as jnp
import numpy as np
from jax import lax
from jax.experimental import pallas as pl
from jax.experimental.pallas import tpu as pltpu
from jax.sharding import Mesh
from jax.sharding import PartitionSpec as P

MIB = 2**20


def attend(
    core_ref,
    length_hbm,
    position_hbm,
    rate_hbm,
    query_hbm,
    new_key_hbm,
    new_value_hbm,
    key_hbm,
    value_hbm,
    weight_hbm,
    left_ref,
    send_ref,
    length_ref,
    position_ref,
    rate_ref,
    query_ref,
    new_key_ref,
    new_value_ref,
    key_ref,
    value_ref,
    weight_ref,
    angle,
    rotated,
    fresh0,
    fresh1,
    value0,
    value1,
    attended,
    small_sem,
    cache_sem,
    weight_sem,
):
    steps, rows, head = new_key_ref.shape[1:]
    group = query_ref.shape[3] // head
    length = key_ref.shape[1]
    per_row = steps * group
    blocks, _, width = send_ref.shape
    factor = head**-0.5
    other = 1 - core_ref[0]
    small = [
        pltpu.make_async_copy(source, target, small_sem.at[i])
        for i, (source, target) in enumerate(
            (
                (position_hbm, position_ref),
                (rate_hbm, rate_ref),
                (query_hbm, query_ref),
                (new_key_hbm, new_key_ref),
                (new_value_hbm, new_value_ref),
                (length_hbm, length_ref),
            )
        )
    ]
    caches = [
        pltpu.make_async_copy(key_hbm.at[0], key_ref, cache_sem.at[0]),
        pltpu.make_async_copy(value_hbm.at[0], value_ref, cache_sem.at[1]),
    ]
    weights = []
    for block in range(blocks):
        column = pl.multiple_of((other * blocks + block) * width, width)
        weights.append(
            pltpu.make_async_copy(
                weight_hbm.at[0, :, pl.ds(column, width)], weight_ref.at[block], weight_sem.at[block]
            )
        )
    for copy in small + caches + weights:
        copy.start()
    for copy in small:
        copy.wait()

    rate = rate_ref[...]
    for row in range(rows):
        angle[row : row + 1, :] = position_ref[row].astype(jnp.float32) * jnp.ones_like(rate)
    sign = jnp.where(lax.broadcasted_iota(jnp.int32, (1, head), 1) < head // 2, -1.0, 1.0)
    turns = [(angle[...] + float(s)) * rate for s in range(steps)]
    cosines = [jnp.cos(turn) for turn in turns]
    sines = [jnp.sin(turn) * sign for turn in turns]

    def rot(v, s):
        v = v.astype(jnp.float32)
        out = v * cosines[s] + pltpu.roll(v, head // 2, 1) * sines[s]
        return out.astype(jnp.bfloat16).astype(jnp.float32)

    keys = [rot(new_key_ref[0, s], s) for s in range(steps)]
    fresh = (fresh0, fresh1)
    fresh_values = (value0, value1)
    for s in range(steps):
        for g in range(group):
            at = pl.ds(s * group + g, rows, stride=per_row)
            q = rot(query_ref[0, s, :, g * head : (g + 1) * head], s)
            rotated[at, :] = q
            for m in range(steps):
                if m <= s:
                    score = jnp.sum(q * keys[m], axis=-1, keepdims=True) * factor
                    fresh[m][at, :] = jnp.broadcast_to(score, (rows, head))
                else:
                    fresh[m][at, :] = jnp.full((rows, head), -jnp.inf, jnp.float32)
                fresh_values[m][at, :] = new_value_ref[0, m].astype(jnp.float32)

    lane = lax.broadcasted_iota(jnp.int32, (per_row, length), 1)
    q_all = rotated[...].astype(jnp.bfloat16)
    caches[0].wait()
    scores = []
    for row in range(rows):
        score = lax.dot_general(
            q_all[row * per_row : (row + 1) * per_row],
            key_ref[row],
            (((1,), (1,)), ((), ())),
            preferred_element_type=jnp.float32,
        )
        scores.append(jnp.where(lane < length_ref[row], score * factor, -jnp.inf))
    scores = jnp.concatenate(scores, axis=0)
    new0 = fresh0[...]
    new1 = fresh1[...]
    highest = jnp.maximum(
        jnp.max(scores, axis=-1, keepdims=True), jnp.maximum(new0, new1)[:, 0:1]
    )
    past = jnp.exp(scores - highest)
    new0 = jnp.exp(new0 - highest)
    new1 = jnp.exp(new1 - highest)
    total = jnp.sum(past, axis=-1, keepdims=True) + (new0 + new1)[:, 0:1]
    scale = 1.0 / total
    past = (past * scale).astype(jnp.bfloat16)
    new0 = (new0 * scale).astype(jnp.bfloat16).astype(jnp.float32)
    new1 = (new1 * scale).astype(jnp.bfloat16).astype(jnp.float32)
    caches[1].wait()
    results = [
        jnp.dot(
            past[row * per_row : (row + 1) * per_row],
            value_ref[row],
            preferred_element_type=jnp.float32,
        )
        for row in range(rows)
    ]
    attended[...] = jnp.concatenate(results, axis=0) + new0 * value0[...] + new1 * value1[...]
    left = jnp.concatenate(
        [
            jnp.concatenate(
                [attended[pl.ds(s * group + g, rows, stride=per_row), :] for g in range(group)],
                axis=1,
            )
            for s in range(steps)
        ],
        axis=0,
    ).astype(jnp.bfloat16)
    left_ref[...] = left
    for block in range(blocks):
        weights[block].wait()
        send_ref[block] = jnp.dot(
            left, weight_ref[block], preferred_element_type=jnp.float32
        ).astype(send_ref.dtype)


def project(core_ref, left_ref, weight_hbm, keep_ref, weight_ref, weight_sem):
    blocks, _, width = keep_ref.shape
    copies = []
    for block in range(blocks):
        column = pl.multiple_of((core_ref[0] * blocks + block) * width, width)
        copies.append(
            pltpu.make_async_copy(
                weight_hbm.at[0, :, pl.ds(column, width)], weight_ref.at[block], weight_sem.at[block]
            )
        )
    for copy in copies:
        copy.start()
    for block in range(blocks):
        copies[block].wait()
        keep_ref[block] = jnp.dot(
            left_ref[...], weight_ref[block], preferred_element_type=jnp.float32
        )


def assemble(core_ref, own_ref, other_ref, out_ref, sem):
    blocks, _, width = own_ref.shape
    _, steps, rows, _ = out_ref.shape
    copies = []
    for side, ref in enumerate((own_ref, other_ref)):
        half = core_ref[0] if side == 0 else 1 - core_ref[0]
        for s in range(steps):
            for block in range(blocks):
                at = pl.ds(pl.multiple_of((half * blocks + block) * width, width), width)
                copies.append(
                    pltpu.make_async_copy(
                        ref.at[block, s * rows : (s + 1) * rows],
                        out_ref.at[0, s, :, at],
                        sem.at[side, s, block],
                    )
                )
    for copy in copies:
        copy.start()
    for copy in copies:
        copy.wait()


VMEM = pl.BlockSpec(memory_space=pltpu.VMEM)
SMEM = pl.BlockSpec(memory_space=pltpu.SMEM)
HBM = pl.BlockSpec(memory_space=pltpu.HBM)
ANY = pl.BlockSpec(memory_space=pl.ANY)
SWAP = [(0, 1), (1, 0)]


def per_device(
    hidden_in,
    queries,
    new_keys,
    new_values,
    cache_keys,
    cache_values,
    out_weight,
    cache_lengths,
    positions,
):
    cores = lax.axis_size("core")
    chips = lax.axis_size("z")
    sections = lax.axis_size("section")
    steps, rows, model = hidden_in.shape
    length, head = cache_keys.shape[2:]
    group = queries.shape[3] // head
    depth = group * head
    share = model // (cores * chips)
    flat = steps * rows
    pairs = rows * steps * group
    core = lax.axis_index("core").astype(jnp.int32).reshape(1)
    half = head // 2
    rates = np.float32(500000.0) ** (-np.arange(half, dtype=np.float32) * np.float32(2.0 / head))
    rates = np.concatenate([rates, rates]).astype(np.float32)[None]
    left, send = pl.pallas_call(
        attend,
        out_shape=(
            jax.ShapeDtypeStruct((flat, depth), jnp.bfloat16),
            jax.ShapeDtypeStruct((chips, flat, share), jnp.bfloat16),
        ),
        in_specs=[SMEM] + [HBM] * 9,
        out_specs=(VMEM, VMEM),
        scratch_shapes=[
            pltpu.SMEM((rows,), jnp.int32),
            pltpu.SMEM((rows,), jnp.int32),
            pltpu.VMEM((1, head), jnp.float32),
            pltpu.VMEM(queries.shape, jnp.bfloat16),
            pltpu.VMEM(new_keys.shape, jnp.bfloat16),
            pltpu.VMEM(new_values.shape, jnp.bfloat16),
            pltpu.VMEM((rows, length, head), jnp.bfloat16),
            pltpu.VMEM((rows, length, head), jnp.bfloat16),
            pltpu.VMEM((chips, depth, share), jnp.bfloat16),
            pltpu.VMEM((rows, head), jnp.float32),
        ]
        + [pltpu.VMEM((pairs, head), jnp.float32)] * 6
        + [
            pltpu.SemaphoreType.DMA((6,)),
            pltpu.SemaphoreType.DMA((2,)),
            pltpu.SemaphoreType.DMA((chips,)),
        ],
        compiler_params=pltpu.CompilerParams(vmem_limit_bytes=59 * MIB),
        name="attend",
    )(
        core,
        cache_lengths,
        positions,
        jnp.asarray(rates),
        queries,
        new_keys,
        new_values,
        cache_keys,
        cache_values,
        out_weight,
    )
    got = lax.ppermute(send, "core", SWAP)
    keep = pl.pallas_call(
        project,
        out_shape=jax.ShapeDtypeStruct((chips, flat, share), jnp.float32),
        in_specs=[SMEM, VMEM, HBM],
        out_specs=VMEM,
        scratch_shapes=[
            pltpu.VMEM((chips, depth, share), jnp.bfloat16),
            pltpu.SemaphoreType.DMA((chips,)),
        ],
        cost_estimate=pl.CostEstimate(
            flops=flat * depth * model, bytes_accessed=depth * model, transcendentals=0
        ),
        compiler_params=pltpu.CompilerParams(vmem_limit_bytes=56 * MIB),
        name="project",
    )(core, left, out_weight)
    paired = (keep + got.astype(jnp.float32)).astype(jnp.bfloat16)
    parts = lax.all_to_all(paired, "z", 0, 0, tiled=True)
    update = jnp.sum(parts.astype(jnp.float32), axis=0).astype(jnp.bfloat16)
    updates = [
        lax.ppermute(update, "section", [(i, i + by) for i in range(sections - by)])
        for by in range(sections - 1, 0, -1)
    ] + [update]
    place = (core[0] * chips + lax.axis_index("z").astype(jnp.int32)) * share
    current = lax.dynamic_slice(hidden_in, (0, 0, place), (steps, rows, share)).reshape(flat, share)
    for term in updates:
        current = (current.astype(jnp.float32) + term.astype(jnp.float32)).astype(jnp.bfloat16)
    state = jnp.broadcast_to(current, (chips, flat, share))
    own = lax.all_to_all(state, "z", 0, 0, tiled=True)
    other = lax.ppermute(own, "core", SWAP)
    return pl.pallas_call(
        assemble,
        out_shape=jax.ShapeDtypeStruct((1, steps, rows, model), jnp.bfloat16),
        in_specs=[SMEM, ANY, ANY],
        out_specs=HBM,
        scratch_shapes=[pltpu.SemaphoreType.DMA((2, steps, chips))],
        compiler_params=pltpu.CompilerParams(vmem_limit_bytes=MIB),
        name="assemble",
    )(core, own, other)


def solution(mesh):
    sizes = dict(mesh.shape)
    split = Mesh(
        mesh.devices.reshape(sizes["dp"], sizes["section"], sizes["tensor"] // 2, 2),
        ("dp", "section", "z", "core"),
    )
    tensor = ("z", "core")
    placed = (
        P(None, "dp", None),
        P("section", None, "dp", tensor),
        P("section", None, "dp", tensor),
        P("section", None, "dp", tensor),
        P("section", "dp", None, tensor),
        P("section", "dp", None, tensor),
        P("section", tensor, None),
        P("dp"),
        P("dp"),
    )
    return jax.shard_map(
        per_device,
        mesh=split,
        in_specs=placed,
        out_specs=P("section", None, "dp", None),
        check_vma=False,
    )
```

time: 86.1 us -> 76.3 us (0.89)
  blocking collectives: 40.7 us -> 17.6 us
  waiting for transfers between devices: 4.69 us -> 20.8 us
  local copies, waits for them, and re-layouts: 9.46 us -> 0.06 us
  starting transfers between devices: 16.6 us -> 21.5 us
  other arithmetic: 0.16 us -> 2.31 us
    all_to_all x1 -> x0, blocking collectives: 23.1 us -> none  [per_device(): parts = lax.all_to_all(paired, 'z', 0, 0, tiled=True)]
    all_to_all x0 -> x1, waiting for transfers between devices: none -> 18 us  [per_device(): parts = lax.all_to_all(paired, 'z', 0, 0, tiled=True)]
    unnamed x24 -> x2, local copies, waits for them, and re-layouts: 8.8 us -> 0.01 us
    all_to_all x0 -> x1, starting transfers between devices: none -> 6.45 us  [per_device(): parts = lax.all_to_all(paired, 'z', 0, 0, tiled=True)]
    convert_element_type x1, other arithmetic: 0.16 us -> 2.18 us  [per_device(): paired = (keep + got.astype(jnp.float32)).astype(jnp.bfloat16)]
    ppermute x1, waiting for transfers between devices: 1.54 us -> 0.01 us  [per_device(): got = lax.ppermute(send, 'core', SWAP)]
    pallas_call x1, Pallas kernels: 2.24 us -> 1.23 us  [per_device(): pl.pallas_call(assemble, out_shape=jax.ShapeDtypeStruct((1, steps, rows,...]
    ppermute x1, starting transfers between devices: 4.21 us -> 3.26 us  [per_device(): other = lax.ppermute(own, 'core', SWAP)]
  transfers between devices with their start and end apart: 5 -> 6, of which waited for: 4 -> 3; matrix products, arithmetic and copies ran while one was open for 0% -> 0% of each run, Pallas kernels for 0% -> 6%
where the time goes in v2:
time: 76.3 us; the launch traced here: 76 us
  starting transfers between devices  21.5 us (28%)
  waiting for transfers between devices  20.8 us (27%)
  blocking collectives  17.6 us (23%)
  Pallas kernels  13.6 us (18%)
  other arithmetic  2.31 us (3%)
    all_to_all x1, waiting for transfers between devices, per_device(): parts = lax.all_to_all(paired, 'z', 0, 0, tiled=True)  18 us
    all_to_all x1, blocking collectives, per_device(): own = lax.all_to_all(state, 'z', 0, 0, tiled=True)  17.6 us
    ppermute x3, starting transfers between devices, per_device(): lax.ppermute(update, 'section', [(i, i + by) for i in range(sections - by)])  8.42 us
    pallas_call x1, Pallas kernels, per_device(): pl.pallas_call(attend, out_shape=(jax.ShapeDtypeStruct((flat, depth), jnp...  7.84 us
    all_to_all x1, starting transfers between devices, per_device(): parts = lax.all_to_all(paired, 'z', 0, 0, tiled=True)  6.45 us
    pallas_call x1, Pallas kernels, per_device(): pl.pallas_call(project, out_shape=jax.ShapeDtypeStruct((chips, flat, shar...  4.58 us
    ppermute x1, starting transfers between devices, per_device(): got = lax.ppermute(send, 'core', SWAP)  3.33 us
    ppermute x1, starting transfers between devices, per_device(): other = lax.ppermute(own, 'core', SWAP)  3.26 us
  transfers between devices with their start and end apart: 6, of which 3 were waited for; matrix products, arithmetic and copies ran while one was open for 0% of the time, Pallas kernels for 6%

profile of v2, /device:TPU:1, one launch (start us, length us, event | category | flops | bytes accessed | tf_op | source)
XLA Modules:
  0.0 76.0 jit_solution(1345232395042712743)
XLA Ops:
  0.0 0.0 copy-start
  0.0 7.8 %attend.1 = (bf16[64,512]{1,0:T(8,128)(2,1)}, bf16[8,64,512]{2,1,0:T(8,128)(2,1)}) custom-call(s32[1]{0:T(128)} %bitcast.core_ref, s32[32]{0:T(128)} %length_hbm.1, s32[32]{0:T(128)} %position_hbm.1, f32[1,128]{1,0:T(1,128)} %constant.21.clone.rate_hbm, bf16[1,2,32,512]{3,2,1,0:T(8,128)(2,1)} %query_hbm.1, bf16[1,2,32,128]{3,2,1,0:T(8,128)(2,1)} %new_key_hbm.1, ...), custom_call_target="tpu_custom_call" | custom-call | tf_op jit(solution)/shard_map/attend/pallas_call | solution.py:239
  7.8 3.3 %collective-permute-start = (bf16[8,64,512]{2,1,0:T(8,128)(2,1)}, bf16[8,64,512]{2,1,0:T(8,128)(2,1)S(1)}, u32[]{:S(2)}, u32[]{:S(2)}) collective-permute-start(bf16[8,64,512]{2,1,0:T(8,128)(2,1)} %get-tuple-element.8), channel_id=1, source_target_pairs={{0,1},{1,0},{2,3},{3,2},{4,5},{5,4},{6,7},{7,6},{8,9},{9,8},{10,11... | collective-permute-start | bytes 1572872 | tf_op jit(solution)/shard_map/ppermute | solution.py:279
  11.2 4.6 %project.1 = f32[8,64,512]{2,1,0:T(8,128)} custom-call(s32[1]{0:T(128)} %bitcast.core_ref, bf16[64,512]{1,0:T(8,128)(2,1)} %get-tuple-element.7.left_ref, bf16[1,512,8192]{2,1,0:T(8,128)(2,1)} %weight_hbm.3), custom_call_target="tpu_custom_call" | custom-call | flops 268435456 | bytes 4194304 | tf_op jit(solution)/shard_map/project/pallas_call | solution.py:280
  15.8 0.0 collective-permute-done
  15.8 2.2 %add_convert_fusion = bf16[8,64,512]{2,1,0:T(8,128)(2,1)} fusion(f32[8,64,512]{2,1,0:T(8,128)} %project.1, bf16[8,64,512]{2,1,0:T(8,128)(2,1)S(1)} %collective-permute-done), kind=kLoop, calls=%fused_computation | loop fusion | flops 786432 | bytes 2097152 | tf_op jit(solution)/shard_map/convert_element_type | solution.py:295
  18.0 6.5 %all-to-all-start = ((bf16[8,64,512]{2,1,0:T(8,128)(2,1)}), bf16[8,64,512]{2,1,0:T(8,128)(2,1)S(1)}, u32[]{:S(2)}, u32[]{:S(2)}) async-start(bf16[8,64,512]{2,1,0:T(8,128)(2,1)} %add_convert_fusion), calls=%async_computation | async-start | bytes 1048576 | tf_op jit(solution)/shard_map/all_to_all | solution.py:296
  24.4 18.0 %all-to-all-done = bf16[8,64,512]{2,1,0:T(8,128)(2,1)S(1)} async-done(((bf16[8,64,512]{2,1,0:T(8,128)(2,1)}), bf16[8,64,512]{2,1,0:T(8,128)(2,1)S(1)}, u32[]{:S(2)}, u32[]{:S(2)}) %all-to-all-start) | async-done | bytes 524320 | tf_op jit(solution)/shard_map/all_to_all | solution.py:296
  42.4 0.1 reduce_sum.12
  42.5 4.6 %collective-permute-start.1 = (bf16[64,512]{1,0:T(8,128)(2,1)S(1)}, bf16[64,512]{1,0:T(8,128)(2,1)S(1)}, u32[]{:S(2)}, u32[]{:S(2)}) collective-permute-start(bf16[64,512]{1,0:T(8,128)(2,1)S(1)} %reduce_sum.12), channel_id=1, source_target_pairs={{0,48},{1,49},{2,50},{3,51},{4,52},{5,53},{6,54},{7,55},{8,56},{9,... | collective-permute-start | bytes 196616 | tf_op jit(solution)/shard_map/ppermute | solution.py:299
  47.2 1.3 %collective-permute-start.2 = (bf16[64,512]{1,0:T(8,128)(2,1)S(1)}, bf16[64,512]{1,0:T(8,128)(2,1)S(1)}, u32[]{:S(2)}, u32[]{:S(2)}) collective-permute-start(bf16[64,512]{1,0:T(8,128)(2,1)S(1)} %reduce_sum.12), channel_id=1, source_target_pairs={{0,32},{16,48},{1,33},{17,49},{2,34},{18,50},{3,35},{19,51},{4,36}... | collective-permute-start | bytes 196616 | tf_op jit(solution)/shard_map/ppermute | solution.py:299
  48.5 2.5 %collective-permute-start.3 = (bf16[64,512]{1,0:T(8,128)(2,1)S(1)}, bf16[64,512]{1,0:T(8,128)(2,1)S(1)}, u32[]{:S(2)}, u32[]{:S(2)}) collective-permute-start(bf16[64,512]{1,0:T(8,128)(2,1)S(1)} %reduce_sum.12), channel_id=1, source_target_pairs={{0,16},{16,32},{32,48},{1,17},{17,33},{33,49},{2,18},{18,34},{34,5... | collective-permute-start | bytes 196616 | tf_op jit(solution)/shard_map/ppermute | solution.py:299
  51.0 0.0 copy-done
  51.0 0.0 collective-permute-done.1
  51.0 0.0 collective-permute-done.2
  51.0 1.3 %collective-permute-done.3 = bf16[64,512]{1,0:T(8,128)(2,1)S(1)} collective-permute-done((bf16[64,512]{1,0:T(8,128)(2,1)S(1)}, bf16[64,512]{1,0:T(8,128)(2,1)S(1)}, u32[]{:S(2)}, u32[]{:S(2)}) %collective-permute-start.3) | collective-permute-done | bytes 65568 | tf_op jit(solution)/shard_map/ppermute | solution.py:299
  52.4 17.6 %all_to_all.10.own_ref = bf16[8,64,512]{2,1,0:T(8,128)(2,1)S(1)} all-to-all(bf16[8,64,512]{2,1,0:T(8,128)(2,1)S(1)} %broadcast_in_dim.3), channel_id=1, replica_groups=mesh['dp'=4,'section'=4,'z'=8,'core'=2] {'z'}, dimensions={0} | all-to-all | bytes 1048576 | tf_op jit(solution)/shard_map/all_to_all | solution.py:307
  70.0 3.3 %collective-permute-start.4 = (bf16[8,64,512]{2,1,0:T(8,128)(2,1)S(1)}, bf16[8,64,512]{2,1,0:T(8,128)(2,1)S(1)}, u32[]{:S(2)}, u32[]{:S(2)}) collective-permute-start(bf16[8,64,512]{2,1,0:T(8,128)(2,1)S(1)} %all_to_all.10.own_ref), channel_id=1, source_target_pairs={{0,1},{1,0},{2,3},{3,2},{4,5},{5,4},{6,7},{7,6},{8,9},{9,8},{10,11... | collective-permute-start | bytes 1572872 | tf_op jit(solution)/shard_map/ppermute | solution.py:308
  73.2 1.5 %collective-permute-done.4.other_ref = bf16[8,64,512]{2,1,0:T(8,128)(2,1)S(1)} collective-permute-done((bf16[8,64,512]{2,1,0:T(8,128)(2,1)S(1)}, bf16[8,64,512]{2,1,0:T(8,128)(2,1)S(1)}, u32[]{:S(2)}, u32[]{:S(2)}) %collective-permute-start.4) | collective-permute-done | bytes 524320 | tf_op jit(solution)/shard_map/ppermute | solution.py:308
  74.8 1.2 %assemble.1 = bf16[1,2,32,8192]{3,2,1,0:T(8,128)(2,1)} custom-call(s32[1]{0:T(128)} %bitcast.core_ref, bf16[8,64,512]{2,1,0:T(8,128)(2,1)S(1)} %all_to_all.10.own_ref, bf16[8,64,512]{2,1,0:T(8,128)(2,1)S(1)} %collective-permute-done.4.other_ref), custom_call_target="tpu_custom_call" | custom-call | tf_op jit(solution)/shard_map/assemble/pallas_call | solution.py:309
  (3 shorter events, 0.1 us)
Async XLA Ops:
  0.0 51.0 %copy-start = (bf16[2,32,8192]{2,1,0:T(8,128)(2,1)S(1)}, bf16[2,32,8192]{2,1,0:T(8,128)(2,1)}, u32[]{:S(2)}) copy-start(bf16[2,32,8192]{2,1,0:T(8,128)(2,1)} %param.10) | copy-start | bytes 3145732
  7.8 7.9 %collective-permute-start = (bf16[8,64,512]{2,1,0:T(8,128)(2,1)}, bf16[8,64,512]{2,1,0:T(8,128)(2,1)S(1)}, u32[]{:S(2)}, u32[]{:S(2)}) collective-permute-start(bf16[8,64,512]{2,1,0:T(8,128)(2,1)} %get-tuple-element.8), channel_id=1, source_target_pairs={{0,1},{1,0},{2,3},{3,2},{4,5},{5,4},{6,7},{7,6},{8,9},{9,8},{10,11... | collective-permute-start | bytes 1572872 | tf_op jit(solution)/shard_map/ppermute | solution.py:279
  18.0 24.5 %all-to-all-start = ((bf16[8,64,512]{2,1,0:T(8,128)(2,1)}), bf16[8,64,512]{2,1,0:T(8,128)(2,1)S(1)}, u32[]{:S(2)}, u32[]{:S(2)}) async-start(bf16[8,64,512]{2,1,0:T(8,128)(2,1)} %add_convert_fusion), calls=%async_computation | async-start | bytes 1048576 | tf_op jit(solution)/shard_map/all_to_all | solution.py:296
  42.5 8.5 %collective-permute-start.1 = (bf16[64,512]{1,0:T(8,128)(2,1)S(1)}, bf16[64,512]{1,0:T(8,128)(2,1)S(1)}, u32[]{:S(2)}, u32[]{:S(2)}) collective-permute-start(bf16[64,512]{1,0:T(8,128)(2,1)S(1)} %reduce_sum.12), channel_id=1, source_target_pairs={{0,48},{1,49},{2,50},{3,51},{4,52},{5,53},{6,54},{7,55},{8,56},{9,... | collective-permute-start | bytes 196616 | tf_op jit(solution)/shard_map/ppermute | solution.py:299
  47.2 3.8 %collective-permute-start.2 = (bf16[64,512]{1,0:T(8,128)(2,1)S(1)}, bf16[64,512]{1,0:T(8,128)(2,1)S(1)}, u32[]{:S(2)}, u32[]{:S(2)}) collective-permute-start(bf16[64,512]{1,0:T(8,128)(2,1)S(1)} %reduce_sum.12), channel_id=1, source_target_pairs={{0,32},{16,48},{1,33},{17,49},{2,34},{18,50},{3,35},{19,51},{4,36}... | collective-permute-start | bytes 196616 | tf_op jit(solution)/shard_map/ppermute | solution.py:299
  48.5 3.8 %collective-permute-start.3 = (bf16[64,512]{1,0:T(8,128)(2,1)S(1)}, bf16[64,512]{1,0:T(8,128)(2,1)S(1)}, u32[]{:S(2)}, u32[]{:S(2)}) collective-permute-start(bf16[64,512]{1,0:T(8,128)(2,1)S(1)} %reduce_sum.12), channel_id=1, source_target_pairs={{0,16},{16,32},{32,48},{1,17},{17,33},{33,49},{2,18},{18,34},{34,5... | collective-permute-start | bytes 196616 | tf_op jit(solution)/shard_map/ppermute | solution.py:299
  70.0 4.8 %collective-permute-start.4 = (bf16[8,64,512]{2,1,0:T(8,128)(2,1)S(1)}, bf16[8,64,512]{2,1,0:T(8,128)(2,1)S(1)}, u32[]{:S(2)}, u32[]{:S(2)}) collective-permute-start(bf16[8,64,512]{2,1,0:T(8,128)(2,1)S(1)} %all_to_all.10.own_ref), channel_id=1, source_target_pairs={{0,1},{1,0},{2,3},{3,2},{4,5},{5,4},{6,7},{7,6},{8,9},{9,8},{10,11... | collective-permute-start | bytes 1572872 | tf_op jit(solution)/shard_map/ppermute | solution.py:308

commit v3 on v2

v3 whole, which is shorter than its diff:
```python
import jax
import jax.numpy as jnp
import numpy as np
from jax import lax
from jax.experimental import pallas as pl
from jax.experimental.pallas import tpu as pltpu
from jax.sharding import Mesh
from jax.sharding import PartitionSpec as P

KIB = 1024
OFFSETS = (-2, 1, 4, -1, 2, -3, 0, 3)
TO_UP, TO_DOWN, STAY = slice(0, 3), slice(3, 5), slice(5, 8)
GROUP = 4


def attend(
    core_ref,
    chip_ref,
    length_hbm,
    position_hbm,
    rate_hbm,
    query_hbm,
    new_key_hbm,
    new_value_hbm,
    key_hbm,
    value_hbm,
    weight_hbm,
    hidden_hbm,
    send_ref,
    keep_ref,
    near_ref,
    length_ref,
    position_ref,
    rate_ref,
    query_ref,
    new_key_ref,
    new_value_ref,
    key_ref,
    value_ref,
    weight_ref,
    rotated,
    fresh0,
    fresh1,
    value0,
    value1,
    lengths,
    turns,
    attended,
    small_sem,
    hidden_sem,
    cache_sem,
    weight_sem,
):
    rows, length, head = key_ref.shape
    flat, width = near_ref.shape
    steps = flat // rows
    depth = weight_ref.shape[1]
    group = depth // head
    per_row = steps * group
    chips = send_ref.shape[0]
    factor = head**-0.5
    core = core_ref[0]
    chip = chip_ref[0]

    def columns(half, offset):
        block = half * chips + lax.rem(chip + (offset + chips), chips)
        return pl.ds(pl.multiple_of(block * width, width), width)

    small = [
        pltpu.make_async_copy(source, target, small_sem.at[i])
        for i, (source, target) in enumerate(
            (
                (position_hbm, position_ref),
                (rate_hbm, rate_ref),
                (length_hbm, length_ref),
                (new_key_hbm, new_key_ref),
                (query_hbm, query_ref),
                (new_value_hbm, new_value_ref),
            )
        )
    ]
    caches = [
        pltpu.make_async_copy(key_hbm.at[0], key_ref, cache_sem.at[0]),
        pltpu.make_async_copy(value_hbm.at[0], value_ref, cache_sem.at[1]),
    ]
    weights = []
    for half in (1 - core, core):
        for offset in OFFSETS:
            slot = len(weights)
            weights.append(
                pltpu.make_async_copy(
                    weight_hbm.at[0, :, columns(half, offset)],
                    weight_ref.at[slot],
                    weight_sem.at[slot],
                )
            )
    hidden = [
        pltpu.make_async_copy(
            hidden_hbm.at[s, :, columns(core, 0)],
            near_ref.at[s * rows : (s + 1) * rows],
            hidden_sem.at[s],
        )
        for s in range(steps)
    ]
    for copy in small + caches:
        copy.start()

    for copy in small:
        copy.wait()
    for row in range(rows):
        for s in range(steps):
            at = s * rows + row
            when = (position_ref[row] + s).astype(jnp.float32)
            turns[at : at + 1, :] = jnp.full((1, head), when, jnp.float32)
        limit = length_ref[row].astype(jnp.float32)
        lengths[row * per_row : (row + 1) * per_row, :] = jnp.full((per_row, head), limit, jnp.float32)
    sign = jnp.where(lax.broadcasted_iota(jnp.int32, (1, head), 1) < head // 2, -1.0, 1.0)
    turn = turns[...] * rate_ref[...]
    cosine = jnp.cos(turn)
    sine = jnp.sin(turn) * sign

    def rot(v):
        v = v.astype(jnp.float32).reshape(flat, head)
        out = v * cosine + pltpu.roll(v, head // 2, 1) * sine
        return out.astype(jnp.bfloat16).astype(jnp.float32)

    keys = rot(new_key_ref[0])
    fresh = (fresh0, fresh1)
    fresh_values = (value0, value1)
    for g in range(group):
        q = rot(query_ref[0, :, :, g * head : (g + 1) * head])
        for s in range(steps):
            at = pl.ds(s * group + g, rows, stride=per_row)
            mine = q[s * rows : (s + 1) * rows]
            rotated[at, :] = mine
            for m in range(steps):
                if m <= s:
                    score = jnp.sum(mine * keys[m * rows : (m + 1) * rows], axis=-1, keepdims=True)
                    fresh[m][at, :] = jnp.broadcast_to(score * factor, (rows, head))
                else:
                    fresh[m][at, :] = jnp.full((rows, head), -jnp.inf, jnp.float32)
                fresh_values[m][at, :] = new_value_ref[0, m].astype(jnp.float32)

    q_all = rotated[...].astype(jnp.bfloat16)
    caches[0].wait()
    for copy in weights[:chips]:
        copy.start()
    scores = jnp.concatenate(
        [
            lax.dot_general(
                q_all[row * per_row : (row + 1) * per_row],
                key_ref[row],
                (((1,), (1,)), ((), ())),
                preferred_element_type=jnp.float32,
            )
            for row in range(rows)
        ],
        axis=0,
    )
    lane = lax.broadcasted_iota(jnp.int32, (1, length), 1).astype(jnp.float32)
    limit = jnp.concatenate([lengths[...]] * (length // head), axis=1)
    scores = jnp.where(lane < limit, scores * factor, -jnp.inf)
    new0 = fresh0[...]
    new1 = fresh1[...]
    highest = jnp.maximum(
        jnp.max(scores, axis=-1, keepdims=True), jnp.maximum(new0, new1)[:, 0:1]
    )
    past = jnp.exp(scores - highest)
    new0 = jnp.exp(new0 - highest)
    new1 = jnp.exp(new1 - highest)
    total = jnp.sum(past, axis=-1, keepdims=True) + (new0 + new1)[:, 0:1]
    scale = 1.0 / total
    past = (past * scale).astype(jnp.bfloat16)
    new0 = (new0 * scale).astype(jnp.bfloat16).astype(jnp.float32)
    new1 = (new1 * scale).astype(jnp.bfloat16).astype(jnp.float32)
    caches[1].wait()
    for copy in weights[chips:] + hidden:
        copy.start()
    results = jnp.concatenate(
        [
            jnp.dot(
                past[row * per_row : (row + 1) * per_row],
                value_ref[row],
                preferred_element_type=jnp.float32,
            )
            for row in range(rows)
        ],
        axis=0,
    )
    attended[...] = results + new0 * value0[...] + new1 * value1[...]
    left = jnp.concatenate(
        [
            jnp.concatenate(
                [attended[pl.ds(s * group + g, rows, stride=per_row), :] for g in range(group)],
                axis=1,
            )
            for s in range(steps)
        ],
        axis=0,
    ).astype(jnp.bfloat16)
    for first in range(0, len(weights), GROUP):
        for slot in range(first, first + GROUP):
            weights[slot].wait()
        for slot in range(first, first + GROUP):
            partial = jnp.dot(left, weight_ref[slot], preferred_element_type=jnp.float32)
            target = send_ref if slot < chips else keep_ref
            target[slot % chips] = partial.astype(target.dtype)
    for copy in hidden:
        copy.wait()


PIECES = (
    (False, (3,)),
    (False, (0,)),
    (False, (-3,)),
    (False, (2, -1, -4)),
    (False, (1, -2)),
    (True, (3, 0, -3)),
    (True, (2, -1, -4)),
    (True, (1, -2)),
)


def assemble(core_ref, chip_ref, *refs):
    parts, out_ref, sem = refs[:-2], refs[-2], refs[-1]
    core, chip = core_ref[0], chip_ref[0]
    model = out_ref.shape[1]
    copies = []
    for ref, (swapped, offsets) in zip(parts, PIECES):
        half = 1 - core if swapped else core
        width = ref.shape[-1]
        chips = model // width // 2
        for i, offset in enumerate(offsets):
            block = half * chips + lax.rem(chip + (offset + chips), chips)
            at = pl.ds(pl.multiple_of(block * width, width), width)
            copies.append(
                pltpu.make_async_copy(ref.at[i], out_ref.at[:, at], sem.at[len(copies)])
            )
    for copy in copies:
        copy.start()
    for copy in copies:
        copy.wait()


VMEM = pl.BlockSpec(memory_space=pltpu.VMEM)
SMEM = pl.BlockSpec(memory_space=pltpu.SMEM)
HBM = pl.BlockSpec(memory_space=pltpu.HBM)
ANY = pl.BlockSpec(memory_space=pl.ANY)
SWAP = [(0, 1), (1, 0)]


def widen(array):
    return array.astype(jnp.float32)


def narrow(array):
    return array.astype(jnp.bfloat16)


def per_device(
    hidden_in,
    queries,
    new_keys,
    new_values,
    cache_keys,
    cache_values,
    out_weight,
    cache_lengths,
    positions,
):
    cores = lax.axis_size("core")
    chips = lax.axis_size("z")
    sections = lax.axis_size("section")
    steps, rows, model = hidden_in.shape
    length, head = cache_keys.shape[2:]
    depth = queries.shape[3]
    share = model // (cores * chips)
    flat = steps * rows
    pairs = flat * depth // head
    half = head // 2
    rates = np.float32(500000.0) ** (-np.arange(half, dtype=np.float32) * np.float32(2.0 / head))
    rates = np.concatenate([rates, rates]).astype(np.float32)[None]
    core = lax.axis_index("core").astype(jnp.int32).reshape(1)
    chip = lax.axis_index("z").astype(jnp.int32).reshape(1)

    def shift(array, by):
        return lax.ppermute(array, "z", [(i, (i + by) % chips) for i in range(chips)])

    send, keep, current = pl.pallas_call(
        attend,
        out_shape=(
            jax.ShapeDtypeStruct((chips, flat, share), jnp.bfloat16),
            jax.ShapeDtypeStruct((chips, flat, share), jnp.float32),
            jax.ShapeDtypeStruct((flat, share), jnp.bfloat16),
        ),
        in_specs=[SMEM, SMEM] + [HBM] * 10,
        out_specs=(VMEM, VMEM, VMEM),
        scratch_shapes=[
            pltpu.SMEM((rows,), jnp.int32),
            pltpu.SMEM((rows,), jnp.int32),
            pltpu.VMEM((1, head), jnp.float32),
            pltpu.VMEM(queries.shape, jnp.bfloat16),
            pltpu.VMEM(new_keys.shape, jnp.bfloat16),
            pltpu.VMEM(new_values.shape, jnp.bfloat16),
            pltpu.VMEM((rows, length, head), jnp.bfloat16),
            pltpu.VMEM((rows, length, head), jnp.bfloat16),
            pltpu.VMEM((cores * chips, depth, share), jnp.bfloat16),
        ]
        + [pltpu.VMEM((pairs, head), jnp.float32)] * 6
        + [
            pltpu.VMEM((flat, head), jnp.float32),
            pltpu.VMEM((pairs, head), jnp.float32),
            pltpu.SemaphoreType.DMA((6,)),
            pltpu.SemaphoreType.DMA((steps,)),
            pltpu.SemaphoreType.DMA((2,)),
            pltpu.SemaphoreType.DMA((cores * chips,)),
        ],
        compiler_params=pltpu.CompilerParams(vmem_limit_bytes=58368 * KIB),
        name="attend",
    )(
        core,
        chip,
        cache_lengths,
        positions,
        jnp.asarray(rates),
        queries,
        new_keys,
        new_values,
        cache_keys,
        cache_values,
        out_weight,
        hidden_in,
    )

    got = lax.ppermute(send, "core", SWAP)
    paired = lambda part: keep[part] + widen(got[part])
    up = shift(narrow(paired(TO_UP)), 1)
    down = shift(narrow(paired(TO_DOWN)), -1)
    stay = paired(STAY)
    above = shift(narrow(stay[2] + widen(up[2]) + widen(down[1])), 3)
    below = shift(narrow(stay[0] + widen(up[0])), -3)
    update = narrow(stay[1] + widen(up[1]) + widen(down[0]) + widen(above) + widen(below))
    updates = [
        lax.ppermute(update, "section", [(i, i + by) for i in range(sections - by)])
        for by in (1,2,3)
    ]
    updates = [updates[(1,2,3).index(by)] for by in range(sections - 1, 0, -1)] + [update]
    for term in updates:
        current = narrow(widen(current) + widen(term))
    mine = current[None]
    near = [shift(mine, -3), mine, shift(mine, 3)]
    up = shift(jnp.concatenate(near), 1)
    down = shift(jnp.concatenate(near[1:]), -1)
    pieces = near + [up, down]
    pieces = pieces + [
        lax.ppermute(piece, "core", SWAP)
        for piece in (jnp.concatenate(near), up, down)
    ]
    states = pl.pallas_call(
        assemble,
        out_shape=jax.ShapeDtypeStruct((flat, model), jnp.bfloat16),
        in_specs=[SMEM, SMEM] + [ANY] * len(pieces),
        out_specs=HBM,
        scratch_shapes=[pltpu.SemaphoreType.DMA((cores * chips,))],
        compiler_params=pltpu.CompilerParams(vmem_limit_bytes=1024 * KIB),
        name="assemble",
    )(core, chip, *pieces)
    return states.reshape(1, steps, rows, model)


def solution(mesh):
    sizes = dict(mesh.shape)
    split = Mesh(
        mesh.devices.reshape(sizes["dp"], sizes["section"], sizes["tensor"] // 2, 2),
        ("dp", "section", "z", "core"),
    )
    tensor = ("z", "core")
    placed = (
        P(None, "dp", None),
        P("section", None, "dp", tensor),
        P("section", None, "dp", tensor),
        P("section", None, "dp", tensor),
        P("section", "dp", None, tensor),
        P("section", "dp", None, tensor),
        P("section", tensor, None),
        P("dp"),
        P("dp"),
    )
    return jax.shard_map(
        per_device,
        mesh=split,
        in_specs=placed,
        out_specs=P("section", None, "dp", None),
        check_vma=False,
    )
```

time: 76.3 us -> 65.4 us (0.86)
  blocking collectives: 17.6 us -> 0 us
  starting transfers between devices: 21.5 us -> 38.8 us
  waiting for transfers between devices: 20.8 us -> 15 us
  Pallas kernels: 13.6 us -> 8.95 us
    ppermute x1 -> x11, starting transfers between devices: 3.26 us -> 26.4 us  [the longest x8 17.9 us: shift(): lax.ppermute(array, 'z', [(i, (i + by) % chips) for i in range(chips)])]
    all_to_all x1 -> x0, waiting for transfers between devices: 18 us -> none  [per_device(): parts = lax.all_to_all(paired, 'z', 0, 0, tiled=True)]
    all_to_all x1 -> x0, blocking collectives: 17.6 us -> none  [per_device(): own = lax.all_to_all(state, 'z', 0, 0, tiled=True)]
    ppermute x1 -> x11, waiting for transfers between devices: 1.54 us -> 12 us  [the longest x8 11 us: shift(): lax.ppermute(array, 'z', [(i, (i + by) % chips) for i in range(chips)])]
    all_to_all x1 -> x0, starting transfers between devices: 6.45 us -> none  [per_device(): parts = lax.all_to_all(paired, 'z', 0, 0, tiled=True)]
    pallas_call x3 -> x2, Pallas kernels: 13.6 us -> 8.95 us  [the longest x1 7.86 us: per_device(): pl.pallas_call(attend, out_shape=(jax.ShapeDtypeStruct((chips, flat, shar...]
    ppermute x1, waiting for transfers between devices: 0.01 us -> 1.75 us  [per_device(): got = lax.ppermute(send, 'core', SWAP)]
    convert_element_type x2 -> x4, other arithmetic: 2.23 us -> 2.29 us  [narrow(): return array.astype(jnp.bfloat16)]
  transfers between devices with their start and end apart: 6 -> 15, of which waited for: 3 -> 9; matrix products, arithmetic and copies ran while one was open for 0% -> 2% of each run, Pallas kernels for 6% -> 0%
where the time goes in v3:
time: 65.4 us; the launch traced here: 65.2 us
  starting transfers between devices  38.8 us (59%)
  waiting for transfers between devices  15 us (23%)
  Pallas kernels  8.95 us (14%)
  other arithmetic  2.38 us (4%)
    ppermute x8, starting transfers between devices, shift(): lax.ppermute(array, 'z', [(i, (i + by) % chips) for i in range(chips)])  17.9 us
    ppermute x8, waiting for transfers between devices, shift(): lax.ppermute(array, 'z', [(i, (i + by) % chips) for i in range(chips)])  11 us
    ppermute x3, starting transfers between devices, per_device(): lax.ppermute(update, 'section', [(i, i + by) for i in range(sections - by)])  9.02 us
    ppermute x3, starting transfers between devices, per_device(): lax.ppermute(piece, 'core', SWAP)  8.51 us
    pallas_call x1, Pallas kernels, per_device(): pl.pallas_call(attend, out_shape=(jax.ShapeDtypeStruct((chips, flat, shar...  7.86 us
    ppermute x1, starting transfers between devices, per_device(): got = lax.ppermute(send, 'core', SWAP)  3.33 us
    convert_element_type x4, other arithmetic, narrow(): return array.astype(jnp.bfloat16)  2.29 us
    ppermute x1, waiting for transfers between devices, per_device(): got = lax.ppermute(send, 'core', SWAP)  1.75 us
  transfers between devices with their start and end apart: 15, of which 9 were waited for; matrix products, arithmetic and copies ran while one was open for 2% of the time, Pallas kernels for 0%

profile of v3, /device:TPU:1, one launch (start us, length us, event | category | flops | bytes accessed | tf_op | source)
XLA Modules:
  0.0 65.2 jit_solution(11546657190739738375)
XLA Ops:
  0.0 7.9 %attend.1 = (bf16[8,64,512]{2,1,0:T(8,128)(2,1)}, f32[8,64,512]{2,1,0:T(8,128)}, bf16[64,512]{1,0:T(8,128)(2,1)}) custom-call(s32[1]{0:T(128)} %bitcast.core_ref, s32[1]{0:T(128)} %bitcast.1.chip_ref, s32[32]{0:T(128)} %length_hbm.1, s32[32]{0:T(128)} %position_hbm.1, f32[1,128]{1,0:T(1,128)} %constant.10.clone.rate_hbm, bf16[1,2,32,512]{3,2,1,0:T(8,128)(2,1)} %query_hbm.1, ...), custom_call_target="tpu_custom_call" | custom-call | tf_op jit(solution)/shard_map/attend/pallas_call | solution.py:289
  7.9 3.3 %collective-permute-start = (bf16[8,64,512]{2,1,0:T(8,128)(2,1)}, bf16[8,64,512]{2,1,0:T(8,128)(2,1)S(1)}, u32[]{:S(2)}, u32[]{:S(2)}) collective-permute-start(bf16[8,64,512]{2,1,0:T(8,128)(2,1)} %get-tuple-element.10), channel_id=1, source_target_pairs={{0,1},{1,0},{2,3},{3,2},{4,5},{5,4},{6,7},{7,6},{8,9},{9,8},{10,11... | collective-permute-start | bytes 1572872 | tf_op jit(solution)/shard_map/ppermute | solution.py:335
  11.2 1.7 %collective-permute-done = bf16[8,64,512]{2,1,0:T(8,128)(2,1)S(1)} collective-permute-done((bf16[8,64,512]{2,1,0:T(8,128)(2,1)}, bf16[8,64,512]{2,1,0:T(8,128)(2,1)S(1)}, u32[]{:S(2)}, u32[]{:S(2)}) %collective-permute-start) | collective-permute-done | bytes 524320 | tf_op jit(solution)/shard_map/ppermute | solution.py:335
  13.0 1.2 %add_convert_fusion = (bf16[3,64,512]{2,1,0:T(8,128)(2,1)S(1)}, f32[3,64,512]{2,1,0:T(8,128)S(1)}) fusion(f32[8,64,512]{2,1,0:T(8,128)} %get-tuple-element.9, bf16[8,64,512]{2,1,0:T(8,128)(2,1)S(1)} %collective-permute-done), kind=kLoop, calls=%fused_computation | loop fusion | flops 491520 | bytes 1769472 | tf_op jit(solution)/shard_map/convert_element_type | solution.py:257
  14.3 1.0 %add_convert_fusion.1 = bf16[2,64,512]{2,1,0:T(8,128)(2,1)S(1)} fusion(f32[8,64,512]{2,1,0:T(8,128)} %get-tuple-element.9, bf16[8,64,512]{2,1,0:T(8,128)(2,1)S(1)} %collective-permute-done), kind=kLoop, calls=%fused_computation.2 | loop fusion | flops 196608 | bytes 524288 | tf_op jit(solution)/shard_map/convert_element_type | solution.py:257
  15.3 3.9 %collective-permute-start.2 = (bf16[2,64,512]{2,1,0:T(8,128)(2,1)S(1)}, bf16[2,64,512]{2,1,0:T(8,128)(2,1)S(1)}, u32[]{:S(2)}, u32[]{:S(2)}) collective-permute-start(bf16[2,64,512]{2,1,0:T(8,128)(2,1)S(1)} %add_convert_fusion.1), channel_id=1, source_target_pairs={{0,14},{2,0},{4,2},{6,4},{8,6},{10,8},{12,10},{14,12},{1,15},{3,1}... | collective-permute-start | bytes 393224 | tf_op jit(solution)/shard_map/ppermute | solution.py:287
  19.2 2.5 %collective-permute-done.2 = bf16[2,64,512]{2,1,0:T(8,128)(2,1)S(1)} collective-permute-done((bf16[2,64,512]{2,1,0:T(8,128)(2,1)S(1)}, bf16[2,64,512]{2,1,0:T(8,128)(2,1)S(1)}, u32[]{:S(2)}, u32[]{:S(2)}) %collective-permute-start.2) | collective-permute-done | bytes 131104 | tf_op jit(solution)/shard_map/ppermute | solution.py:287
  21.7 1.4 %collective-permute-done.1 = bf16[3,64,512]{2,1,0:T(8,128)(2,1)S(1)} collective-permute-done((bf16[3,64,512]{2,1,0:T(8,128)(2,1)S(1)}, bf16[3,64,512]{2,1,0:T(8,128)(2,1)S(1)}, u32[]{:S(2)}, u32[]{:S(2)}) %collective-permute-start.1) | collective-permute-done | bytes 196640 | tf_op jit(solution)/shard_map/ppermute | solution.py:287
  23.1 3.4 %collective-permute-start.3 = (bf16[64,512]{1,0:T(8,128)(2,1)S(1)}, bf16[64,512]{1,0:T(8,128)(2,1)S(1)}, u32[]{:S(2)}, u32[]{:S(2)}) collective-permute-start(bf16[64,512]{1,0:T(8,128)(2,1)S(1)} %get-tuple-element.13), channel_id=1, source_target_pairs={{0,6},{2,8},{4,10},{6,12},{8,14},{10,0},{12,2},{14,4},{1,7},{3,9},... | collective-permute-start | bytes 196616 | tf_op jit(solution)/shard_map/ppermute | solution.py:287
  26.5 1.2 %collective-permute-start.4 = (bf16[64,512]{1,0:T(8,128)(2,1)S(1)}, bf16[64,512]{1,0:T(8,128)(2,1)S(1)}, u32[]{:S(2)}, u32[]{:S(2)}) collective-permute-start(bf16[64,512]{1,0:T(8,128)(2,1)S(1)} %get-tuple-element.14), channel_id=1, source_target_pairs={{0,10},{2,12},{4,14},{6,0},{8,2},{10,4},{12,6},{14,8},{1,11},{3,13... | collective-permute-start | bytes 196616 | tf_op jit(solution)/shard_map/ppermute | solution.py:287
  27.7 3.2 %collective-permute-done.3 = bf16[64,512]{1,0:T(8,128)(2,1)S(1)} collective-permute-done((bf16[64,512]{1,0:T(8,128)(2,1)S(1)}, bf16[64,512]{1,0:T(8,128)(2,1)S(1)}, u32[]{:S(2)}, u32[]{:S(2)}) %collective-permute-start.3) | collective-permute-done | bytes 65568 | tf_op jit(solution)/shard_map/ppermute | solution.py:287
  31.8 3.2 %collective-permute-start.7 = (bf16[64,512]{1,0:T(8,128)(2,1)S(1)}, bf16[64,512]{1,0:T(8,128)(2,1)S(1)}, u32[]{:S(2)}, u32[]{:S(2)}) collective-permute-start(bf16[64,512]{1,0:T(8,128)(2,1)S(1)} %fusion.7), channel_id=1, source_target_pairs={{0,16},{16,32},{32,48},{1,17},{17,33},{33,49},{2,18},{18,34},{34,5... | collective-permute-start | bytes 196616 | tf_op jit(solution)/shard_map/ppermute | solution.py:344
  35.0 4.5 %collective-permute-start.6 = (bf16[64,512]{1,0:T(8,128)(2,1)S(1)}, bf16[64,512]{1,0:T(8,128)(2,1)S(1)}, u32[]{:S(2)}, u32[]{:S(2)}) collective-permute-start(bf16[64,512]{1,0:T(8,128)(2,1)S(1)} %fusion.7), channel_id=1, source_target_pairs={{0,32},{16,48},{1,33},{17,49},{2,34},{18,50},{3,35},{19,51},{4,36}... | collective-permute-start | bytes 196616 | tf_op jit(solution)/shard_map/ppermute | solution.py:344
  39.5 1.3 %collective-permute-start.5 = (bf16[64,512]{1,0:T(8,128)(2,1)S(1)}, bf16[64,512]{1,0:T(8,128)(2,1)S(1)}, u32[]{:S(2)}, u32[]{:S(2)}) collective-permute-start(bf16[64,512]{1,0:T(8,128)(2,1)S(1)} %fusion.7), channel_id=1, source_target_pairs={{0,48},{1,49},{2,50},{3,51},{4,52},{5,53},{6,54},{7,55},{8,56},{9,... | collective-permute-start | bytes 196616 | tf_op jit(solution)/shard_map/ppermute | solution.py:344
  41.0 1.1 %collective-permute-done.5 = bf16[64,512]{1,0:T(8,128)(2,1)S(1)} collective-permute-done((bf16[64,512]{1,0:T(8,128)(2,1)S(1)}, bf16[64,512]{1,0:T(8,128)(2,1)S(1)}, u32[]{:S(2)}, u32[]{:S(2)}) %collective-permute-start.5) | collective-permute-done | bytes 65568 | tf_op jit(solution)/shard_map/ppermute | solution.py:344
  42.2 2.2 %collective-permute-start.9 = (bf16[1,64,512]{2,1,0:T(8,128)(2,1)S(1)}, bf16[1,64,512]{2,1,0:T(8,128)(2,1)S(1)}, u32[]{:S(2)}, u32[]{:S(2)}) collective-permute-start(bf16[1,64,512]{2,1,0:T(8,128)(2,1)S(1)} %fusion.8.refs_1_), channel_id=1, source_target_pairs={{0,6},{2,8},{4,10},{6,12},{8,14},{10,0},{12,2},{14,4},{1,7},{3,9},... | collective-permute-start | bytes 196616 | tf_op jit(solution)/shard_map/ppermute | solution.py:287
  44.4 2.3 %collective-permute-start.8 = (bf16[1,64,512]{2,1,0:T(8,128)(2,1)S(1)}, bf16[1,64,512]{2,1,0:T(8,128)(2,1)S(1)}, u32[]{:S(2)}, u32[]{:S(2)}) collective-permute-start(bf16[1,64,512]{2,1,0:T(8,128)(2,1)S(1)} %fusion.8.refs_1_), channel_id=1, source_target_pairs={{0,10},{2,12},{4,14},{6,0},{8,2},{10,4},{12,6},{14,8},{1,11},{3,13... | collective-permute-start | bytes 196616 | tf_op jit(solution)/shard_map/ppermute | solution.py:287
  46.7 3.0 %collective-permute-done.9.refs_2_ = bf16[1,64,512]{2,1,0:T(8,128)(2,1)S(1)} collective-permute-done((bf16[1,64,512]{2,1,0:T(8,128)(2,1)S(1)}, bf16[1,64,512]{2,1,0:T(8,128)(2,1)S(1)}, u32[]{:S(2)}, u32[]{:S(2)}) %collective-permute-start.9) | collective-permute-done | bytes 65568 | tf_op jit(solution)/shard_map/ppermute | solution.py:287
  49.8 2.0 %collective-permute-start.10 = (bf16[3,64,512]{2,1,0:T(8,128)(2,1)S(1)}, bf16[3,64,512]{2,1,0:T(8,128)(2,1)S(1)}, u32[]{:S(2)}, u32[]{:S(2)}) collective-permute-start(bf16[3,64,512]{2,1,0:T(8,128)(2,1)S(1)} %pad_maximum_fusion), channel_id=1, source_target_pairs={{0,2},{2,4},{4,6},{6,8},{8,10},{10,12},{12,14},{14,0},{1,3},{3,5},... | collective-permute-start | bytes 589832 | tf_op jit(solution)/shard_map/ppermute | solution.py:287
  51.8 2.8 %collective-permute-start.11 = (bf16[2,64,512]{2,1,0:T(8,128)(2,1)S(1)}, bf16[2,64,512]{2,1,0:T(8,128)(2,1)S(1)}, u32[]{:S(2)}, u32[]{:S(2)}) collective-permute-start(bf16[2,64,512]{2,1,0:T(8,128)(2,1)S(1)} %pad_maximum_fusion.1), channel_id=1, source_target_pairs={{0,14},{2,0},{4,2},{6,4},{8,6},{10,8},{12,10},{14,12},{1,15},{3,1}... | collective-permute-start | bytes 393224 | tf_op jit(solution)/shard_map/ppermute | solution.py:287
  54.6 4.6 %collective-permute-start.12 = (bf16[3,64,512]{2,1,0:T(8,128)(2,1)S(1)}, bf16[3,64,512]{2,1,0:T(8,128)(2,1)S(1)}, u32[]{:S(2)}, u32[]{:S(2)}) collective-permute-start(bf16[3,64,512]{2,1,0:T(8,128)(2,1)S(1)} %pad_maximum_fusion), channel_id=1, source_target_pairs={{0,1},{1,0},{2,3},{3,2},{4,5},{5,4},{6,7},{7,6},{8,9},{9,8},{10,11... | collective-permute-start | bytes 589832 | tf_op jit(solution)/shard_map/ppermute | solution.py:356
  59.2 3.5 %collective-permute-start.13 = (bf16[3,64,512]{2,1,0:T(8,128)(2,1)S(1)}, bf16[3,64,512]{2,1,0:T(8,128)(2,1)S(1)}, u32[]{:S(2)}, u32[]{:S(2)}) collective-permute-start(bf16[3,64,512]{2,1,0:T(8,128)(2,1)S(1)} %collective-permute-done.10.refs_3_), channel_id=1, source_target_pairs={{0,1},{1,0},{2,3},{3,2},{4,5},{5,4},{6,7},{7,6},{8,9},{9,8},{10,11... | collective-permute-start | bytes 589832 | tf_op jit(solution)/shard_map/ppermute | solution.py:356
  63.1 1.0 %collective-permute-done.14.refs_7_ = bf16[2,64,512]{2,1,0:T(8,128)(2,1)S(1)} collective-permute-done((bf16[2,64,512]{2,1,0:T(8,128)(2,1)S(1)}, bf16[2,64,512]{2,1,0:T(8,128)(2,1)S(1)}, u32[]{:S(2)}, u32[]{:S(2)}) %collective-permute-start.14) | collective-permute-done | bytes 131104 | tf_op jit(solution)/shard_map/ppermute | solution.py:356
  64.1 1.1 %assemble.1 = bf16[64,8192]{1,0:T(8,128)(2,1)} custom-call(s32[1]{0:T(128)} %bitcast.core_ref, s32[1]{0:T(128)} %bitcast.1.chip_ref, bf16[1,64,512]{2,1,0:T(8,128)(2,1)S(1)} %collective-permute-done.8.refs_0_, bf16[1,64,512]{2,1,0:T(8,128)(2,1)S(1)} %fusion.8.refs_1_, bf16[1,64,512]{2,1,0:T(8,128)(2,1)S(1)} %collective-permute-done.9.refs_2_, ...), custom_call_target="tpu_custom_call" | custom-call | tf_op jit(solution)/shard_map/assemble/pallas_call | solution.py:359
  (17 shorter events, 1.7 us)
Async XLA Ops:
  7.9 34.3 %copy-start = (bf16[64,512]{1,0:T(8,128)(2,1)S(1)}, bf16[64,512]{1,0:T(8,128)(2,1)}, u32[]{:S(2)}) copy-start(bf16[64,512]{1,0:T(8,128)(2,1)} %get-tuple-element.8) | copy-start | bytes 196612
  7.9 5.1 %collective-permute-start = (bf16[8,64,512]{2,1,0:T(8,128)(2,1)}, bf16[8,64,512]{2,1,0:T(8,128)(2,1)S(1)}, u32[]{:S(2)}, u32[]{:S(2)}) collective-permute-start(bf16[8,64,512]{2,1,0:T(8,128)(2,1)} %get-tuple-element.10), channel_id=1, source_target_pairs={{0,1},{1,0},{2,3},{3,2},{4,5},{5,4},{6,7},{7,6},{8,9},{9,8},{10,11... | collective-permute-start | bytes 1572872 | tf_op jit(solution)/shard_map/ppermute | solution.py:335
  14.2 8.9 %collective-permute-start.1 = (bf16[3,64,512]{2,1,0:T(8,128)(2,1)S(1)}, bf16[3,64,512]{2,1,0:T(8,128)(2,1)S(1)}, u32[]{:S(2)}, u32[]{:S(2)}) collective-permute-start(bf16[3,64,512]{2,1,0:T(8,128)(2,1)S(1)} %get-tuple-element.11), channel_id=1, source_target_pairs={{0,2},{2,4},{4,6},{6,8},{8,10},{10,12},{12,14},{14,0},{1,3},{3,5},... | collective-permute-start | bytes 589832 | tf_op jit(solution)/shard_map/ppermute | solution.py:287
  15.3 6.4 %collective-permute-start.2 = (bf16[2,64,512]{2,1,0:T(8,128)(2,1)S(1)}, bf16[2,64,512]{2,1,0:T(8,128)(2,1)S(1)}, u32[]{:S(2)}, u32[]{:S(2)}) collective-permute-start(bf16[2,64,512]{2,1,0:T(8,128)(2,1)S(1)} %add_convert_fusion.1), channel_id=1, source_target_pairs={{0,14},{2,0},{4,2},{6,4},{8,6},{10,8},{12,10},{14,12},{1,15},{3,1}... | collective-permute-start | bytes 393224 | tf_op jit(solution)/shard_map/ppermute | solution.py:287
  23.1 7.8 %collective-permute-start.3 = (bf16[64,512]{1,0:T(8,128)(2,1)S(1)}, bf16[64,512]{1,0:T(8,128)(2,1)S(1)}, u32[]{:S(2)}, u32[]{:S(2)}) collective-permute-start(bf16[64,512]{1,0:T(8,128)(2,1)S(1)} %get-tuple-element.13), channel_id=1, source_target_pairs={{0,6},{2,8},{4,10},{6,12},{8,14},{10,0},{12,2},{14,4},{1,7},{3,9},... | collective-permute-start | bytes 196616 | tf_op jit(solution)/shard_map/ppermute | solution.py:287
  26.5 5.2 %collective-permute-start.4 = (bf16[64,512]{1,0:T(8,128)(2,1)S(1)}, bf16[64,512]{1,0:T(8,128)(2,1)S(1)}, u32[]{:S(2)}, u32[]{:S(2)}) collective-permute-start(bf16[64,512]{1,0:T(8,128)(2,1)S(1)} %get-tuple-element.14), channel_id=1, source_target_pairs={{0,10},{2,12},{4,14},{6,0},{8,2},{10,4},{12,6},{14,8},{1,11},{3,13... | collective-permute-start | bytes 196616 | tf_op jit(solution)/shard_map/ppermute | solution.py:287
  31.8 9.1 %collective-permute-start.7 = (bf16[64,512]{1,0:T(8,128)(2,1)S(1)}, bf16[64,512]{1,0:T(8,128)(2,1)S(1)}, u32[]{:S(2)}, u32[]{:S(2)}) collective-permute-start(bf16[64,512]{1,0:T(8,128)(2,1)S(1)} %fusion.7), channel_id=1, source_target_pairs={{0,16},{16,32},{32,48},{1,17},{17,33},{33,49},{2,18},{18,34},{34,5... | collective-permute-start | bytes 196616 | tf_op jit(solution)/shard_map/ppermute | solution.py:344
  35.0 6.1 %collective-permute-start.6 = (bf16[64,512]{1,0:T(8,128)(2,1)S(1)}, bf16[64,512]{1,0:T(8,128)(2,1)S(1)}, u32[]{:S(2)}, u32[]{:S(2)}) collective-permute-start(bf16[64,512]{1,0:T(8,128)(2,1)S(1)} %fusion.7), channel_id=1, source_target_pairs={{0,32},{16,48},{1,33},{17,49},{2,34},{18,50},{3,35},{19,51},{4,36}... | collective-permute-start | bytes 196616 | tf_op jit(solution)/shard_map/ppermute | solution.py:344
  39.5 2.6 %collective-permute-start.5 = (bf16[64,512]{1,0:T(8,128)(2,1)S(1)}, bf16[64,512]{1,0:T(8,128)(2,1)S(1)}, u32[]{:S(2)}, u32[]{:S(2)}) collective-permute-start(bf16[64,512]{1,0:T(8,128)(2,1)S(1)} %fusion.7), channel_id=1, source_target_pairs={{0,48},{1,49},{2,50},{3,51},{4,52},{5,53},{6,54},{7,55},{8,56},{9,... | collective-permute-start | bytes 196616 | tf_op jit(solution)/shard_map/ppermute | solution.py:344
  42.2 7.6 %collective-permute-start.9 = (bf16[1,64,512]{2,1,0:T(8,128)(2,1)S(1)}, bf16[1,64,512]{2,1,0:T(8,128)(2,1)S(1)}, u32[]{:S(2)}, u32[]{:S(2)}) collective-permute-start(bf16[1,64,512]{2,1,0:T(8,128)(2,1)S(1)} %fusion.8.refs_1_), channel_id=1, source_target_pairs={{0,6},{2,8},{4,10},{6,12},{8,14},{10,0},{12,2},{14,4},{1,7},{3,9},... | collective-permute-start | bytes 196616 | tf_op jit(solution)/shard_map/ppermute | solution.py:287
  44.4 5.4 %collective-permute-start.8 = (bf16[1,64,512]{2,1,0:T(8,128)(2,1)S(1)}, bf16[1,64,512]{2,1,0:T(8,128)(2,1)S(1)}, u32[]{:S(2)}, u32[]{:S(2)}) collective-permute-start(bf16[1,64,512]{2,1,0:T(8,128)(2,1)S(1)} %fusion.8.refs_1_), channel_id=1, source_target_pairs={{0,10},{2,12},{4,14},{6,0},{8,2},{10,4},{12,6},{14,8},{1,11},{3,13... | collective-permute-start | bytes 196616 | tf_op jit(solution)/shard_map/ppermute | solution.py:287
  49.8 9.4 %collective-permute-start.10 = (bf16[3,64,512]{2,1,0:T(8,128)(2,1)S(1)}, bf16[3,64,512]{2,1,0:T(8,128)(2,1)S(1)}, u32[]{:S(2)}, u32[]{:S(2)}) collective-permute-start(bf16[3,64,512]{2,1,0:T(8,128)(2,1)S(1)} %pad_maximum_fusion), channel_id=1, source_target_pairs={{0,2},{2,4},{4,6},{6,8},{8,10},{10,12},{12,14},{14,0},{1,3},{3,5},... | collective-permute-start | bytes 589832 | tf_op jit(solution)/shard_map/ppermute | solution.py:287
  51.8 11.0 %collective-permute-start.11 = (bf16[2,64,512]{2,1,0:T(8,128)(2,1)S(1)}, bf16[2,64,512]{2,1,0:T(8,128)(2,1)S(1)}, u32[]{:S(2)}, u32[]{:S(2)}) collective-permute-start(bf16[2,64,512]{2,1,0:T(8,128)(2,1)S(1)} %pad_maximum_fusion.1), channel_id=1, source_target_pairs={{0,14},{2,0},{4,2},{6,4},{8,6},{10,8},{12,10},{14,12},{1,15},{3,1}... | collective-permute-start | bytes 393224 | tf_op jit(solution)/shard_map/ppermute | solution.py:287
  54.6 8.5 %collective-permute-start.12 = (bf16[3,64,512]{2,1,0:T(8,128)(2,1)S(1)}, bf16[3,64,512]{2,1,0:T(8,128)(2,1)S(1)}, u32[]{:S(2)}, u32[]{:S(2)}) collective-permute-start(bf16[3,64,512]{2,1,0:T(8,128)(2,1)S(1)} %pad_maximum_fusion), channel_id=1, source_target_pairs={{0,1},{1,0},{2,3},{3,2},{4,5},{5,4},{6,7},{7,6},{8,9},{9,8},{10,11... | collective-permute-start | bytes 589832 | tf_op jit(solution)/shard_map/ppermute | solution.py:356
  59.2 4.9 %collective-permute-start.13 = (bf16[3,64,512]{2,1,0:T(8,128)(2,1)S(1)}, bf16[3,64,512]{2,1,0:T(8,128)(2,1)S(1)}, u32[]{:S(2)}, u32[]{:S(2)}) collective-permute-start(bf16[3,64,512]{2,1,0:T(8,128)(2,1)S(1)} %collective-permute-done.10.refs_3_), channel_id=1, source_target_pairs={{0,1},{1,0},{2,3},{3,2},{4,5},{5,4},{6,7},{7,6},{8,9},{9,8},{10,11... | collective-permute-start | bytes 589832 | tf_op jit(solution)/shard_map/ppermute | solution.py:356
  62.8 1.3 %collective-permute-start.14 = (bf16[2,64,512]{2,1,0:T(8,128)(2,1)S(1)}, bf16[2,64,512]{2,1,0:T(8,128)(2,1)S(1)}, u32[]{:S(2)}, u32[]{:S(2)}) collective-permute-start(bf16[2,64,512]{2,1,0:T(8,128)(2,1)S(1)} %collective-permute-done.11.refs_4_), channel_id=1, source_target_pairs={{0,1},{1,0},{2,3},{3,2},{4,5},{5,4},{6,7},{7,6},{8,9},{9,8},{10,11... | collective-permute-start | bytes 393224 | tf_op jit(solution)/shard_map/ppermute | solution.py:356

commit v4 on v3

--- a/solution.py
+++ b/solution.py
@@ -315,21 +315,26 @@
             pltpu.SemaphoreType.DMA((2,)),
             pltpu.SemaphoreType.DMA((cores * chips,)),
         ],
-        compiler_params=pltpu.CompilerParams(vmem_limit_bytes=58368 * KIB),
+        compiler_params=pltpu.CompilerParams(vmem_limit_bytes=40960 * KIB),
         name="attend",
     )(
         core,
         chip,
-        cache_lengths,
-        positions,
-        jnp.asarray(rates),
-        queries,
-        new_keys,
-        new_values,
-        cache_keys,
-        cache_values,
-        out_weight,
-        hidden_in,
+        *(
+            pltpu.with_memory_space_constraint(array, pltpu.HBM)
+            for array in (
+                cache_lengths,
+                positions,
+                jnp.asarray(rates),
+                queries,
+                new_keys,
+                new_values,
+                cache_keys,
+                cache_values,
+                out_weight,
+                hidden_in,
+            )
+        ),
     )
 
     got = lax.ppermute(send, "core", SWAP)

time: 65.4 us -> 62.9 us (0.962)
  other arithmetic: 2.38 us -> 0.34 us
  Pallas kernels: 8.95 us -> 7.8 us
    convert_element_type x4, other arithmetic: 2.29 us -> 0.25 us  [narrow(): return array.astype(jnp.bfloat16)]
    pallas_call x1, Pallas kernels: 7.86 us -> 6.71 us  [per_device(): pl.pallas_call(attend, out_shape=(jax.ShapeDtypeStruct((chips, flat, shar...]
  transfers between devices with their start and end apart: 15 -> 15, of which waited for: 9 -> 8; matrix products, arithmetic and copies ran while one was open for 2% -> 0% of each run, Pallas kernels for 0% -> 0%
where the time goes in v4:
time: 62.9 us; the launch traced here: 62.8 us
  starting transfers between devices  39.3 us (62%)
  waiting for transfers between devices  15.2 us (24%)
  Pallas kernels  7.8 us (12%)
    ppermute x8, starting transfers between devices, shift(): lax.ppermute(array, 'z', [(i, (i + by) % chips) for i in range(chips)])  18 us
    ppermute x8, waiting for transfers between devices, shift(): lax.ppermute(array, 'z', [(i, (i + by) % chips) for i in range(chips)])  11 us
    ppermute x3, starting transfers between devices, per_device(): lax.ppermute(piece, 'core', SWAP)  9.03 us
    ppermute x3, starting transfers between devices, per_device(): lax.ppermute(update, 'section', [(i, i + by) for i in range(sections - by)])  9.02 us
    pallas_call x1, Pallas kernels, per_device(): pl.pallas_call(attend, out_shape=(jax.ShapeDtypeStruct((chips, flat, shar...  6.71 us
    ppermute x1, starting transfers between devices, per_device(): got = lax.ppermute(send, 'core', SWAP)  3.33 us
    ppermute x1, waiting for transfers between devices, per_device(): got = lax.ppermute(send, 'core', SWAP)  1.54 us
    ppermute x3, waiting for transfers between devices, per_device(): lax.ppermute(piece, 'core', SWAP)  1.35 us
  transfers between devices with their start and end apart: 15, of which 8 were waited for; matrix products, arithmetic and copies ran while one was open for 0% of the time, Pallas kernels for 0%

profile of v4, /device:TPU:1, one launch (start us, length us, event | category | flops | bytes accessed | tf_op | source)
XLA Modules:
  0.0 62.8 jit_solution(12963578618213292303)
XLA Ops:
  0.0 6.7 %attend.1 = (bf16[8,64,512]{2,1,0:T(8,128)(2,1)S(1)}, f32[8,64,512]{2,1,0:T(8,128)S(1)}, bf16[64,512]{1,0:T(8,128)(2,1)S(1)}) custom-call(s32[1]{0:T(128)} %bitcast.core_ref, s32[1]{0:T(128)} %bitcast.1.chip_ref, s32[32]{0:T(128)} %length_hbm.1, s32[32]{0:T(128)} %position_hbm.1, f32[1,128]{1,0:T(1,128)} %constant.10.clone.rate_hbm, ...), custom_call_target="tpu_custom_call" | custom-call | tf_op jit(solution)/shard_map/attend/pallas_call | solution.py:289
  6.7 3.3 %collective-permute-start = (bf16[8,64,512]{2,1,0:T(8,128)(2,1)S(1)}, bf16[8,64,512]{2,1,0:T(8,128)(2,1)S(1)}, u32[]{:S(2)}, u32[]{:S(2)}) collective-permute-start(bf16[8,64,512]{2,1,0:T(8,128)(2,1)S(1)} %get-tuple-element.10), channel_id=1, source_target_pairs={{0,1},{1,0},{2,3},{3,2},{4,5},{5,4},{6,7},{7,6},{8,9},{9,8},{10,11... | collective-permute-start | bytes 1572872 | tf_op jit(solution)/shard_map/ppermute | solution.py:340
  10.0 1.5 %collective-permute-done = bf16[8,64,512]{2,1,0:T(8,128)(2,1)S(1)} collective-permute-done((bf16[8,64,512]{2,1,0:T(8,128)(2,1)S(1)}, bf16[8,64,512]{2,1,0:T(8,128)(2,1)S(1)}, u32[]{:S(2)}, u32[]{:S(2)}) %collective-permute-start) | collective-permute-done | bytes 524320 | tf_op jit(solution)/shard_map/ppermute | solution.py:340
  11.6 0.1 add_convert_fusion
  11.7 0.1 collective-permute-start.1
  11.8 3.9 %collective-permute-start.2 = (bf16[2,64,512]{2,1,0:T(8,128)(2,1)S(1)}, bf16[2,64,512]{2,1,0:T(8,128)(2,1)S(1)}, u32[]{:S(2)}, u32[]{:S(2)}) collective-permute-start(bf16[2,64,512]{2,1,0:T(8,128)(2,1)S(1)} %add_convert_fusion.1), channel_id=1, source_target_pairs={{0,14},{2,0},{4,2},{6,4},{8,6},{10,8},{12,10},{14,12},{1,15},{3,1}... | collective-permute-start | bytes 393224 | tf_op jit(solution)/shard_map/ppermute | solution.py:287
  15.8 2.5 %collective-permute-done.2 = bf16[2,64,512]{2,1,0:T(8,128)(2,1)S(1)} collective-permute-done((bf16[2,64,512]{2,1,0:T(8,128)(2,1)S(1)}, bf16[2,64,512]{2,1,0:T(8,128)(2,1)S(1)}, u32[]{:S(2)}, u32[]{:S(2)}) %collective-permute-start.2) | collective-permute-done | bytes 131104 | tf_op jit(solution)/shard_map/ppermute | solution.py:287
  18.3 2.3 %collective-permute-done.1 = bf16[3,64,512]{2,1,0:T(8,128)(2,1)S(1)} collective-permute-done((bf16[3,64,512]{2,1,0:T(8,128)(2,1)S(1)}, bf16[3,64,512]{2,1,0:T(8,128)(2,1)S(1)}, u32[]{:S(2)}, u32[]{:S(2)}) %collective-permute-start.1) | collective-permute-done | bytes 196640 | tf_op jit(solution)/shard_map/ppermute | solution.py:287
  20.7 2.4 %collective-permute-start.3 = (bf16[64,512]{1,0:T(8,128)(2,1)S(1)}, bf16[64,512]{1,0:T(8,128)(2,1)S(1)}, u32[]{:S(2)}, u32[]{:S(2)}) collective-permute-start(bf16[64,512]{1,0:T(8,128)(2,1)S(1)} %get-tuple-element.13), channel_id=1, source_target_pairs={{0,6},{2,8},{4,10},{6,12},{8,14},{10,0},{12,2},{14,4},{1,7},{3,9},... | collective-permute-start | bytes 196616 | tf_op jit(solution)/shard_map/ppermute | solution.py:287
  23.1 2.1 %collective-permute-start.4 = (bf16[64,512]{1,0:T(8,128)(2,1)S(1)}, bf16[64,512]{1,0:T(8,128)(2,1)S(1)}, u32[]{:S(2)}, u32[]{:S(2)}) collective-permute-start(bf16[64,512]{1,0:T(8,128)(2,1)S(1)} %get-tuple-element.14), channel_id=1, source_target_pairs={{0,10},{2,12},{4,14},{6,0},{8,2},{10,4},{12,6},{14,8},{1,11},{3,13... | collective-permute-start | bytes 196616 | tf_op jit(solution)/shard_map/ppermute | solution.py:287
  25.2 2.0 %collective-permute-done.3 = bf16[64,512]{1,0:T(8,128)(2,1)S(1)} collective-permute-done((bf16[64,512]{1,0:T(8,128)(2,1)S(1)}, bf16[64,512]{1,0:T(8,128)(2,1)S(1)}, u32[]{:S(2)}, u32[]{:S(2)}) %collective-permute-start.3) | collective-permute-done | bytes 65568 | tf_op jit(solution)/shard_map/ppermute | solution.py:287
  27.2 1.1 %collective-permute-done.4 = bf16[64,512]{1,0:T(8,128)(2,1)S(1)} collective-permute-done((bf16[64,512]{1,0:T(8,128)(2,1)S(1)}, bf16[64,512]{1,0:T(8,128)(2,1)S(1)}, u32[]{:S(2)}, u32[]{:S(2)}) %collective-permute-start.4) | collective-permute-done | bytes 65568 | tf_op jit(solution)/shard_map/ppermute | solution.py:287
  28.3 3.2 %collective-permute-start.7 = (bf16[64,512]{1,0:T(8,128)(2,1)S(1)}, bf16[64,512]{1,0:T(8,128)(2,1)S(1)}, u32[]{:S(2)}, u32[]{:S(2)}) collective-permute-start(bf16[64,512]{1,0:T(8,128)(2,1)S(1)} %fusion.7), channel_id=1, source_target_pairs={{0,16},{16,32},{32,48},{1,17},{17,33},{33,49},{2,18},{18,34},{34,5... | collective-permute-start | bytes 196616 | tf_op jit(solution)/shard_map/ppermute | solution.py:349
  31.6 4.5 %collective-permute-start.6 = (bf16[64,512]{1,0:T(8,128)(2,1)S(1)}, bf16[64,512]{1,0:T(8,128)(2,1)S(1)}, u32[]{:S(2)}, u32[]{:S(2)}) collective-permute-start(bf16[64,512]{1,0:T(8,128)(2,1)S(1)} %fusion.7), channel_id=1, source_target_pairs={{0,32},{16,48},{1,33},{17,49},{2,34},{18,50},{3,35},{19,51},{4,36}... | collective-permute-start | bytes 196616 | tf_op jit(solution)/shard_map/ppermute | solution.py:349
  36.1 1.3 %collective-permute-start.5 = (bf16[64,512]{1,0:T(8,128)(2,1)S(1)}, bf16[64,512]{1,0:T(8,128)(2,1)S(1)}, u32[]{:S(2)}, u32[]{:S(2)}) collective-permute-start(bf16[64,512]{1,0:T(8,128)(2,1)S(1)} %fusion.7), channel_id=1, source_target_pairs={{0,48},{1,49},{2,50},{3,51},{4,52},{5,53},{6,54},{7,55},{8,56},{9,... | collective-permute-start | bytes 196616 | tf_op jit(solution)/shard_map/ppermute | solution.py:349
  37.4 1.3 %collective-permute-done.5 = bf16[64,512]{1,0:T(8,128)(2,1)S(1)} collective-permute-done((bf16[64,512]{1,0:T(8,128)(2,1)S(1)}, bf16[64,512]{1,0:T(8,128)(2,1)S(1)}, u32[]{:S(2)}, u32[]{:S(2)}) %collective-permute-start.5) | collective-permute-done | bytes 65568 | tf_op jit(solution)/shard_map/ppermute | solution.py:349
  38.8 2.4 %collective-permute-start.9 = (bf16[1,64,512]{2,1,0:T(8,128)(2,1)S(1)}, bf16[1,64,512]{2,1,0:T(8,128)(2,1)S(1)}, u32[]{:S(2)}, u32[]{:S(2)}) collective-permute-start(bf16[1,64,512]{2,1,0:T(8,128)(2,1)S(1)} %fusion.8.refs_1_), channel_id=1, source_target_pairs={{0,6},{2,8},{4,10},{6,12},{8,14},{10,0},{12,2},{14,4},{1,7},{3,9},... | collective-permute-start | bytes 196616 | tf_op jit(solution)/shard_map/ppermute | solution.py:287
  41.1 2.2 %collective-permute-start.8 = (bf16[1,64,512]{2,1,0:T(8,128)(2,1)S(1)}, bf16[1,64,512]{2,1,0:T(8,128)(2,1)S(1)}, u32[]{:S(2)}, u32[]{:S(2)}) collective-permute-start(bf16[1,64,512]{2,1,0:T(8,128)(2,1)S(1)} %fusion.8.refs_1_), channel_id=1, source_target_pairs={{0,10},{2,12},{4,14},{6,0},{8,2},{10,4},{12,6},{14,8},{1,11},{3,13... | collective-permute-start | bytes 196616 | tf_op jit(solution)/shard_map/ppermute | solution.py:287
  43.3 3.1 %collective-permute-done.9.refs_2_ = bf16[1,64,512]{2,1,0:T(8,128)(2,1)S(1)} collective-permute-done((bf16[1,64,512]{2,1,0:T(8,128)(2,1)S(1)}, bf16[1,64,512]{2,1,0:T(8,128)(2,1)S(1)}, u32[]{:S(2)}, u32[]{:S(2)}) %collective-permute-start.9) | collective-permute-done | bytes 65568 | tf_op jit(solution)/shard_map/ppermute | solution.py:287
  46.4 4.8 %collective-permute-start.10 = (bf16[3,64,512]{2,1,0:T(8,128)(2,1)S(1)}, bf16[3,64,512]{2,1,0:T(8,128)(2,1)S(1)}, u32[]{:S(2)}, u32[]{:S(2)}) collective-permute-start(bf16[3,64,512]{2,1,0:T(8,128)(2,1)S(1)} %pad_maximum_fusion), channel_id=1, source_target_pairs={{0,2},{2,4},{4,6},{6,8},{8,10},{10,12},{12,14},{14,0},{1,3},{3,5},... | collective-permute-start | bytes 589832 | tf_op jit(solution)/shard_map/ppermute | solution.py:287
  51.3 5.5 %collective-permute-start.12 = (bf16[3,64,512]{2,1,0:T(8,128)(2,1)S(1)}, bf16[3,64,512]{2,1,0:T(8,128)(2,1)S(1)}, u32[]{:S(2)}, u32[]{:S(2)}) collective-permute-start(bf16[3,64,512]{2,1,0:T(8,128)(2,1)S(1)} %pad_maximum_fusion), channel_id=1, source_target_pairs={{0,1},{1,0},{2,3},{3,2},{4,5},{5,4},{6,7},{7,6},{8,9},{9,8},{10,11... | collective-permute-start | bytes 589832 | tf_op jit(solution)/shard_map/ppermute | solution.py:361
  56.8 3.5 %collective-permute-start.13 = (bf16[3,64,512]{2,1,0:T(8,128)(2,1)S(1)}, bf16[3,64,512]{2,1,0:T(8,128)(2,1)S(1)}, u32[]{:S(2)}, u32[]{:S(2)}) collective-permute-start(bf16[3,64,512]{2,1,0:T(8,128)(2,1)S(1)} %collective-permute-done.10.refs_3_), channel_id=1, source_target_pairs={{0,1},{1,0},{2,3},{3,2},{4,5},{5,4},{6,7},{7,6},{8,9},{9,8},{10,11... | collective-permute-start | bytes 589832 | tf_op jit(solution)/shard_map/ppermute | solution.py:361
  60.3 1.3 %collective-permute-done.14.refs_7_ = bf16[2,64,512]{2,1,0:T(8,128)(2,1)S(1)} collective-permute-done((bf16[2,64,512]{2,1,0:T(8,128)(2,1)S(1)}, bf16[2,64,512]{2,1,0:T(8,128)(2,1)S(1)}, u32[]{:S(2)}, u32[]{:S(2)}) %collective-permute-start.14) | collective-permute-done | bytes 131104 | tf_op jit(solution)/shard_map/ppermute | solution.py:361
  61.7 1.1 %assemble.1 = bf16[64,8192]{1,0:T(8,128)(2,1)} custom-call(s32[1]{0:T(128)} %bitcast.core_ref, s32[1]{0:T(128)} %bitcast.1.chip_ref, bf16[1,64,512]{2,1,0:T(8,128)(2,1)S(1)} %collective-permute-done.8.refs_0_, bf16[1,64,512]{2,1,0:T(8,128)(2,1)S(1)} %fusion.8.refs_1_, bf16[1,64,512]{2,1,0:T(8,128)(2,1)S(1)} %collective-permute-done.9.refs_2_, ...), custom_call_target="tpu_custom_call" | custom-call | tf_op jit(solution)/shard_map/assemble/pallas_call | solution.py:364
  (15 shorter events, 0.3 us)
Async XLA Ops:
  6.7 4.9 %collective-permute-start = (bf16[8,64,512]{2,1,0:T(8,128)(2,1)S(1)}, bf16[8,64,512]{2,1,0:T(8,128)(2,1)S(1)}, u32[]{:S(2)}, u32[]{:S(2)}) collective-permute-start(bf16[8,64,512]{2,1,0:T(8,128)(2,1)S(1)} %get-tuple-element.10), channel_id=1, source_target_pairs={{0,1},{1,0},{2,3},{3,2},{4,5},{5,4},{6,7},{7,6},{8,9},{9,8},{10,11... | collective-permute-start | bytes 1572872 | tf_op jit(solution)/shard_map/ppermute | solution.py:340
  11.7 8.9 %collective-permute-start.1 = (bf16[3,64,512]{2,1,0:T(8,128)(2,1)S(1)}, bf16[3,64,512]{2,1,0:T(8,128)(2,1)S(1)}, u32[]{:S(2)}, u32[]{:S(2)}) collective-permute-start(bf16[3,64,512]{2,1,0:T(8,128)(2,1)S(1)} %get-tuple-element.11), channel_id=1, source_target_pairs={{0,2},{2,4},{4,6},{6,8},{8,10},{10,12},{12,14},{14,0},{1,3},{3,5},... | collective-permute-start | bytes 589832 | tf_op jit(solution)/shard_map/ppermute | solution.py:287
  11.8 6.4 %collective-permute-start.2 = (bf16[2,64,512]{2,1,0:T(8,128)(2,1)S(1)}, bf16[2,64,512]{2,1,0:T(8,128)(2,1)S(1)}, u32[]{:S(2)}, u32[]{:S(2)}) collective-permute-start(bf16[2,64,512]{2,1,0:T(8,128)(2,1)S(1)} %add_convert_fusion.1), channel_id=1, source_target_pairs={{0,14},{2,0},{4,2},{6,4},{8,6},{10,8},{12,10},{14,12},{1,15},{3,1}... | collective-permute-start | bytes 393224 | tf_op jit(solution)/shard_map/ppermute | solution.py:287
  20.7 6.6 %collective-permute-start.3 = (bf16[64,512]{1,0:T(8,128)(2,1)S(1)}, bf16[64,512]{1,0:T(8,128)(2,1)S(1)}, u32[]{:S(2)}, u32[]{:S(2)}) collective-permute-start(bf16[64,512]{1,0:T(8,128)(2,1)S(1)} %get-tuple-element.13), channel_id=1, source_target_pairs={{0,6},{2,8},{4,10},{6,12},{8,14},{10,0},{12,2},{14,4},{1,7},{3,9},... | collective-permute-start | bytes 196616 | tf_op jit(solution)/shard_map/ppermute | solution.py:287
  23.1 5.2 %collective-permute-start.4 = (bf16[64,512]{1,0:T(8,128)(2,1)S(1)}, bf16[64,512]{1,0:T(8,128)(2,1)S(1)}, u32[]{:S(2)}, u32[]{:S(2)}) collective-permute-start(bf16[64,512]{1,0:T(8,128)(2,1)S(1)} %get-tuple-element.14), channel_id=1, source_target_pairs={{0,10},{2,12},{4,14},{6,0},{8,2},{10,4},{12,6},{14,8},{1,11},{3,13... | collective-permute-start | bytes 196616 | tf_op jit(solution)/shard_map/ppermute | solution.py:287
  28.3 9.1 %collective-permute-start.7 = (bf16[64,512]{1,0:T(8,128)(2,1)S(1)}, bf16[64,512]{1,0:T(8,128)(2,1)S(1)}, u32[]{:S(2)}, u32[]{:S(2)}) collective-permute-start(bf16[64,512]{1,0:T(8,128)(2,1)S(1)} %fusion.7), channel_id=1, source_target_pairs={{0,16},{16,32},{32,48},{1,17},{17,33},{33,49},{2,18},{18,34},{34,5... | collective-permute-start | bytes 196616 | tf_op jit(solution)/shard_map/ppermute | solution.py:349
  31.6 5.9 %collective-permute-start.6 = (bf16[64,512]{1,0:T(8,128)(2,1)S(1)}, bf16[64,512]{1,0:T(8,128)(2,1)S(1)}, u32[]{:S(2)}, u32[]{:S(2)}) collective-permute-start(bf16[64,512]{1,0:T(8,128)(2,1)S(1)} %fusion.7), channel_id=1, source_target_pairs={{0,32},{16,48},{1,33},{17,49},{2,34},{18,50},{3,35},{19,51},{4,36}... | collective-permute-start | bytes 196616 | tf_op jit(solution)/shard_map/ppermute | solution.py:349
  36.1 2.6 %collective-permute-start.5 = (bf16[64,512]{1,0:T(8,128)(2,1)S(1)}, bf16[64,512]{1,0:T(8,128)(2,1)S(1)}, u32[]{:S(2)}, u32[]{:S(2)}) collective-permute-start(bf16[64,512]{1,0:T(8,128)(2,1)S(1)} %fusion.7), channel_id=1, source_target_pairs={{0,48},{1,49},{2,50},{3,51},{4,52},{5,53},{6,54},{7,55},{8,56},{9,... | collective-permute-start | bytes 196616 | tf_op jit(solution)/shard_map/ppermute | solution.py:349
  38.8 7.6 %collective-permute-start.9 = (bf16[1,64,512]{2,1,0:T(8,128)(2,1)S(1)}, bf16[1,64,512]{2,1,0:T(8,128)(2,1)S(1)}, u32[]{:S(2)}, u32[]{:S(2)}) collective-permute-start(bf16[1,64,512]{2,1,0:T(8,128)(2,1)S(1)} %fusion.8.refs_1_), channel_id=1, source_target_pairs={{0,6},{2,8},{4,10},{6,12},{8,14},{10,0},{12,2},{14,4},{1,7},{3,9},... | collective-permute-start | bytes 196616 | tf_op jit(solution)/shard_map/ppermute | solution.py:287
  41.1 5.2 %collective-permute-start.8 = (bf16[1,64,512]{2,1,0:T(8,128)(2,1)S(1)}, bf16[1,64,512]{2,1,0:T(8,128)(2,1)S(1)}, u32[]{:S(2)}, u32[]{:S(2)}) collective-permute-start(bf16[1,64,512]{2,1,0:T(8,128)(2,1)S(1)} %fusion.8.refs_1_), channel_id=1, source_target_pairs={{0,10},{2,12},{4,14},{6,0},{8,2},{10,4},{12,6},{14,8},{1,11},{3,13... | collective-permute-start | bytes 196616 | tf_op jit(solution)/shard_map/ppermute | solution.py:287
  46.4 10.4 %collective-permute-start.10 = (bf16[3,64,512]{2,1,0:T(8,128)(2,1)S(1)}, bf16[3,64,512]{2,1,0:T(8,128)(2,1)S(1)}, u32[]{:S(2)}, u32[]{:S(2)}) collective-permute-start(bf16[3,64,512]{2,1,0:T(8,128)(2,1)S(1)} %pad_maximum_fusion), channel_id=1, source_target_pairs={{0,2},{2,4},{4,6},{6,8},{8,10},{10,12},{12,14},{14,0},{1,3},{3,5},... | collective-permute-start | bytes 589832 | tf_op jit(solution)/shard_map/ppermute | solution.py:287
  51.2 9.1 %collective-permute-start.11 = (bf16[2,64,512]{2,1,0:T(8,128)(2,1)S(1)}, bf16[2,64,512]{2,1,0:T(8,128)(2,1)S(1)}, u32[]{:S(2)}, u32[]{:S(2)}) collective-permute-start(bf16[2,64,512]{2,1,0:T(8,128)(2,1)S(1)} %pad_maximum_fusion.1), channel_id=1, source_target_pairs={{0,14},{2,0},{4,2},{6,4},{8,6},{10,8},{12,10},{14,12},{1,15},{3,1}... | collective-permute-start | bytes 393224 | tf_op jit(solution)/shard_map/ppermute | solution.py:287
  51.3 9.0 %collective-permute-start.12 = (bf16[3,64,512]{2,1,0:T(8,128)(2,1)S(1)}, bf16[3,64,512]{2,1,0:T(8,128)(2,1)S(1)}, u32[]{:S(2)}, u32[]{:S(2)}) collective-permute-start(bf16[3,64,512]{2,1,0:T(8,128)(2,1)S(1)} %pad_maximum_fusion), channel_id=1, source_target_pairs={{0,1},{1,0},{2,3},{3,2},{4,5},{5,4},{6,7},{7,6},{8,9},{9,8},{10,11... | collective-permute-start | bytes 589832 | tf_op jit(solution)/shard_map/ppermute | solution.py:361
  56.8 4.9 %collective-permute-start.13 = (bf16[3,64,512]{2,1,0:T(8,128)(2,1)S(1)}, bf16[3,64,512]{2,1,0:T(8,128)(2,1)S(1)}, u32[]{:S(2)}, u32[]{:S(2)}) collective-permute-start(bf16[3,64,512]{2,1,0:T(8,128)(2,1)S(1)} %collective-permute-done.10.refs_3_), channel_id=1, source_target_pairs={{0,1},{1,0},{2,3},{3,2},{4,5},{5,4},{6,7},{7,6},{8,9},{9,8},{10,11... | collective-permute-start | bytes 589832 | tf_op jit(solution)/shard_map/ppermute | solution.py:361
  60.3 1.3 %collective-permute-start.14 = (bf16[2,64,512]{2,1,0:T(8,128)(2,1)S(1)}, bf16[2,64,512]{2,1,0:T(8,128)(2,1)S(1)}, u32[]{:S(2)}, u32[]{:S(2)}) collective-permute-start(bf16[2,64,512]{2,1,0:T(8,128)(2,1)S(1)} %collective-permute-done.11.refs_4_), channel_id=1, source_target_pairs={{0,1},{1,0},{2,3},{3,2},{4,5},{5,4},{6,7},{7,6},{8,9},{9,8},{10,11... | collective-permute-start | bytes 393224 | tf_op jit(solution)/shard_map/ppermute | solution.py:361

commit v5 on v4

--- a/solution.py
+++ b/solution.py
@@ -63,7 +63,7 @@
     chip = chip_ref[0]
 
     def columns(half, offset):
-        block = half * chips + lax.rem(chip + (offset + chips), chips)
+        block = half * chips + lax.rem(chip + ((1 - 2 * half) * offset + chips), chips)
         return pl.ds(pl.multiple_of(block * width, width), width)
 
     small = [
@@ -210,14 +210,15 @@
 
 
 PIECES = (
-    (False, (3,)),
+    (False, (-2,)),
     (False, (0,)),
-    (False, (-3,)),
-    (False, (2, -1, -4)),
-    (False, (1, -2)),
-    (True, (3, 0, -3)),
-    (True, (2, -1, -4)),
-    (True, (1, -2)),
+    (False, (2,)),
+    (False, (4,)),
+    (False, (-3, -1)),
+    (False, (3, 1)),
+    (True, (-2, 0, 2, 4)),
+    (True, (-3, -1)),
+    (True, (3, 1)),
 )
 
 
@@ -231,7 +232,7 @@
         width = ref.shape[-1]
         chips = model // width // 2
         for i, offset in enumerate(offsets):
-            block = half * chips + lax.rem(chip + (offset + chips), chips)
+            block = half * chips + lax.rem(chip + ((1 - 2 * half) * offset + chips), chips)
             at = pl.ds(pl.multiple_of(block * width, width), width)
             copies.append(
                 pltpu.make_async_copy(ref.at[i], out_ref.at[:, at], sem.at[len(copies)])
@@ -284,7 +285,12 @@
     chip = lax.axis_index("z").astype(jnp.int32).reshape(1)
 
     def shift(array, by):
-        return lax.ppermute(array, "z", [(i, (i + by) % chips) for i in range(chips)])
+        pairs = []
+        for i in range(chips):
+            for c in range(cores):
+                j = (i + (1 - 2 * c) * by) % chips
+                pairs.append((i * cores + c, j * cores + c))
+        return lax.ppermute(array, ("z", "core"), pairs)
 
     send, keep, current = pl.pallas_call(
         attend,
@@ -345,21 +351,28 @@
     above = shift(narrow(stay[2] + widen(up[2]) + widen(down[1])), 3)
     below = shift(narrow(stay[0] + widen(up[0])), -3)
     update = narrow(stay[1] + widen(up[1]) + widen(down[0]) + widen(above) + widen(below))
+    section = lax.axis_index("section")
     updates = [
-        lax.ppermute(update, "section", [(i, i + by) for i in range(sections - by)])
+        jnp.where(
+            section >= by,
+            lax.ppermute(update, "section", [(i, (i + by) % sections) for i in range(sections)]),
+            0,
+        )
         for by in (1,2,3)
     ]
     updates = [updates[(1,2,3).index(by)] for by in range(sections - 1, 0, -1)] + [update]
     for term in updates:
         current = narrow(widen(current) + widen(term))
     mine = current[None]
-    near = [shift(mine, -3), mine, shift(mine, 3)]
-    up = shift(jnp.concatenate(near), 1)
-    down = shift(jnp.concatenate(near[1:]), -1)
-    pieces = near + [up, down]
-    pieces = pieces + [
+    below = shift(mine, 2)
+    above = shift(mine, -2)
+    across = shift(mine, 4)
+    up = shift(jnp.concatenate([below, mine]), 1)
+    down = shift(jnp.concatenate([above, mine]), -1)
+    pieces = [below, mine, above, across, up, down]
+    pieces += [
         lax.ppermute(piece, "core", SWAP)
-        for piece in (jnp.concatenate(near), up, down)
+        for piece in (jnp.concatenate([below, mine, above, across]), up, down)
     ]
     states = pl.pallas_call(
         assemble,

time: 62.9 us -> 58.8 us (0.935)
  waiting for transfers between devices: 15.2 us -> 13.1 us
  starting transfers between devices: 39.3 us -> 37.4 us
    ppermute x11 -> x12, starting transfers between devices: 27 us -> 25.2 us  [the longest x9 20.1 us: shift(): return lax.ppermute(array, ('z', 'core'), pairs)]
    ppermute x11 -> x12, waiting for transfers between devices: 12.3 us -> 10.6 us  [the longest x9 8.55 us: shift(): return lax.ppermute(array, ('z', 'core'), pairs)]
  transfers between devices with their start and end apart: 15 -> 16, of which waited for: 8 -> 9; matrix products, arithmetic and copies ran while one was open for 0% -> 0% of each run, Pallas kernels for 0% -> 0%
where the time goes in v5:
time: 58.8 us; the launch traced here: 58.7 us
  starting transfers between devices  37.4 us (64%)
  waiting for transfers between devices  13.1 us (22%)
  Pallas kernels  7.8 us (13%)
    ppermute x9, starting transfers between devices, shift(): return lax.ppermute(array, ('z', 'core'), pairs)  20.1 us
    ppermute x3, starting transfers between devices, per_device(): lax.ppermute(piece, 'core', SWAP)  8.87 us
    ppermute x9, waiting for transfers between devices, shift(): return lax.ppermute(array, ('z', 'core'), pairs)  8.55 us
    pallas_call x1, Pallas kernels, per_device(): pl.pallas_call(attend, out_shape=(jax.ShapeDtypeStruct((chips, flat, shar...  6.71 us
    ppermute x3, starting transfers between devices, per_device(): lax.ppermute(update, 'section', [(i, (i + by) % sections) for i in range(...  5.06 us
    ppermute x1, starting transfers between devices, per_device(): got = lax.ppermute(send, 'core', SWAP)  3.33 us
    ppermute x3, waiting for transfers between devices, per_device(): lax.ppermute(update, 'section', [(i, (i + by) % sections) for i in range(...  2.05 us
    ppermute x1, waiting for transfers between devices, per_device(): got = lax.ppermute(send, 'core', SWAP)  1.54 us
  transfers between devices with their start and end apart: 16, of which 9 were waited for; matrix products, arithmetic and copies ran while one was open for 0% of the time, Pallas kernels for 0%

profile of v5, /device:TPU:1, one launch (start us, length us, event | category | flops | bytes accessed | tf_op | source)
XLA Modules:
  0.0 58.7 jit_solution(4430765477234448358)
XLA Ops:
  0.0 6.7 %attend.1 = (bf16[8,64,512]{2,1,0:T(8,128)(2,1)S(1)}, f32[8,64,512]{2,1,0:T(8,128)S(1)}, bf16[64,512]{1,0:T(8,128)(2,1)S(1)}) custom-call(s32[1]{0:T(128)} %bitcast.core_ref, s32[1]{0:T(128)} %bitcast.1.chip_ref, s32[32]{0:T(128)} %length_hbm.1, s32[32]{0:T(128)} %position_hbm.1, f32[1,128]{1,0:T(1,128)} %constant.25.clone.rate_hbm, ...), custom_call_target="tpu_custom_call" | custom-call | tf_op jit(solution)/shard_map/attend/pallas_call | solution.py:295
  6.7 3.3 %collective-permute-start = (bf16[8,64,512]{2,1,0:T(8,128)(2,1)S(1)}, bf16[8,64,512]{2,1,0:T(8,128)(2,1)S(1)}, u32[]{:S(2)}, u32[]{:S(2)}) collective-permute-start(bf16[8,64,512]{2,1,0:T(8,128)(2,1)S(1)} %get-tuple-element.10), channel_id=1, source_target_pairs={{0,1},{1,0},{2,3},{3,2},{4,5},{5,4},{6,7},{7,6},{8,9},{9,8},{10,11... | collective-permute-start | bytes 1572872 | tf_op jit(solution)/shard_map/ppermute | solution.py:346
  10.0 1.5 %collective-permute-done = bf16[8,64,512]{2,1,0:T(8,128)(2,1)S(1)} collective-permute-done((bf16[8,64,512]{2,1,0:T(8,128)(2,1)S(1)}, bf16[8,64,512]{2,1,0:T(8,128)(2,1)S(1)}, u32[]{:S(2)}, u32[]{:S(2)}) %collective-permute-start) | collective-permute-done | bytes 524320 | tf_op jit(solution)/shard_map/ppermute | solution.py:346
  11.7 3.9 %collective-permute-start.1 = (bf16[3,64,512]{2,1,0:T(8,128)(2,1)S(1)}, bf16[3,64,512]{2,1,0:T(8,128)(2,1)S(1)}, u32[]{:S(2)}, u32[]{:S(2)}) collective-permute-start(bf16[3,64,512]{2,1,0:T(8,128)(2,1)S(1)} %get-tuple-element.11), channel_id=1, source_target_pairs={{0,2},{1,15},{2,4},{3,1},{4,6},{5,3},{6,8},{7,5},{8,10},{9,7},{10,... | collective-permute-start | bytes 589832 | tf_op jit(solution)/shard_map/ppermute | solution.py:293
  15.7 5.0 %collective-permute-done.2 = bf16[2,64,512]{2,1,0:T(8,128)(2,1)S(1)} collective-permute-done((bf16[2,64,512]{2,1,0:T(8,128)(2,1)S(1)}, bf16[2,64,512]{2,1,0:T(8,128)(2,1)S(1)}, u32[]{:S(2)}, u32[]{:S(2)}) %collective-permute-start.2) | collective-permute-done | bytes 131104 | tf_op jit(solution)/shard_map/ppermute | solution.py:293
  20.9 4.5 %collective-permute-start.3 = (bf16[64,512]{1,0:T(8,128)(2,1)S(1)}, bf16[64,512]{1,0:T(8,128)(2,1)S(1)}, u32[]{:S(2)}, u32[]{:S(2)}) collective-permute-start(bf16[64,512]{1,0:T(8,128)(2,1)S(1)} %get-tuple-element.13), channel_id=1, source_target_pairs={{0,6},{1,11},{2,8},{3,13},{4,10},{5,15},{6,12},{7,1},{8,14},{9,3},... | collective-permute-start | bytes 196616 | tf_op jit(solution)/shard_map/ppermute | solution.py:293
  25.4 2.9 %collective-permute-done.4 = bf16[64,512]{1,0:T(8,128)(2,1)S(1)} collective-permute-done((bf16[64,512]{1,0:T(8,128)(2,1)S(1)}, bf16[64,512]{1,0:T(8,128)(2,1)S(1)}, u32[]{:S(2)}, u32[]{:S(2)}) %collective-permute-start.4) | collective-permute-done | bytes 65568 | tf_op jit(solution)/shard_map/ppermute | solution.py:293
  28.3 0.3 collective-permute-done.3
  28.6 1.4 %collective-permute-start.7 = (bf16[64,512]{1,0:T(8,128)(2,1)S(1)}, bf16[64,512]{1,0:T(8,128)(2,1)S(1)}, u32[]{:S(2)}, u32[]{:S(2)}) collective-permute-start(bf16[64,512]{1,0:T(8,128)(2,1)S(1)} %fusion.7), channel_id=1, source_target_pairs={{0,16},{16,32},{32,48},{48,0},{1,17},{17,33},{33,49},{49,1},{2,18}... | collective-permute-start | bytes 196616 | tf_op jit(solution)/shard_map/ppermute | solution.py:358
  30.0 2.6 %collective-permute-start.6 = (bf16[64,512]{1,0:T(8,128)(2,1)S(1)}, bf16[64,512]{1,0:T(8,128)(2,1)S(1)}, u32[]{:S(2)}, u32[]{:S(2)}) collective-permute-start(bf16[64,512]{1,0:T(8,128)(2,1)S(1)} %fusion.7), channel_id=1, source_target_pairs={{0,32},{16,48},{32,0},{48,16},{1,33},{17,49},{33,1},{49,17},{2,34}... | collective-permute-start | bytes 196616 | tf_op jit(solution)/shard_map/ppermute | solution.py:358
  32.6 1.1 %collective-permute-start.5 = (bf16[64,512]{1,0:T(8,128)(2,1)S(1)}, bf16[64,512]{1,0:T(8,128)(2,1)S(1)}, u32[]{:S(2)}, u32[]{:S(2)}) collective-permute-start(bf16[64,512]{1,0:T(8,128)(2,1)S(1)} %fusion.7), channel_id=1, source_target_pairs={{0,48},{16,0},{32,16},{48,32},{1,49},{17,1},{33,17},{49,33},{2,50}... | collective-permute-start | bytes 196616 | tf_op jit(solution)/shard_map/ppermute | solution.py:358
  33.7 1.3 %collective-permute-done.6 = bf16[64,512]{1,0:T(8,128)(2,1)S(1)} collective-permute-done((bf16[64,512]{1,0:T(8,128)(2,1)S(1)}, bf16[64,512]{1,0:T(8,128)(2,1)S(1)}, u32[]{:S(2)}, u32[]{:S(2)}) %collective-permute-start.6) | collective-permute-done | bytes 65568 | tf_op jit(solution)/shard_map/ppermute | solution.py:358
  35.0 0.8 %collective-permute-done.5 = bf16[64,512]{1,0:T(8,128)(2,1)S(1)} collective-permute-done((bf16[64,512]{1,0:T(8,128)(2,1)S(1)}, bf16[64,512]{1,0:T(8,128)(2,1)S(1)}, u32[]{:S(2)}, u32[]{:S(2)}) %collective-permute-start.5) | collective-permute-done | bytes 65568 | tf_op jit(solution)/shard_map/ppermute | solution.py:358
  35.8 2.3 %collective-permute-start.8 = (bf16[1,64,512]{2,1,0:T(8,128)(2,1)S(1)}, bf16[1,64,512]{2,1,0:T(8,128)(2,1)S(1)}, u32[]{:S(2)}, u32[]{:S(2)}) collective-permute-start(bf16[1,64,512]{2,1,0:T(8,128)(2,1)S(1)} %fusion.8.refs_1_), channel_id=1, source_target_pairs={{0,4},{1,13},{2,6},{3,15},{4,8},{5,1},{6,10},{7,3},{8,12},{9,5},{1... | collective-permute-start | bytes 196616 | tf_op jit(solution)/shard_map/ppermute | solution.py:293
  38.1 1.0 %collective-permute-start.9 = (bf16[1,64,512]{2,1,0:T(8,128)(2,1)S(1)}, bf16[1,64,512]{2,1,0:T(8,128)(2,1)S(1)}, u32[]{:S(2)}, u32[]{:S(2)}) collective-permute-start(bf16[1,64,512]{2,1,0:T(8,128)(2,1)S(1)} %fusion.8.refs_1_), channel_id=1, source_target_pairs={{0,12},{1,5},{2,14},{3,7},{4,0},{5,9},{6,2},{7,11},{8,4},{9,13},{1... | collective-permute-start | bytes 196616 | tf_op jit(solution)/shard_map/ppermute | solution.py:293
  39.0 3.9 %collective-permute-start.10 = (bf16[1,64,512]{2,1,0:T(8,128)(2,1)S(1)}, bf16[1,64,512]{2,1,0:T(8,128)(2,1)S(1)}, u32[]{:S(2)}, u32[]{:S(2)}) collective-permute-start(bf16[1,64,512]{2,1,0:T(8,128)(2,1)S(1)} %fusion.8.refs_1_), channel_id=1, source_target_pairs={{0,8},{1,9},{2,10},{3,11},{4,12},{5,13},{6,14},{7,15},{8,0},{9,1},... | collective-permute-start | bytes 196616 | tf_op jit(solution)/shard_map/ppermute | solution.py:293
  43.0 0.3 collective-permute-done.9.refs_2_
  43.3 4.4 %collective-permute-start.11 = (bf16[2,64,512]{2,1,0:T(8,128)(2,1)S(1)}, bf16[2,64,512]{2,1,0:T(8,128)(2,1)S(1)}, u32[]{:S(2)}, u32[]{:S(2)}) collective-permute-start(bf16[2,64,512]{2,1,0:T(8,128)(2,1)S(1)} %get-tuple-element.16), channel_id=1, source_target_pairs={{0,2},{1,15},{2,4},{3,1},{4,6},{5,3},{6,8},{7,5},{8,10},{9,7},{10,... | collective-permute-start | bytes 393224 | tf_op jit(solution)/shard_map/ppermute | solution.py:293
  47.7 6.0 %collective-permute-start.13 = (bf16[4,64,512]{2,1,0:T(8,128)(2,1)S(1)}, bf16[4,64,512]{2,1,0:T(8,128)(2,1)S(1)}, u32[]{:S(2)}, u32[]{:S(2)}) collective-permute-start(bf16[4,64,512]{2,1,0:T(8,128)(2,1)S(1)} %pad_maximum_fusion), channel_id=1, source_target_pairs={{0,1},{1,0},{2,3},{3,2},{4,5},{5,4},{6,7},{7,6},{8,9},{9,8},{10,11... | collective-permute-start | bytes 786440 | tf_op jit(solution)/shard_map/ppermute | solution.py:374
  53.7 2.5 %collective-permute-start.14 = (bf16[2,64,512]{2,1,0:T(8,128)(2,1)S(1)}, bf16[2,64,512]{2,1,0:T(8,128)(2,1)S(1)}, u32[]{:S(2)}, u32[]{:S(2)}) collective-permute-start(bf16[2,64,512]{2,1,0:T(8,128)(2,1)S(1)} %collective-permute-done.11.refs_4_), channel_id=1, source_target_pairs={{0,1},{1,0},{2,3},{3,2},{4,5},{5,4},{6,7},{7,6},{8,9},{9,8},{10,11... | collective-permute-start | bytes 393224 | tf_op jit(solution)/shard_map/ppermute | solution.py:374
  56.3 0.4 collective-permute-start.15
  56.6 0.6 %collective-permute-done.14.refs_7_ = bf16[2,64,512]{2,1,0:T(8,128)(2,1)S(1)} collective-permute-done((bf16[2,64,512]{2,1,0:T(8,128)(2,1)S(1)}, bf16[2,64,512]{2,1,0:T(8,128)(2,1)S(1)}, u32[]{:S(2)}, u32[]{:S(2)}) %collective-permute-start.14) | collective-permute-done | bytes 131104 | tf_op jit(solution)/shard_map/ppermute | solution.py:374
  57.2 0.4 collective-permute-done.15.refs_8_
  57.6 1.1 %assemble.1 = bf16[64,8192]{1,0:T(8,128)(2,1)} custom-call(s32[1]{0:T(128)} %bitcast.core_ref, s32[1]{0:T(128)} %bitcast.1.chip_ref, bf16[1,64,512]{2,1,0:T(8,128)(2,1)S(1)} %collective-permute-done.8.refs_0_, bf16[1,64,512]{2,1,0:T(8,128)(2,1)S(1)} %fusion.8.refs_1_, bf16[1,64,512]{2,1,0:T(8,128)(2,1)S(1)} %collective-permute-done.9.refs_2_, ...), custom_call_target="tpu_custom_call" | custom-call | tf_op jit(solution)/shard_map/assemble/pallas_call | solution.py:377
  (17 shorter events, 0.5 us)
Async XLA Ops:
  6.7 4.9 %collective-permute-start = (bf16[8,64,512]{2,1,0:T(8,128)(2,1)S(1)}, bf16[8,64,512]{2,1,0:T(8,128)(2,1)S(1)}, u32[]{:S(2)}, u32[]{:S(2)}) collective-permute-start(bf16[8,64,512]{2,1,0:T(8,128)(2,1)S(1)} %get-tuple-element.10), channel_id=1, source_target_pairs={{0,1},{1,0},{2,3},{3,2},{4,5},{5,4},{6,7},{7,6},{8,9},{9,8},{10,11... | collective-permute-start | bytes 1572872 | tf_op jit(solution)/shard_map/ppermute | solution.py:346
  11.7 9.1 %collective-permute-start.1 = (bf16[3,64,512]{2,1,0:T(8,128)(2,1)S(1)}, bf16[3,64,512]{2,1,0:T(8,128)(2,1)S(1)}, u32[]{:S(2)}, u32[]{:S(2)}) collective-permute-start(bf16[3,64,512]{2,1,0:T(8,128)(2,1)S(1)} %get-tuple-element.11), channel_id=1, source_target_pairs={{0,2},{1,15},{2,4},{3,1},{4,6},{5,3},{6,8},{7,5},{8,10},{9,7},{10,... | collective-permute-start | bytes 589832 | tf_op jit(solution)/shard_map/ppermute | solution.py:293
  15.7 5.1 %collective-permute-start.2 = (bf16[2,64,512]{2,1,0:T(8,128)(2,1)S(1)}, bf16[2,64,512]{2,1,0:T(8,128)(2,1)S(1)}, u32[]{:S(2)}, u32[]{:S(2)}) collective-permute-start(bf16[2,64,512]{2,1,0:T(8,128)(2,1)S(1)} %add_convert_fusion.1), channel_id=1, source_target_pairs={{0,14},{1,3},{2,0},{3,5},{4,2},{5,7},{6,4},{7,9},{8,6},{9,11},{10,... | collective-permute-start | bytes 393224 | tf_op jit(solution)/shard_map/ppermute | solution.py:293
  20.8 7.4 %collective-permute-start.4 = (bf16[64,512]{1,0:T(8,128)(2,1)S(1)}, bf16[64,512]{1,0:T(8,128)(2,1)S(1)}, u32[]{:S(2)}, u32[]{:S(2)}) collective-permute-start(bf16[64,512]{1,0:T(8,128)(2,1)S(1)} %get-tuple-element.14), channel_id=1, source_target_pairs={{0,10},{1,7},{2,12},{3,9},{4,14},{5,11},{6,0},{7,13},{8,2},{9,15},... | collective-permute-start | bytes 196616 | tf_op jit(solution)/shard_map/ppermute | solution.py:293
  20.9 7.7 %collective-permute-start.3 = (bf16[64,512]{1,0:T(8,128)(2,1)S(1)}, bf16[64,512]{1,0:T(8,128)(2,1)S(1)}, u32[]{:S(2)}, u32[]{:S(2)}) collective-permute-start(bf16[64,512]{1,0:T(8,128)(2,1)S(1)} %get-tuple-element.13), channel_id=1, source_target_pairs={{0,6},{1,11},{2,8},{3,13},{4,10},{5,15},{6,12},{7,1},{8,14},{9,3},... | collective-permute-start | bytes 196616 | tf_op jit(solution)/shard_map/ppermute | solution.py:293
  28.6 5.1 %collective-permute-start.7 = (bf16[64,512]{1,0:T(8,128)(2,1)S(1)}, bf16[64,512]{1,0:T(8,128)(2,1)S(1)}, u32[]{:S(2)}, u32[]{:S(2)}) collective-permute-start(bf16[64,512]{1,0:T(8,128)(2,1)S(1)} %fusion.7), channel_id=1, source_target_pairs={{0,16},{16,32},{32,48},{48,0},{1,17},{17,33},{33,49},{49,1},{2,18}... | collective-permute-start | bytes 196616 | tf_op jit(solution)/shard_map/ppermute | solution.py:358
  30.0 5.0 %collective-permute-start.6 = (bf16[64,512]{1,0:T(8,128)(2,1)S(1)}, bf16[64,512]{1,0:T(8,128)(2,1)S(1)}, u32[]{:S(2)}, u32[]{:S(2)}) collective-permute-start(bf16[64,512]{1,0:T(8,128)(2,1)S(1)} %fusion.7), channel_id=1, source_target_pairs={{0,32},{16,48},{32,0},{48,16},{1,33},{17,49},{33,1},{49,17},{2,34}... | collective-permute-start | bytes 196616 | tf_op jit(solution)/shard_map/ppermute | solution.py:358
  32.6 3.1 %collective-permute-start.5 = (bf16[64,512]{1,0:T(8,128)(2,1)S(1)}, bf16[64,512]{1,0:T(8,128)(2,1)S(1)}, u32[]{:S(2)}, u32[]{:S(2)}) collective-permute-start(bf16[64,512]{1,0:T(8,128)(2,1)S(1)} %fusion.7), channel_id=1, source_target_pairs={{0,48},{16,0},{32,16},{48,32},{1,49},{17,1},{33,17},{49,33},{2,50}... | collective-permute-start | bytes 196616 | tf_op jit(solution)/shard_map/ppermute | solution.py:358
  35.8 7.2 %collective-permute-start.8 = (bf16[1,64,512]{2,1,0:T(8,128)(2,1)S(1)}, bf16[1,64,512]{2,1,0:T(8,128)(2,1)S(1)}, u32[]{:S(2)}, u32[]{:S(2)}) collective-permute-start(bf16[1,64,512]{2,1,0:T(8,128)(2,1)S(1)} %fusion.8.refs_1_), channel_id=1, source_target_pairs={{0,4},{1,13},{2,6},{3,15},{4,8},{5,1},{6,10},{7,3},{8,12},{9,5},{1... | collective-permute-start | bytes 196616 | tf_op jit(solution)/shard_map/ppermute | solution.py:293
  38.1 5.2 %collective-permute-start.9 = (bf16[1,64,512]{2,1,0:T(8,128)(2,1)S(1)}, bf16[1,64,512]{2,1,0:T(8,128)(2,1)S(1)}, u32[]{:S(2)}, u32[]{:S(2)}) collective-permute-start(bf16[1,64,512]{2,1,0:T(8,128)(2,1)S(1)} %fusion.8.refs_1_), channel_id=1, source_target_pairs={{0,12},{1,5},{2,14},{3,7},{4,0},{5,9},{6,2},{7,11},{8,4},{9,13},{1... | collective-permute-start | bytes 196616 | tf_op jit(solution)/shard_map/ppermute | solution.py:293
  39.0 8.6 %collective-permute-start.10 = (bf16[1,64,512]{2,1,0:T(8,128)(2,1)S(1)}, bf16[1,64,512]{2,1,0:T(8,128)(2,1)S(1)}, u32[]{:S(2)}, u32[]{:S(2)}) collective-permute-start(bf16[1,64,512]{2,1,0:T(8,128)(2,1)S(1)} %fusion.8.refs_1_), channel_id=1, source_target_pairs={{0,8},{1,9},{2,10},{3,11},{4,12},{5,13},{6,14},{7,15},{8,0},{9,1},... | collective-permute-start | bytes 196616 | tf_op jit(solution)/shard_map/ppermute | solution.py:293
  43.3 10.4 %collective-permute-start.11 = (bf16[2,64,512]{2,1,0:T(8,128)(2,1)S(1)}, bf16[2,64,512]{2,1,0:T(8,128)(2,1)S(1)}, u32[]{:S(2)}, u32[]{:S(2)}) collective-permute-start(bf16[2,64,512]{2,1,0:T(8,128)(2,1)S(1)} %get-tuple-element.16), channel_id=1, source_target_pairs={{0,2},{1,15},{2,4},{3,1},{4,6},{5,3},{6,8},{7,5},{8,10},{9,7},{10,... | collective-permute-start | bytes 393224 | tf_op jit(solution)/shard_map/ppermute | solution.py:293
  47.7 8.6 %collective-permute-start.12 = (bf16[2,64,512]{2,1,0:T(8,128)(2,1)S(1)}, bf16[2,64,512]{2,1,0:T(8,128)(2,1)S(1)}, u32[]{:S(2)}, u32[]{:S(2)}) collective-permute-start(bf16[2,64,512]{2,1,0:T(8,128)(2,1)S(1)} %get-tuple-element.15), channel_id=1, source_target_pairs={{0,14},{1,3},{2,0},{3,5},{4,2},{5,7},{6,4},{7,9},{8,6},{9,11},{10,... | collective-permute-start | bytes 393224 | tf_op jit(solution)/shard_map/ppermute | solution.py:293
  47.7 9.9 %collective-permute-start.13 = (bf16[4,64,512]{2,1,0:T(8,128)(2,1)S(1)}, bf16[4,64,512]{2,1,0:T(8,128)(2,1)S(1)}, u32[]{:S(2)}, u32[]{:S(2)}) collective-permute-start(bf16[4,64,512]{2,1,0:T(8,128)(2,1)S(1)} %pad_maximum_fusion), channel_id=1, source_target_pairs={{0,1},{1,0},{2,3},{3,2},{4,5},{5,4},{6,7},{7,6},{8,9},{9,8},{10,11... | collective-permute-start | bytes 786440 | tf_op jit(solution)/shard_map/ppermute | solution.py:374
  53.7 3.5 %collective-permute-start.14 = (bf16[2,64,512]{2,1,0:T(8,128)(2,1)S(1)}, bf16[2,64,512]{2,1,0:T(8,128)(2,1)S(1)}, u32[]{:S(2)}, u32[]{:S(2)}) collective-permute-start(bf16[2,64,512]{2,1,0:T(8,128)(2,1)S(1)} %collective-permute-done.11.refs_4_), channel_id=1, source_target_pairs={{0,1},{1,0},{2,3},{3,2},{4,5},{5,4},{6,7},{7,6},{8,9},{9,8},{10,11... | collective-permute-start | bytes 393224 | tf_op jit(solution)/shard_map/ppermute | solution.py:374
  56.3 1.3 %collective-permute-start.15 = (bf16[2,64,512]{2,1,0:T(8,128)(2,1)S(1)}, bf16[2,64,512]{2,1,0:T(8,128)(2,1)S(1)}, u32[]{:S(2)}, u32[]{:S(2)}) collective-permute-start(bf16[2,64,512]{2,1,0:T(8,128)(2,1)S(1)} %collective-permute-done.12.refs_5_), channel_id=1, source_target_pairs={{0,1},{1,0},{2,3},{3,2},{4,5},{5,4},{6,7},{7,6},{8,9},{9,8},{10,11... | collective-permute-start | bytes 393224 | tf_op jit(solution)/shard_map/ppermute | solution.py:374

commit v6 on v5

--- a/solution.py
+++ b/solution.py
@@ -8,8 +8,8 @@
 from jax.sharding import PartitionSpec as P
 
 KIB = 1024
-OFFSETS = (-2, 1, 4, -1, 2, -3, 0, 3)
-TO_UP, TO_DOWN, STAY = slice(0, 3), slice(3, 5), slice(5, 8)
+OFFSETS = (1, 3, -1, -3, 4, 2, 0, -2)
+TO_UP, TO_DOWN, ACROSS, STAY = slice(0, 2), slice(2, 4), slice(4, 5), slice(5, 8)
 GROUP = 4
 
 
@@ -345,12 +345,16 @@
 
     got = lax.ppermute(send, "core", SWAP)
     paired = lambda part: keep[part] + widen(got[part])
-    up = shift(narrow(paired(TO_UP)), 1)
-    down = shift(narrow(paired(TO_DOWN)), -1)
-    stay = paired(STAY)
-    above = shift(narrow(stay[2] + widen(up[2]) + widen(down[1])), 3)
-    below = shift(narrow(stay[0] + widen(up[0])), -3)
-    update = narrow(stay[1] + widen(up[1]) + widen(down[0]) + widen(above) + widen(below))
+    up, down, across, stay = lax.optimization_barrier(
+        (narrow(paired(TO_UP)), narrow(paired(TO_DOWN)), narrow(paired(ACROSS)), paired(STAY))
+    )
+    up = shift(up, 1)
+    down = shift(down, -1)
+    across = shift(across, 4)
+    above = shift(narrow(stay[0] + widen(up[1])), 2)
+    below = shift(narrow(stay[2] + widen(down[1])), -2)
+    update = stay[1] + widen(up[0]) + widen(down[0]) + widen(across[0])
+    update = narrow(update + widen(above) + widen(below))
     section = lax.axis_index("section")
     updates = [
         jnp.where(

time: 58.8 us -> 57.6 us (0.980)
  starting transfers between devices: 37.4 us -> 30.2 us
  waiting for transfers between devices: 13.1 us -> 19.1 us
    ppermute x9 -> x10, starting transfers between devices: 20.1 us -> 16.2 us  [shift(): return lax.ppermute(array, ('z', 'core'), pairs)]
    ppermute x9 -> x10, waiting for transfers between devices: 8.55 us -> 11.9 us  [shift(): return lax.ppermute(array, ('z', 'core'), pairs)]
    ppermute x3, waiting for transfers between devices: 2.05 us -> 4.74 us  [per_device(): lax.ppermute(update, 'section', [(i, (i + by) % sections) for i in range(...]
    ppermute x3, starting transfers between devices: 8.87 us -> 6.83 us  [per_device(): lax.ppermute(piece, 'core', SWAP)]
    ppermute x3, starting transfers between devices: 5.06 us -> 3.85 us  [per_device(): lax.ppermute(update, 'section', [(i, (i + by) % sections) for i in range(...]
  transfers between devices with their start and end apart: 16 -> 17, of which waited for: 9 -> 10; matrix products, arithmetic and copies ran while one was open for 0% -> 0% of each run, Pallas kernels for 0% -> 0%
where the time goes in v6:
time: 57.6 us
  starting transfers between devices  30.2 us (52%)
  waiting for transfers between devices  19.1 us (33%)
  Pallas kernels  7.81 us (14%)
    ppermute x10, starting transfers between devices, shift(): return lax.ppermute(array, ('z', 'core'), pairs)  16.2 us
    ppermute x10, waiting for transfers between devices, shift(): return lax.ppermute(array, ('z', 'core'), pairs)  11.9 us
    ppermute x3, starting transfers between devices, per_device(): lax.ppermute(piece, 'core', SWAP)  6.83 us
    pallas_call x1, Pallas kernels, per_device(): pl.pallas_call(attend, out_shape=(jax.ShapeDtypeStruct((chips, flat, shar...  6.73 us
    ppermute x3, waiting for transfers between devices, per_device(): lax.ppermute(update, 'section', [(i, (i + by) % sections) for i in range(...  4.74 us
    ppermute x3, starting transfers between devices, per_device(): lax.ppermute(update, 'section', [(i, (i + by) % sections) for i in range(...  3.85 us
    ppermute x1, starting transfers between devices, per_device(): got = lax.ppermute(send, 'core', SWAP)  3.33 us
    ppermute x1, waiting for transfers between devices, per_device(): got = lax.ppermute(send, 'core', SWAP)  1.54 us
  transfers between devices with their start and end apart: 17, of which 10 were waited for; matrix products, arithmetic and copies ran while one was open for 0% of the time, Pallas kernels for 0%

profile of v6, /device:TPU:1, one launch (start us, length us, event | category | flops | bytes accessed | tf_op | source)
XLA Modules:
  0.0 57.6 jit_solution(4754676104280167564)
XLA Ops:
  0.0 6.7 %attend.1 = (bf16[8,64,512]{2,1,0:T(8,128)(2,1)S(1)}, f32[8,64,512]{2,1,0:T(8,128)S(1)}, bf16[64,512]{1,0:T(8,128)(2,1)S(1)}) custom-call(s32[1]{0:T(128)} %bitcast.core_ref, s32[1]{0:T(128)} %bitcast.1.chip_ref, s32[32]{0:T(128)} %length_hbm.1, s32[32]{0:T(128)} %position_hbm.1, f32[1,128]{1,0:T(1,128)} %constant.25.clone.rate_hbm, ...), custom_call_target="tpu_custom_call" | custom-call | tf_op jit(solution)/shard_map/attend/pallas_call | solution.py:295
  6.7 3.3 %collective-permute-start = (bf16[8,64,512]{2,1,0:T(8,128)(2,1)S(1)}, bf16[8,64,512]{2,1,0:T(8,128)(2,1)S(1)}, u32[]{:S(2)}, u32[]{:S(2)}) collective-permute-start(bf16[8,64,512]{2,1,0:T(8,128)(2,1)S(1)} %get-tuple-element.14), channel_id=1, source_target_pairs={{0,1},{1,0},{2,3},{3,2},{4,5},{5,4},{6,7},{7,6},{8,9},{9,8},{10,11... | collective-permute-start | bytes 1572872 | tf_op jit(solution)/shard_map/ppermute | solution.py:346
  10.1 1.5 %collective-permute-done = bf16[8,64,512]{2,1,0:T(8,128)(2,1)S(1)} collective-permute-done((bf16[8,64,512]{2,1,0:T(8,128)(2,1)S(1)}, bf16[8,64,512]{2,1,0:T(8,128)(2,1)S(1)}, u32[]{:S(2)}, u32[]{:S(2)}) %collective-permute-start) | collective-permute-done | bytes 524320 | tf_op jit(solution)/shard_map/ppermute | solution.py:346
  11.8 3.9 %collective-permute-start.1 = (bf16[2,64,512]{2,1,0:T(8,128)(2,1)S(1)}, bf16[2,64,512]{2,1,0:T(8,128)(2,1)S(1)}, u32[]{:S(2)}, u32[]{:S(2)}) collective-permute-start(bf16[2,64,512]{2,1,0:T(8,128)(2,1)S(1)} %get-tuple-element.16), channel_id=1, source_target_pairs={{0,2},{1,15},{2,4},{3,1},{4,6},{5,3},{6,8},{7,5},{8,10},{9,7},{10,... | collective-permute-start | bytes 393224 | tf_op jit(solution)/shard_map/ppermute | solution.py:293
  15.7 2.8 %collective-permute-start.3 = (bf16[1,64,512]{2,1,0:T(8,128)(2,1)S(1)}, bf16[1,64,512]{2,1,0:T(8,128)(2,1)S(1)}, u32[]{:S(2)}, u32[]{:S(2)}) collective-permute-start(bf16[1,64,512]{2,1,0:T(8,128)(2,1)S(1)} %add_convert_fusion.8), channel_id=1, source_target_pairs={{0,8},{1,9},{2,10},{3,11},{4,12},{5,13},{6,14},{7,15},{8,0},{9,1},... | collective-permute-start | bytes 196616 | tf_op jit(solution)/shard_map/ppermute | solution.py:293
  18.5 2.2 %collective-permute-done.2 = bf16[2,64,512]{2,1,0:T(8,128)(2,1)S(1)} collective-permute-done((bf16[2,64,512]{2,1,0:T(8,128)(2,1)S(1)}, bf16[2,64,512]{2,1,0:T(8,128)(2,1)S(1)}, u32[]{:S(2)}, u32[]{:S(2)}) %collective-permute-start.2) | collective-permute-done | bytes 131104 | tf_op jit(solution)/shard_map/ppermute | solution.py:293
  20.7 1.6 %collective-permute-start.4 = (bf16[64,512]{1,0:T(8,128)(2,1)S(1)}, bf16[64,512]{1,0:T(8,128)(2,1)S(1)}, u32[]{:S(2)}, u32[]{:S(2)}) collective-permute-start(bf16[64,512]{1,0:T(8,128)(2,1)S(1)} %get-tuple-element.21), channel_id=1, source_target_pairs={{0,4},{1,13},{2,6},{3,15},{4,8},{5,1},{6,10},{7,3},{8,12},{9,5},{1... | collective-permute-start | bytes 196616 | tf_op jit(solution)/shard_map/ppermute | solution.py:293
  22.4 0.8 %collective-permute-start.5 = (bf16[64,512]{1,0:T(8,128)(2,1)S(1)}, bf16[64,512]{1,0:T(8,128)(2,1)S(1)}, u32[]{:S(2)}, u32[]{:S(2)}) collective-permute-start(bf16[64,512]{1,0:T(8,128)(2,1)S(1)} %get-tuple-element.22), channel_id=1, source_target_pairs={{0,12},{1,5},{2,14},{3,7},{4,0},{5,9},{6,2},{7,11},{8,4},{9,13},{1... | collective-permute-start | bytes 196616 | tf_op jit(solution)/shard_map/ppermute | solution.py:293
  23.2 2.6 %collective-permute-done.4 = bf16[64,512]{1,0:T(8,128)(2,1)S(1)} collective-permute-done((bf16[64,512]{1,0:T(8,128)(2,1)S(1)}, bf16[64,512]{1,0:T(8,128)(2,1)S(1)}, u32[]{:S(2)}, u32[]{:S(2)}) %collective-permute-start.4) | collective-permute-done | bytes 65568 | tf_op jit(solution)/shard_map/ppermute | solution.py:293
  25.8 2.2 %collective-permute-done.5 = bf16[64,512]{1,0:T(8,128)(2,1)S(1)} collective-permute-done((bf16[64,512]{1,0:T(8,128)(2,1)S(1)}, bf16[64,512]{1,0:T(8,128)(2,1)S(1)}, u32[]{:S(2)}, u32[]{:S(2)}) %collective-permute-start.5) | collective-permute-done | bytes 65568 | tf_op jit(solution)/shard_map/ppermute | solution.py:293
  28.1 2.8 %collective-permute-start.6 = (bf16[64,512]{1,0:T(8,128)(2,1)S(1)}, bf16[64,512]{1,0:T(8,128)(2,1)S(1)}, u32[]{:S(2)}, u32[]{:S(2)}) collective-permute-start(bf16[64,512]{1,0:T(8,128)(2,1)S(1)} %fusion.1), channel_id=1, source_target_pairs={{0,48},{16,0},{32,16},{48,32},{1,49},{17,1},{33,17},{49,33},{2,50}... | collective-permute-start | bytes 196616 | tf_op jit(solution)/shard_map/ppermute | solution.py:362
  31.2 0.7 %collective-permute-start.8 = (bf16[64,512]{1,0:T(8,128)(2,1)S(1)}, bf16[64,512]{1,0:T(8,128)(2,1)S(1)}, u32[]{:S(2)}, u32[]{:S(2)}) collective-permute-start(bf16[64,512]{1,0:T(8,128)(2,1)S(1)} %fusion.1), channel_id=1, source_target_pairs={{0,16},{16,32},{32,48},{48,0},{1,17},{17,33},{33,49},{49,1},{2,18}... | collective-permute-start | bytes 196616 | tf_op jit(solution)/shard_map/ppermute | solution.py:362
  32.2 3.4 %collective-permute-done.7 = bf16[64,512]{1,0:T(8,128)(2,1)S(1)} collective-permute-done((bf16[64,512]{1,0:T(8,128)(2,1)S(1)}, bf16[64,512]{1,0:T(8,128)(2,1)S(1)}, u32[]{:S(2)}, u32[]{:S(2)}) %collective-permute-start.7) | collective-permute-done | bytes 65568 | tf_op jit(solution)/shard_map/ppermute | solution.py:362
  35.6 1.1 %collective-permute-done.8 = bf16[64,512]{1,0:T(8,128)(2,1)S(1)} collective-permute-done((bf16[64,512]{1,0:T(8,128)(2,1)S(1)}, bf16[64,512]{1,0:T(8,128)(2,1)S(1)}, u32[]{:S(2)}, u32[]{:S(2)}) %collective-permute-start.8) | collective-permute-done | bytes 65568 | tf_op jit(solution)/shard_map/ppermute | solution.py:362
  36.8 3.6 %collective-permute-start.9 = (bf16[1,64,512]{2,1,0:T(8,128)(2,1)S(1)}, bf16[1,64,512]{2,1,0:T(8,128)(2,1)S(1)}, u32[]{:S(2)}, u32[]{:S(2)}) collective-permute-start(bf16[1,64,512]{2,1,0:T(8,128)(2,1)S(1)} %fusion.4.refs_1_), channel_id=1, source_target_pairs={{0,4},{1,13},{2,6},{3,15},{4,8},{5,1},{6,10},{7,3},{8,12},{9,5},{1... | collective-permute-start | bytes 196616 | tf_op jit(solution)/shard_map/ppermute | solution.py:293
  40.4 0.5 collective-permute-start.11
  40.9 1.8 %collective-permute-done.10.refs_2_ = bf16[1,64,512]{2,1,0:T(8,128)(2,1)S(1)} collective-permute-done((bf16[1,64,512]{2,1,0:T(8,128)(2,1)S(1)}, bf16[1,64,512]{2,1,0:T(8,128)(2,1)S(1)}, u32[]{:S(2)}, u32[]{:S(2)}) %collective-permute-start.10) | collective-permute-done | bytes 65568 | tf_op jit(solution)/shard_map/ppermute | solution.py:293
  42.7 2.9 %collective-permute-start.12 = (bf16[2,64,512]{2,1,0:T(8,128)(2,1)S(1)}, bf16[2,64,512]{2,1,0:T(8,128)(2,1)S(1)}, u32[]{:S(2)}, u32[]{:S(2)}) collective-permute-start(bf16[2,64,512]{2,1,0:T(8,128)(2,1)S(1)} %get-tuple-element.24), channel_id=1, source_target_pairs={{0,2},{1,15},{2,4},{3,1},{4,6},{5,3},{6,8},{7,5},{8,10},{9,7},{10,... | collective-permute-start | bytes 393224 | tf_op jit(solution)/shard_map/ppermute | solution.py:293
  45.6 3.0 %collective-permute-done.11.refs_3_ = bf16[1,64,512]{2,1,0:T(8,128)(2,1)S(1)} collective-permute-done((bf16[1,64,512]{2,1,0:T(8,128)(2,1)S(1)}, bf16[1,64,512]{2,1,0:T(8,128)(2,1)S(1)}, u32[]{:S(2)}, u32[]{:S(2)}) %collective-permute-start.11) | collective-permute-done | bytes 65568 | tf_op jit(solution)/shard_map/ppermute | solution.py:293
  48.7 3.4 %collective-permute-start.14 = (bf16[4,64,512]{2,1,0:T(8,128)(2,1)S(1)}, bf16[4,64,512]{2,1,0:T(8,128)(2,1)S(1)}, u32[]{:S(2)}, u32[]{:S(2)}) collective-permute-start(bf16[4,64,512]{2,1,0:T(8,128)(2,1)S(1)} %pad_maximum_fusion), channel_id=1, source_target_pairs={{0,1},{1,0},{2,3},{3,2},{4,5},{5,4},{6,7},{7,6},{8,9},{9,8},{10,11... | collective-permute-start | bytes 786440 | tf_op jit(solution)/shard_map/ppermute | solution.py:378
  52.0 2.5 %collective-permute-start.15 = (bf16[2,64,512]{2,1,0:T(8,128)(2,1)S(1)}, bf16[2,64,512]{2,1,0:T(8,128)(2,1)S(1)}, u32[]{:S(2)}, u32[]{:S(2)}) collective-permute-start(bf16[2,64,512]{2,1,0:T(8,128)(2,1)S(1)} %collective-permute-done.12.refs_4_), channel_id=1, source_target_pairs={{0,1},{1,0},{2,3},{3,2},{4,5},{5,4},{6,7},{7,6},{8,9},{9,8},{10,11... | collective-permute-start | bytes 393224 | tf_op jit(solution)/shard_map/ppermute | solution.py:378
  54.6 0.9 %collective-permute-start.16 = (bf16[2,64,512]{2,1,0:T(8,128)(2,1)S(1)}, bf16[2,64,512]{2,1,0:T(8,128)(2,1)S(1)}, u32[]{:S(2)}, u32[]{:S(2)}) collective-permute-start(bf16[2,64,512]{2,1,0:T(8,128)(2,1)S(1)} %collective-permute-done.13.refs_5_), channel_id=1, source_target_pairs={{0,1},{1,0},{2,3},{3,2},{4,5},{5,4},{6,7},{7,6},{8,9},{9,8},{10,11... | collective-permute-start | bytes 393224 | tf_op jit(solution)/shard_map/ppermute | solution.py:378
  55.5 0.9 %collective-permute-done.16.refs_8_ = bf16[2,64,512]{2,1,0:T(8,128)(2,1)S(1)} collective-permute-done((bf16[2,64,512]{2,1,0:T(8,128)(2,1)S(1)}, bf16[2,64,512]{2,1,0:T(8,128)(2,1)S(1)}, u32[]{:S(2)}, u32[]{:S(2)}) %collective-permute-start.16) | collective-permute-done | bytes 131104 | tf_op jit(solution)/shard_map/ppermute | solution.py:378
  56.5 1.1 %assemble.1 = bf16[64,8192]{1,0:T(8,128)(2,1)} custom-call(s32[1]{0:T(128)} %bitcast.core_ref, s32[1]{0:T(128)} %bitcast.1.chip_ref, bf16[1,64,512]{2,1,0:T(8,128)(2,1)S(1)} %collective-permute-done.9.refs_0_, bf16[1,64,512]{2,1,0:T(8,128)(2,1)S(1)} %fusion.4.refs_1_, bf16[1,64,512]{2,1,0:T(8,128)(2,1)S(1)} %collective-permute-done.10.refs_2_, ...), custom_call_target="tpu_custom_call" | custom-call | tf_op jit(solution)/shard_map/assemble/pallas_call | solution.py:381
  (20 shorter events, 1.1 us)
Async XLA Ops:
  6.7 4.9 %collective-permute-start = (bf16[8,64,512]{2,1,0:T(8,128)(2,1)S(1)}, bf16[8,64,512]{2,1,0:T(8,128)(2,1)S(1)}, u32[]{:S(2)}, u32[]{:S(2)}) collective-permute-start(bf16[8,64,512]{2,1,0:T(8,128)(2,1)S(1)} %get-tuple-element.14), channel_id=1, source_target_pairs={{0,1},{1,0},{2,3},{3,2},{4,5},{5,4},{6,7},{7,6},{8,9},{9,8},{10,11... | collective-permute-start | bytes 1572872 | tf_op jit(solution)/shard_map/ppermute | solution.py:346
  11.8 6.7 %collective-permute-start.1 = (bf16[2,64,512]{2,1,0:T(8,128)(2,1)S(1)}, bf16[2,64,512]{2,1,0:T(8,128)(2,1)S(1)}, u32[]{:S(2)}, u32[]{:S(2)}) collective-permute-start(bf16[2,64,512]{2,1,0:T(8,128)(2,1)S(1)} %get-tuple-element.16), channel_id=1, source_target_pairs={{0,2},{1,15},{2,4},{3,1},{4,6},{5,3},{6,8},{7,5},{8,10},{9,7},{10,... | collective-permute-start | bytes 393224 | tf_op jit(solution)/shard_map/ppermute | solution.py:293
  15.7 5.0 %collective-permute-start.2 = (bf16[2,64,512]{2,1,0:T(8,128)(2,1)S(1)}, bf16[2,64,512]{2,1,0:T(8,128)(2,1)S(1)}, u32[]{:S(2)}, u32[]{:S(2)}) collective-permute-start(bf16[2,64,512]{2,1,0:T(8,128)(2,1)S(1)} %get-tuple-element.17), channel_id=1, source_target_pairs={{0,14},{1,3},{2,0},{3,5},{4,2},{5,7},{6,4},{7,9},{8,6},{9,11},{10,... | collective-permute-start | bytes 393224 | tf_op jit(solution)/shard_map/ppermute | solution.py:293
  15.7 7.5 %collective-permute-start.3 = (bf16[1,64,512]{2,1,0:T(8,128)(2,1)S(1)}, bf16[1,64,512]{2,1,0:T(8,128)(2,1)S(1)}, u32[]{:S(2)}, u32[]{:S(2)}) collective-permute-start(bf16[1,64,512]{2,1,0:T(8,128)(2,1)S(1)} %add_convert_fusion.8), channel_id=1, source_target_pairs={{0,8},{1,9},{2,10},{3,11},{4,12},{5,13},{6,14},{7,15},{8,0},{9,1},... | collective-permute-start | bytes 196616 | tf_op jit(solution)/shard_map/ppermute | solution.py:293
  20.7 5.1 %collective-permute-start.4 = (bf16[64,512]{1,0:T(8,128)(2,1)S(1)}, bf16[64,512]{1,0:T(8,128)(2,1)S(1)}, u32[]{:S(2)}, u32[]{:S(2)}) collective-permute-start(bf16[64,512]{1,0:T(8,128)(2,1)S(1)} %get-tuple-element.21), channel_id=1, source_target_pairs={{0,4},{1,13},{2,6},{3,15},{4,8},{5,1},{6,10},{7,3},{8,12},{9,5},{1... | collective-permute-start | bytes 196616 | tf_op jit(solution)/shard_map/ppermute | solution.py:293
  22.4 5.7 %collective-permute-start.5 = (bf16[64,512]{1,0:T(8,128)(2,1)S(1)}, bf16[64,512]{1,0:T(8,128)(2,1)S(1)}, u32[]{:S(2)}, u32[]{:S(2)}) collective-permute-start(bf16[64,512]{1,0:T(8,128)(2,1)S(1)} %get-tuple-element.22), channel_id=1, source_target_pairs={{0,12},{1,5},{2,14},{3,7},{4,0},{5,9},{6,2},{7,11},{8,4},{9,13},{1... | collective-permute-start | bytes 196616 | tf_op jit(solution)/shard_map/ppermute | solution.py:293
  28.1 4.1 %collective-permute-start.6 = (bf16[64,512]{1,0:T(8,128)(2,1)S(1)}, bf16[64,512]{1,0:T(8,128)(2,1)S(1)}, u32[]{:S(2)}, u32[]{:S(2)}) collective-permute-start(bf16[64,512]{1,0:T(8,128)(2,1)S(1)} %fusion.1), channel_id=1, source_target_pairs={{0,48},{16,0},{32,16},{48,32},{1,49},{17,1},{33,17},{49,33},{2,50}... | collective-permute-start | bytes 196616 | tf_op jit(solution)/shard_map/ppermute | solution.py:362
  30.9 4.7 %collective-permute-start.7 = (bf16[64,512]{1,0:T(8,128)(2,1)S(1)}, bf16[64,512]{1,0:T(8,128)(2,1)S(1)}, u32[]{:S(2)}, u32[]{:S(2)}) collective-permute-start(bf16[64,512]{1,0:T(8,128)(2,1)S(1)} %fusion.1), channel_id=1, source_target_pairs={{0,32},{16,48},{32,0},{48,16},{1,33},{17,49},{33,1},{49,17},{2,34}... | collective-permute-start | bytes 196616 | tf_op jit(solution)/shard_map/ppermute | solution.py:362
  31.2 5.4 %collective-permute-start.8 = (bf16[64,512]{1,0:T(8,128)(2,1)S(1)}, bf16[64,512]{1,0:T(8,128)(2,1)S(1)}, u32[]{:S(2)}, u32[]{:S(2)}) collective-permute-start(bf16[64,512]{1,0:T(8,128)(2,1)S(1)} %fusion.1), channel_id=1, source_target_pairs={{0,16},{16,32},{32,48},{48,0},{1,17},{17,33},{33,49},{49,1},{2,18}... | collective-permute-start | bytes 196616 | tf_op jit(solution)/shard_map/ppermute | solution.py:362
  36.7 5.9 %collective-permute-start.10 = (bf16[1,64,512]{2,1,0:T(8,128)(2,1)S(1)}, bf16[1,64,512]{2,1,0:T(8,128)(2,1)S(1)}, u32[]{:S(2)}, u32[]{:S(2)}) collective-permute-start(bf16[1,64,512]{2,1,0:T(8,128)(2,1)S(1)} %fusion.4.refs_1_), channel_id=1, source_target_pairs={{0,12},{1,5},{2,14},{3,7},{4,0},{5,9},{6,2},{7,11},{8,4},{9,13},{1... | collective-permute-start | bytes 196616 | tf_op jit(solution)/shard_map/ppermute | solution.py:293
  36.8 5.8 %collective-permute-start.9 = (bf16[1,64,512]{2,1,0:T(8,128)(2,1)S(1)}, bf16[1,64,512]{2,1,0:T(8,128)(2,1)S(1)}, u32[]{:S(2)}, u32[]{:S(2)}) collective-permute-start(bf16[1,64,512]{2,1,0:T(8,128)(2,1)S(1)} %fusion.4.refs_1_), channel_id=1, source_target_pairs={{0,4},{1,13},{2,6},{3,15},{4,8},{5,1},{6,10},{7,3},{8,12},{9,5},{1... | collective-permute-start | bytes 196616 | tf_op jit(solution)/shard_map/ppermute | solution.py:293
  40.4 8.2 %collective-permute-start.11 = (bf16[1,64,512]{2,1,0:T(8,128)(2,1)S(1)}, bf16[1,64,512]{2,1,0:T(8,128)(2,1)S(1)}, u32[]{:S(2)}, u32[]{:S(2)}) collective-permute-start(bf16[1,64,512]{2,1,0:T(8,128)(2,1)S(1)} %fusion.4.refs_1_), channel_id=1, source_target_pairs={{0,8},{1,9},{2,10},{3,11},{4,12},{5,13},{6,14},{7,15},{8,0},{9,1},... | collective-permute-start | bytes 196616 | tf_op jit(solution)/shard_map/ppermute | solution.py:293
  42.7 9.3 %collective-permute-start.12 = (bf16[2,64,512]{2,1,0:T(8,128)(2,1)S(1)}, bf16[2,64,512]{2,1,0:T(8,128)(2,1)S(1)}, u32[]{:S(2)}, u32[]{:S(2)}) collective-permute-start(bf16[2,64,512]{2,1,0:T(8,128)(2,1)S(1)} %get-tuple-element.24), channel_id=1, source_target_pairs={{0,2},{1,15},{2,4},{3,1},{4,6},{5,3},{6,8},{7,5},{8,10},{9,7},{10,... | collective-permute-start | bytes 393224 | tf_op jit(solution)/shard_map/ppermute | solution.py:293
  45.6 9.0 %collective-permute-start.13 = (bf16[2,64,512]{2,1,0:T(8,128)(2,1)S(1)}, bf16[2,64,512]{2,1,0:T(8,128)(2,1)S(1)}, u32[]{:S(2)}, u32[]{:S(2)}) collective-permute-start(bf16[2,64,512]{2,1,0:T(8,128)(2,1)S(1)} %get-tuple-element.23), channel_id=1, source_target_pairs={{0,14},{1,3},{2,0},{3,5},{4,2},{5,7},{6,4},{7,9},{8,6},{9,11},{10,... | collective-permute-start | bytes 393224 | tf_op jit(solution)/shard_map/ppermute | solution.py:293
  48.7 7.8 %collective-permute-start.14 = (bf16[4,64,512]{2,1,0:T(8,128)(2,1)S(1)}, bf16[4,64,512]{2,1,0:T(8,128)(2,1)S(1)}, u32[]{:S(2)}, u32[]{:S(2)}) collective-permute-start(bf16[4,64,512]{2,1,0:T(8,128)(2,1)S(1)} %pad_maximum_fusion), channel_id=1, source_target_pairs={{0,1},{1,0},{2,3},{3,2},{4,5},{5,4},{6,7},{7,6},{8,9},{9,8},{10,11... | collective-permute-start | bytes 786440 | tf_op jit(solution)/shard_map/ppermute | solution.py:378
  52.0 3.5 %collective-permute-start.15 = (bf16[2,64,512]{2,1,0:T(8,128)(2,1)S(1)}, bf16[2,64,512]{2,1,0:T(8,128)(2,1)S(1)}, u32[]{:S(2)}, u32[]{:S(2)}) collective-permute-start(bf16[2,64,512]{2,1,0:T(8,128)(2,1)S(1)} %collective-permute-done.12.refs_4_), channel_id=1, source_target_pairs={{0,1},{1,0},{2,3},{3,2},{4,5},{5,4},{6,7},{7,6},{8,9},{9,8},{10,11... | collective-permute-start | bytes 393224 | tf_op jit(solution)/shard_map/ppermute | solution.py:378
  54.6 1.9 %collective-permute-start.16 = (bf16[2,64,512]{2,1,0:T(8,128)(2,1)S(1)}, bf16[2,64,512]{2,1,0:T(8,128)(2,1)S(1)}, u32[]{:S(2)}, u32[]{:S(2)}) collective-permute-start(bf16[2,64,512]{2,1,0:T(8,128)(2,1)S(1)} %collective-permute-done.13.refs_5_), channel_id=1, source_target_pairs={{0,1},{1,0},{2,3},{3,2},{4,5},{5,4},{6,7},{7,6},{8,9},{9,8},{10,11... | collective-permute-start | bytes 393224 | tf_op jit(solution)/shard_map/ppermute | solution.py:378

commit v7 on v6

--- a/solution.py
+++ b/solution.py
@@ -10,6 +10,7 @@
 KIB = 1024
 OFFSETS = (1, 3, -1, -3, 4, 2, 0, -2)
 TO_UP, TO_DOWN, ACROSS, STAY = slice(0, 2), slice(2, 4), slice(4, 5), slice(5, 8)
+EARLY = 4
 GROUP = 4
 
 
@@ -26,7 +27,8 @@
     value_hbm,
     weight_hbm,
     hidden_hbm,
-    send_ref,
+    first_ref,
+    second_ref,
     keep_ref,
     near_ref,
     length_ref,
@@ -57,7 +59,8 @@
     depth = weight_ref.shape[1]
     group = depth // head
     per_row = steps * group
-    chips = send_ref.shape[0]
+    chips = keep_ref.shape[0]
+    early = first_ref.shape[0]
     factor = head**-0.5
     core = core_ref[0]
     chip = chip_ref[0]
@@ -203,8 +206,12 @@
             weights[slot].wait()
         for slot in range(first, first + GROUP):
             partial = jnp.dot(left, weight_ref[slot], preferred_element_type=jnp.float32)
-            target = send_ref if slot < chips else keep_ref
-            target[slot % chips] = partial.astype(target.dtype)
+            if slot < early:
+                first_ref[slot] = partial.astype(first_ref.dtype)
+            elif slot < chips:
+                second_ref[slot - early] = partial.astype(second_ref.dtype)
+            else:
+                keep_ref[slot - chips] = partial
     for copy in hidden:
         copy.wait()
 
@@ -216,7 +223,8 @@
     (False, (4,)),
     (False, (-3, -1)),
     (False, (3, 1)),
-    (True, (-2, 0, 2, 4)),
+    (True, (0,)),
+    (True, (-2, 2, 4)),
     (True, (-3, -1)),
     (True, (3, 1)),
 )
@@ -292,15 +300,16 @@
                 pairs.append((i * cores + c, j * cores + c))
         return lax.ppermute(array, ("z", "core"), pairs)
 
-    send, keep, current = pl.pallas_call(
+    first, second, keep, current = pl.pallas_call(
         attend,
         out_shape=(
-            jax.ShapeDtypeStruct((chips, flat, share), jnp.bfloat16),
+            jax.ShapeDtypeStruct((EARLY, flat, share), jnp.bfloat16),
+            jax.ShapeDtypeStruct((chips - EARLY, flat, share), jnp.bfloat16),
             jax.ShapeDtypeStruct((chips, flat, share), jnp.float32),
             jax.ShapeDtypeStruct((flat, share), jnp.bfloat16),
         ),
         in_specs=[SMEM, SMEM] + [HBM] * 10,
-        out_specs=(VMEM, VMEM, VMEM),
+        out_specs=(VMEM, VMEM, VMEM, VMEM),
         scratch_shapes=[
             pltpu.SMEM((rows,), jnp.int32),
             pltpu.SMEM((rows,), jnp.int32),
@@ -343,11 +352,16 @@
         ),
     )
 
-    got = lax.ppermute(send, "core", SWAP)
-    paired = lambda part: keep[part] + widen(got[part])
-    up, down, across, stay = lax.optimization_barrier(
-        (narrow(paired(TO_UP)), narrow(paired(TO_DOWN)), narrow(paired(ACROSS)), paired(STAY))
-    )
+    first = lax.ppermute(first, "core", SWAP)
+    second = lax.ppermute(second, "core", SWAP)
+
+    def paired(part):
+        if part.stop <= EARLY:
+            return keep[part] + widen(first[part])
+        return keep[part] + widen(second[part.start - EARLY : part.stop - EARLY])
+
+    up, down = lax.optimization_barrier((narrow(paired(TO_UP)), narrow(paired(TO_DOWN))))
+    across, stay = lax.optimization_barrier((narrow(paired(ACROSS)), paired(STAY)))
     up = shift(up, 1)
     down = shift(down, -1)
     across = shift(across, 4)
@@ -376,7 +390,7 @@
     pieces = [below, mine, above, across, up, down]
     pieces += [
         lax.ppermute(piece, "core", SWAP)
-        for piece in (jnp.concatenate([below, mine, above, across]), up, down)
+        for piece in (mine, jnp.concatenate([below, above, across]), up, down)
     ]
     states = pl.pallas_call(
         assemble,

time: 57.6 us -> 58.1 us (level)
  starting transfers between devices: 30.2 us -> 31.5 us
  waiting for transfers between devices: 19.1 us -> 18.2 us
    ppermute x3 -> x4, starting transfers between devices: 6.83 us -> 9.01 us  [per_device(): lax.ppermute(piece, 'core', SWAP)]
    ppermute x10, waiting for transfers between devices: 11.9 us -> 10.4 us  [shift(): return lax.ppermute(array, ('z', 'core'), pairs)]
    ppermute x10, starting transfers between devices: 16.2 us -> 15.2 us  [shift(): return lax.ppermute(array, ('z', 'core'), pairs)]
    ppermute x3, waiting for transfers between devices: 4.74 us -> 5.41 us  [per_device(): lax.ppermute(update, 'section', [(i, (i + by) % sections) for i in range(...]
    ppermute x1 -> x2, waiting for transfers between devices: 1.54 us -> 1.06 us  [the longest x1 1.06 us: per_device(): first = lax.ppermute(first, 'core', SWAP)]
    ppermute x3 -> x4, waiting for transfers between devices: 0.99 us -> 1.26 us  [per_device(): lax.ppermute(piece, 'core', SWAP)]
    ppermute x1 -> x2, starting transfers between devices: 3.33 us -> 3.43 us  [the longest x1 3.33 us: per_device(): first = lax.ppermute(first, 'core', SWAP)]
  transfers between devices with their start and end apart: 17 -> 19, of which waited for: 10 -> 11; matrix products, arithmetic and copies ran while one was open for 0% -> 0% of each run, Pallas kernels for 0% -> 0%
where the time goes in v7:
time: 58.1 us; the launch traced here: 58 us
  starting transfers between devices  31.5 us (54%)
  waiting for transfers between devices  18.2 us (31%)
  Pallas kernels  7.83 us (13%)
    ppermute x10, starting transfers between devices, shift(): return lax.ppermute(array, ('z', 'core'), pairs)  15.2 us
    ppermute x10, waiting for transfers between devices, shift(): return lax.ppermute(array, ('z', 'core'), pairs)  10.4 us
    ppermute x4, starting transfers between devices, per_device(): lax.ppermute(piece, 'core', SWAP)  9.01 us
    pallas_call x1, Pallas kernels, per_device(): pl.pallas_call(attend, out_shape=(jax.ShapeDtypeStruct((EARLY, flat, shar...  6.73 us
    ppermute x3, waiting for transfers between devices, per_device(): lax.ppermute(update, 'section', [(i, (i + by) % sections) for i in range(...  5.41 us
    ppermute x3, starting transfers between devices, per_device(): lax.ppermute(update, 'section', [(i, (i + by) % sections) for i in range(...  3.85 us
    ppermute x1, starting transfers between devices, per_device(): first = lax.ppermute(first, 'core', SWAP)  3.33 us
    ppermute x4, waiting for transfers between devices, per_device(): lax.ppermute(piece, 'core', SWAP)  1.26 us
  transfers between devices with their start and end apart: 19, of which 11 were waited for; matrix products, arithmetic and copies ran while one was open for 0% of the time, Pallas kernels for 0%

profile of v7, /device:TPU:1, one launch (start us, length us, event | category | flops | bytes accessed | tf_op | source)
XLA Modules:
  0.0 58.0 jit_solution(5931381111207555508)
XLA Ops:
  0.0 6.7 %attend.1 = (bf16[4,64,512]{2,1,0:T(8,128)(2,1)S(1)}, bf16[4,64,512]{2,1,0:T(8,128)(2,1)S(1)}, f32[8,64,512]{2,1,0:T(8,128)S(1)}, bf16[64,512]{1,0:T(8,128)(2,1)S(1)}) custom-call(s32[1]{0:T(128)} %bitcast.core_ref, s32[1]{0:T(128)} %bitcast.1.chip_ref, s32[32]{0:T(128)} %length_hbm.1, s32[32]{0:T(128)} %position_hbm.1, f32[1,128]{1,0:T(1,128)} %constant.25.clone.rate_hbm, ...), custom_call_target="tpu_custom_call" | custom-call | tf_op jit(solution)/shard_map/attend/pallas_call | solution.py:303
  6.7 3.3 %collective-permute-start.1 = (bf16[4,64,512]{2,1,0:T(8,128)(2,1)S(1)}, bf16[4,64,512]{2,1,0:T(8,128)(2,1)S(1)}, u32[]{:S(2)}, u32[]{:S(2)}) collective-permute-start(bf16[4,64,512]{2,1,0:T(8,128)(2,1)S(1)} %get-tuple-element.17), channel_id=1, source_target_pairs={{0,1},{1,0},{2,3},{3,2},{4,5},{5,4},{6,7},{7,6},{8,9},{9,8},{10,11... | collective-permute-start | bytes 786440 | tf_op jit(solution)/shard_map/ppermute | solution.py:355
  10.2 1.1 %collective-permute-done.1 = bf16[4,64,512]{2,1,0:T(8,128)(2,1)S(1)} collective-permute-done((bf16[4,64,512]{2,1,0:T(8,128)(2,1)S(1)}, bf16[4,64,512]{2,1,0:T(8,128)(2,1)S(1)}, u32[]{:S(2)}, u32[]{:S(2)}) %collective-permute-start.1) | collective-permute-done | bytes 262176 | tf_op jit(solution)/shard_map/ppermute | solution.py:355
  11.3 3.9 %collective-permute-start.2 = (bf16[2,64,512]{2,1,0:T(8,128)(2,1)S(1)}, bf16[2,64,512]{2,1,0:T(8,128)(2,1)S(1)}, u32[]{:S(2)}, u32[]{:S(2)}) collective-permute-start(bf16[2,64,512]{2,1,0:T(8,128)(2,1)S(1)} %get-tuple-element.18), channel_id=1, source_target_pairs={{0,2},{1,15},{2,4},{3,1},{4,6},{5,3},{6,8},{7,5},{8,10},{9,7},{10,... | collective-permute-start | bytes 393224 | tf_op jit(solution)/shard_map/ppermute | solution.py:301
  15.3 2.9 %collective-permute-start.4 = (bf16[1,64,512]{2,1,0:T(8,128)(2,1)S(1)}, bf16[1,64,512]{2,1,0:T(8,128)(2,1)S(1)}, u32[]{:S(2)}, u32[]{:S(2)}) collective-permute-start(bf16[1,64,512]{2,1,0:T(8,128)(2,1)S(1)} %add_convert_fusion.8), channel_id=1, source_target_pairs={{0,8},{1,9},{2,10},{3,11},{4,12},{5,13},{6,14},{7,15},{8,0},{9,1},... | collective-permute-start | bytes 196616 | tf_op jit(solution)/shard_map/ppermute | solution.py:301
  18.2 2.1 %collective-permute-done.3 = bf16[2,64,512]{2,1,0:T(8,128)(2,1)S(1)} collective-permute-done((bf16[2,64,512]{2,1,0:T(8,128)(2,1)S(1)}, bf16[2,64,512]{2,1,0:T(8,128)(2,1)S(1)}, u32[]{:S(2)}, u32[]{:S(2)}) %collective-permute-start.3) | collective-permute-done | bytes 131104 | tf_op jit(solution)/shard_map/ppermute | solution.py:301
  20.3 1.6 %collective-permute-start.5 = (bf16[64,512]{1,0:T(8,128)(2,1)S(1)}, bf16[64,512]{1,0:T(8,128)(2,1)S(1)}, u32[]{:S(2)}, u32[]{:S(2)}) collective-permute-start(bf16[64,512]{1,0:T(8,128)(2,1)S(1)} %get-tuple-element.23), channel_id=1, source_target_pairs={{0,4},{1,13},{2,6},{3,15},{4,8},{5,1},{6,10},{7,3},{8,12},{9,5},{1... | collective-permute-start | bytes 196616 | tf_op jit(solution)/shard_map/ppermute | solution.py:301
  21.9 0.8 %collective-permute-start.6 = (bf16[64,512]{1,0:T(8,128)(2,1)S(1)}, bf16[64,512]{1,0:T(8,128)(2,1)S(1)}, u32[]{:S(2)}, u32[]{:S(2)}) collective-permute-start(bf16[64,512]{1,0:T(8,128)(2,1)S(1)} %get-tuple-element.24), channel_id=1, source_target_pairs={{0,12},{1,5},{2,14},{3,7},{4,0},{5,9},{6,2},{7,11},{8,4},{9,13},{1... | collective-permute-start | bytes 196616 | tf_op jit(solution)/shard_map/ppermute | solution.py:301
  22.7 2.8 %collective-permute-done.5 = bf16[64,512]{1,0:T(8,128)(2,1)S(1)} collective-permute-done((bf16[64,512]{1,0:T(8,128)(2,1)S(1)}, bf16[64,512]{1,0:T(8,128)(2,1)S(1)}, u32[]{:S(2)}, u32[]{:S(2)}) %collective-permute-start.5) | collective-permute-done | bytes 65568 | tf_op jit(solution)/shard_map/ppermute | solution.py:301
  25.5 2.0 %collective-permute-done.6 = bf16[64,512]{1,0:T(8,128)(2,1)S(1)} collective-permute-done((bf16[64,512]{1,0:T(8,128)(2,1)S(1)}, bf16[64,512]{1,0:T(8,128)(2,1)S(1)}, u32[]{:S(2)}, u32[]{:S(2)}) %collective-permute-start.6) | collective-permute-done | bytes 65568 | tf_op jit(solution)/shard_map/ppermute | solution.py:301
  27.6 2.8 %collective-permute-start.7 = (bf16[64,512]{1,0:T(8,128)(2,1)S(1)}, bf16[64,512]{1,0:T(8,128)(2,1)S(1)}, u32[]{:S(2)}, u32[]{:S(2)}) collective-permute-start(bf16[64,512]{1,0:T(8,128)(2,1)S(1)} %fusion.1), channel_id=1, source_target_pairs={{0,48},{16,0},{32,16},{48,32},{1,49},{17,1},{33,17},{49,33},{2,50}... | collective-permute-start | bytes 196616 | tf_op jit(solution)/shard_map/ppermute | solution.py:376
  30.7 0.7 %collective-permute-start.9 = (bf16[64,512]{1,0:T(8,128)(2,1)S(1)}, bf16[64,512]{1,0:T(8,128)(2,1)S(1)}, u32[]{:S(2)}, u32[]{:S(2)}) collective-permute-start(bf16[64,512]{1,0:T(8,128)(2,1)S(1)} %fusion.1), channel_id=1, source_target_pairs={{0,16},{16,32},{32,48},{48,0},{1,17},{17,33},{33,49},{49,1},{2,18}... | collective-permute-start | bytes 196616 | tf_op jit(solution)/shard_map/ppermute | solution.py:376
  31.7 3.4 %collective-permute-done.8 = bf16[64,512]{1,0:T(8,128)(2,1)S(1)} collective-permute-done((bf16[64,512]{1,0:T(8,128)(2,1)S(1)}, bf16[64,512]{1,0:T(8,128)(2,1)S(1)}, u32[]{:S(2)}, u32[]{:S(2)}) %collective-permute-start.8) | collective-permute-done | bytes 65568 | tf_op jit(solution)/shard_map/ppermute | solution.py:376
  35.1 1.8 %collective-permute-done.9 = bf16[64,512]{1,0:T(8,128)(2,1)S(1)} collective-permute-done((bf16[64,512]{1,0:T(8,128)(2,1)S(1)}, bf16[64,512]{1,0:T(8,128)(2,1)S(1)}, u32[]{:S(2)}, u32[]{:S(2)}) %collective-permute-start.9) | collective-permute-done | bytes 65568 | tf_op jit(solution)/shard_map/ppermute | solution.py:376
  37.2 2.2 %collective-permute-start.11 = (bf16[1,64,512]{2,1,0:T(8,128)(2,1)S(1)}, bf16[1,64,512]{2,1,0:T(8,128)(2,1)S(1)}, u32[]{:S(2)}, u32[]{:S(2)}) collective-permute-start(bf16[1,64,512]{2,1,0:T(8,128)(2,1)S(1)} %fusion.4.refs_1_), channel_id=1, source_target_pairs={{0,12},{1,5},{2,14},{3,7},{4,0},{5,9},{6,2},{7,11},{8,4},{9,13},{1... | collective-permute-start | bytes 196616 | tf_op jit(solution)/shard_map/ppermute | solution.py:301
  39.3 2.3 %collective-permute-done.10.refs_0_ = bf16[1,64,512]{2,1,0:T(8,128)(2,1)S(1)} collective-permute-done((bf16[1,64,512]{2,1,0:T(8,128)(2,1)S(1)}, bf16[1,64,512]{2,1,0:T(8,128)(2,1)S(1)}, u32[]{:S(2)}, u32[]{:S(2)}) %collective-permute-start.10) | collective-permute-done | bytes 65568 | tf_op jit(solution)/shard_map/ppermute | solution.py:301
  41.7 0.8 %collective-permute-done.11.refs_2_ = bf16[1,64,512]{2,1,0:T(8,128)(2,1)S(1)} collective-permute-done((bf16[1,64,512]{2,1,0:T(8,128)(2,1)S(1)}, bf16[1,64,512]{2,1,0:T(8,128)(2,1)S(1)}, u32[]{:S(2)}, u32[]{:S(2)}) %collective-permute-start.11) | collective-permute-done | bytes 65568 | tf_op jit(solution)/shard_map/ppermute | solution.py:301
  42.9 3.1 %collective-permute-start.14 = (bf16[2,64,512]{2,1,0:T(8,128)(2,1)S(1)}, bf16[2,64,512]{2,1,0:T(8,128)(2,1)S(1)}, u32[]{:S(2)}, u32[]{:S(2)}) collective-permute-start(bf16[2,64,512]{2,1,0:T(8,128)(2,1)S(1)} %get-tuple-element.25), channel_id=1, source_target_pairs={{0,14},{1,3},{2,0},{3,5},{4,2},{5,7},{6,4},{7,9},{8,6},{9,11},{10,... | collective-permute-start | bytes 393224 | tf_op jit(solution)/shard_map/ppermute | solution.py:301
  46.0 0.5 collective-permute-done.12.refs_3_
  46.5 5.6 %collective-permute-start.16 = (bf16[3,64,512]{2,1,0:T(8,128)(2,1)S(1)}, bf16[3,64,512]{2,1,0:T(8,128)(2,1)S(1)}, u32[]{:S(2)}, u32[]{:S(2)}) collective-permute-start(bf16[3,64,512]{2,1,0:T(8,128)(2,1)S(1)} %pad_maximum_fusion), channel_id=1, source_target_pairs={{0,1},{1,0},{2,3},{3,2},{4,5},{5,4},{6,7},{7,6},{8,9},{9,8},{10,11... | collective-permute-start | bytes 589832 | tf_op jit(solution)/shard_map/ppermute | solution.py:392
  52.1 2.7 %collective-permute-start.17 = (bf16[2,64,512]{2,1,0:T(8,128)(2,1)S(1)}, bf16[2,64,512]{2,1,0:T(8,128)(2,1)S(1)}, u32[]{:S(2)}, u32[]{:S(2)}) collective-permute-start(bf16[2,64,512]{2,1,0:T(8,128)(2,1)S(1)} %collective-permute-done.13.refs_4_), channel_id=1, source_target_pairs={{0,1},{1,0},{2,3},{3,2},{4,5},{5,4},{6,7},{7,6},{8,9},{9,8},{10,11... | collective-permute-start | bytes 393224 | tf_op jit(solution)/shard_map/ppermute | solution.py:392
  54.8 0.7 %collective-permute-start.18 = (bf16[2,64,512]{2,1,0:T(8,128)(2,1)S(1)}, bf16[2,64,512]{2,1,0:T(8,128)(2,1)S(1)}, u32[]{:S(2)}, u32[]{:S(2)}) collective-permute-start(bf16[2,64,512]{2,1,0:T(8,128)(2,1)S(1)} %collective-permute-done.14.refs_5_), channel_id=1, source_target_pairs={{0,1},{1,0},{2,3},{3,2},{4,5},{5,4},{6,7},{7,6},{8,9},{9,8},{10,11... | collective-permute-start | bytes 393224 | tf_op jit(solution)/shard_map/ppermute | solution.py:392
  55.5 1.3 %collective-permute-done.15.refs_6_ = bf16[1,64,512]{2,1,0:T(8,128)(2,1)S(1)} collective-permute-done((bf16[1,64,512]{2,1,0:T(8,128)(2,1)S(1)}, bf16[1,64,512]{2,1,0:T(8,128)(2,1)S(1)}, u32[]{:S(2)}, u32[]{:S(2)}) %collective-permute-start.15) | collective-permute-done | bytes 65568 | tf_op jit(solution)/shard_map/ppermute | solution.py:392
  56.8 1.1 %assemble.1 = bf16[64,8192]{1,0:T(8,128)(2,1)} custom-call(s32[1]{0:T(128)} %bitcast.core_ref, s32[1]{0:T(128)} %bitcast.1.chip_ref, bf16[1,64,512]{2,1,0:T(8,128)(2,1)S(1)} %collective-permute-done.10.refs_0_, bf16[1,64,512]{2,1,0:T(8,128)(2,1)S(1)} %fusion.4.refs_1_, bf16[1,64,512]{2,1,0:T(8,128)(2,1)S(1)} %collective-permute-done.11.refs_2_, ...), custom_call_target="tpu_custom_call" | custom-call | tf_op jit(solution)/shard_map/assemble/pallas_call | solution.py:395
  (24 shorter events, 1.7 us)
Async XLA Ops:
  6.7 4.5 %collective-permute-start.1 = (bf16[4,64,512]{2,1,0:T(8,128)(2,1)S(1)}, bf16[4,64,512]{2,1,0:T(8,128)(2,1)S(1)}, u32[]{:S(2)}, u32[]{:S(2)}) collective-permute-start(bf16[4,64,512]{2,1,0:T(8,128)(2,1)S(1)} %get-tuple-element.17), channel_id=1, source_target_pairs={{0,1},{1,0},{2,3},{3,2},{4,5},{5,4},{6,7},{7,6},{8,9},{9,8},{10,11... | collective-permute-start | bytes 786440 | tf_op jit(solution)/shard_map/ppermute | solution.py:355
  10.1 5.2 %collective-permute-start = (bf16[4,64,512]{2,1,0:T(8,128)(2,1)S(1)}, bf16[4,64,512]{2,1,0:T(8,128)(2,1)S(1)}, u32[]{:S(2)}, u32[]{:S(2)}) collective-permute-start(bf16[4,64,512]{2,1,0:T(8,128)(2,1)S(1)} %get-tuple-element.15), channel_id=1, source_target_pairs={{0,1},{1,0},{2,3},{3,2},{4,5},{5,4},{6,7},{7,6},{8,9},{9,8},{10,11... | collective-permute-start | bytes 786440 | tf_op jit(solution)/shard_map/ppermute | solution.py:356
  11.3 6.9 %collective-permute-start.2 = (bf16[2,64,512]{2,1,0:T(8,128)(2,1)S(1)}, bf16[2,64,512]{2,1,0:T(8,128)(2,1)S(1)}, u32[]{:S(2)}, u32[]{:S(2)}) collective-permute-start(bf16[2,64,512]{2,1,0:T(8,128)(2,1)S(1)} %get-tuple-element.18), channel_id=1, source_target_pairs={{0,2},{1,15},{2,4},{3,1},{4,6},{5,3},{6,8},{7,5},{8,10},{9,7},{10,... | collective-permute-start | bytes 393224 | tf_op jit(solution)/shard_map/ppermute | solution.py:301
  15.2 5.0 %collective-permute-start.3 = (bf16[2,64,512]{2,1,0:T(8,128)(2,1)S(1)}, bf16[2,64,512]{2,1,0:T(8,128)(2,1)S(1)}, u32[]{:S(2)}, u32[]{:S(2)}) collective-permute-start(bf16[2,64,512]{2,1,0:T(8,128)(2,1)S(1)} %get-tuple-element.19), channel_id=1, source_target_pairs={{0,14},{1,3},{2,0},{3,5},{4,2},{5,7},{6,4},{7,9},{8,6},{9,11},{10,... | collective-permute-start | bytes 393224 | tf_op jit(solution)/shard_map/ppermute | solution.py:301
  15.3 7.4 %collective-permute-start.4 = (bf16[1,64,512]{2,1,0:T(8,128)(2,1)S(1)}, bf16[1,64,512]{2,1,0:T(8,128)(2,1)S(1)}, u32[]{:S(2)}, u32[]{:S(2)}) collective-permute-start(bf16[1,64,512]{2,1,0:T(8,128)(2,1)S(1)} %add_convert_fusion.8), channel_id=1, source_target_pairs={{0,8},{1,9},{2,10},{3,11},{4,12},{5,13},{6,14},{7,15},{8,0},{9,1},... | collective-permute-start | bytes 196616 | tf_op jit(solution)/shard_map/ppermute | solution.py:301
  20.3 5.2 %collective-permute-start.5 = (bf16[64,512]{1,0:T(8,128)(2,1)S(1)}, bf16[64,512]{1,0:T(8,128)(2,1)S(1)}, u32[]{:S(2)}, u32[]{:S(2)}) collective-permute-start(bf16[64,512]{1,0:T(8,128)(2,1)S(1)} %get-tuple-element.23), channel_id=1, source_target_pairs={{0,4},{1,13},{2,6},{3,15},{4,8},{5,1},{6,10},{7,3},{8,12},{9,5},{1... | collective-permute-start | bytes 196616 | tf_op jit(solution)/shard_map/ppermute | solution.py:301
  21.9 5.6 %collective-permute-start.6 = (bf16[64,512]{1,0:T(8,128)(2,1)S(1)}, bf16[64,512]{1,0:T(8,128)(2,1)S(1)}, u32[]{:S(2)}, u32[]{:S(2)}) collective-permute-start(bf16[64,512]{1,0:T(8,128)(2,1)S(1)} %get-tuple-element.24), channel_id=1, source_target_pairs={{0,12},{1,5},{2,14},{3,7},{4,0},{5,9},{6,2},{7,11},{8,4},{9,13},{1... | collective-permute-start | bytes 196616 | tf_op jit(solution)/shard_map/ppermute | solution.py:301
  27.6 4.1 %collective-permute-start.7 = (bf16[64,512]{1,0:T(8,128)(2,1)S(1)}, bf16[64,512]{1,0:T(8,128)(2,1)S(1)}, u32[]{:S(2)}, u32[]{:S(2)}) collective-permute-start(bf16[64,512]{1,0:T(8,128)(2,1)S(1)} %fusion.1), channel_id=1, source_target_pairs={{0,48},{16,0},{32,16},{48,32},{1,49},{17,1},{33,17},{49,33},{2,50}... | collective-permute-start | bytes 196616 | tf_op jit(solution)/shard_map/ppermute | solution.py:376
  30.4 4.7 %collective-permute-start.8 = (bf16[64,512]{1,0:T(8,128)(2,1)S(1)}, bf16[64,512]{1,0:T(8,128)(2,1)S(1)}, u32[]{:S(2)}, u32[]{:S(2)}) collective-permute-start(bf16[64,512]{1,0:T(8,128)(2,1)S(1)} %fusion.1), channel_id=1, source_target_pairs={{0,32},{16,48},{32,0},{48,16},{1,33},{17,49},{33,1},{49,17},{2,34}... | collective-permute-start | bytes 196616 | tf_op jit(solution)/shard_map/ppermute | solution.py:376
  30.7 6.1 %collective-permute-start.9 = (bf16[64,512]{1,0:T(8,128)(2,1)S(1)}, bf16[64,512]{1,0:T(8,128)(2,1)S(1)}, u32[]{:S(2)}, u32[]{:S(2)}) collective-permute-start(bf16[64,512]{1,0:T(8,128)(2,1)S(1)} %fusion.1), channel_id=1, source_target_pairs={{0,16},{16,32},{32,48},{48,0},{1,17},{17,33},{33,49},{49,1},{2,18}... | collective-permute-start | bytes 196616 | tf_op jit(solution)/shard_map/ppermute | solution.py:376
  36.9 4.8 %collective-permute-start.10 = (bf16[1,64,512]{2,1,0:T(8,128)(2,1)S(1)}, bf16[1,64,512]{2,1,0:T(8,128)(2,1)S(1)}, u32[]{:S(2)}, u32[]{:S(2)}) collective-permute-start(bf16[1,64,512]{2,1,0:T(8,128)(2,1)S(1)} %fusion.4.refs_1_), channel_id=1, source_target_pairs={{0,4},{1,13},{2,6},{3,15},{4,8},{5,1},{6,10},{7,3},{8,12},{9,5},{1... | collective-permute-start | bytes 196616 | tf_op jit(solution)/shard_map/ppermute | solution.py:301
  37.2 5.3 %collective-permute-start.11 = (bf16[1,64,512]{2,1,0:T(8,128)(2,1)S(1)}, bf16[1,64,512]{2,1,0:T(8,128)(2,1)S(1)}, u32[]{:S(2)}, u32[]{:S(2)}) collective-permute-start(bf16[1,64,512]{2,1,0:T(8,128)(2,1)S(1)} %fusion.4.refs_1_), channel_id=1, source_target_pairs={{0,12},{1,5},{2,14},{3,7},{4,0},{5,9},{6,2},{7,11},{8,4},{9,13},{1... | collective-permute-start | bytes 196616 | tf_op jit(solution)/shard_map/ppermute | solution.py:301
  39.3 7.1 %collective-permute-start.12 = (bf16[1,64,512]{2,1,0:T(8,128)(2,1)S(1)}, bf16[1,64,512]{2,1,0:T(8,128)(2,1)S(1)}, u32[]{:S(2)}, u32[]{:S(2)}) collective-permute-start(bf16[1,64,512]{2,1,0:T(8,128)(2,1)S(1)} %fusion.4.refs_1_), channel_id=1, source_target_pairs={{0,8},{1,9},{2,10},{3,11},{4,12},{5,13},{6,14},{7,15},{8,0},{9,1},... | collective-permute-start | bytes 196616 | tf_op jit(solution)/shard_map/ppermute | solution.py:301
  42.5 9.6 %collective-permute-start.13 = (bf16[2,64,512]{2,1,0:T(8,128)(2,1)S(1)}, bf16[2,64,512]{2,1,0:T(8,128)(2,1)S(1)}, u32[]{:S(2)}, u32[]{:S(2)}) collective-permute-start(bf16[2,64,512]{2,1,0:T(8,128)(2,1)S(1)} %get-tuple-element.26), channel_id=1, source_target_pairs={{0,2},{1,15},{2,4},{3,1},{4,6},{5,3},{6,8},{7,5},{8,10},{9,7},{10,... | collective-permute-start | bytes 393224 | tf_op jit(solution)/shard_map/ppermute | solution.py:301
  42.9 12.0 %collective-permute-start.14 = (bf16[2,64,512]{2,1,0:T(8,128)(2,1)S(1)}, bf16[2,64,512]{2,1,0:T(8,128)(2,1)S(1)}, u32[]{:S(2)}, u32[]{:S(2)}) collective-permute-start(bf16[2,64,512]{2,1,0:T(8,128)(2,1)S(1)} %get-tuple-element.25), channel_id=1, source_target_pairs={{0,14},{1,3},{2,0},{3,5},{4,2},{5,7},{6,4},{7,9},{8,6},{9,11},{10,... | collective-permute-start | bytes 393224 | tf_op jit(solution)/shard_map/ppermute | solution.py:301
  46.5 10.3 %collective-permute-start.16 = (bf16[3,64,512]{2,1,0:T(8,128)(2,1)S(1)}, bf16[3,64,512]{2,1,0:T(8,128)(2,1)S(1)}, u32[]{:S(2)}, u32[]{:S(2)}) collective-permute-start(bf16[3,64,512]{2,1,0:T(8,128)(2,1)S(1)} %pad_maximum_fusion), channel_id=1, source_target_pairs={{0,1},{1,0},{2,3},{3,2},{4,5},{5,4},{6,7},{7,6},{8,9},{9,8},{10,11... | collective-permute-start | bytes 589832 | tf_op jit(solution)/shard_map/ppermute | solution.py:392
  52.1 4.7 %collective-permute-start.17 = (bf16[2,64,512]{2,1,0:T(8,128)(2,1)S(1)}, bf16[2,64,512]{2,1,0:T(8,128)(2,1)S(1)}, u32[]{:S(2)}, u32[]{:S(2)}) collective-permute-start(bf16[2,64,512]{2,1,0:T(8,128)(2,1)S(1)} %collective-permute-done.13.refs_4_), channel_id=1, source_target_pairs={{0,1},{1,0},{2,3},{3,2},{4,5},{5,4},{6,7},{7,6},{8,9},{9,8},{10,11... | collective-permute-start | bytes 393224 | tf_op jit(solution)/shard_map/ppermute | solution.py:392
  54.8 1.9 %collective-permute-start.18 = (bf16[2,64,512]{2,1,0:T(8,128)(2,1)S(1)}, bf16[2,64,512]{2,1,0:T(8,128)(2,1)S(1)}, u32[]{:S(2)}, u32[]{:S(2)}) collective-permute-start(bf16[2,64,512]{2,1,0:T(8,128)(2,1)S(1)} %collective-permute-done.14.refs_5_), channel_id=1, source_target_pairs={{0,1},{1,0},{2,3},{3,2},{4,5},{5,4},{6,7},{7,6},{8,9},{9,8},{10,11... | collective-permute-start | bytes 393224 | tf_op jit(solution)/shard_map/ppermute | solution.py:392
  55.5 1.3 %collective-permute-start.15 = (bf16[1,64,512]{2,1,0:T(8,128)(2,1)S(1)}, bf16[1,64,512]{2,1,0:T(8,128)(2,1)S(1)}, u32[]{:S(2)}, u32[]{:S(2)}) collective-permute-start(bf16[1,64,512]{2,1,0:T(8,128)(2,1)S(1)} %fusion.4.refs_1_), channel_id=1, source_target_pairs={{0,1},{1,0},{2,3},{3,2},{4,5},{5,4},{6,7},{7,6},{8,9},{9,8},{10,11... | collective-permute-start | bytes 196616 | tf_op jit(solution)/shard_map/ppermute | solution.py:392

commit v8 on v6

--- a/solution.py
+++ b/solution.py
@@ -217,8 +217,7 @@
     (False, (-3, -1)),
     (False, (3, 1)),
     (True, (-2, 0, 2, 4)),
-    (True, (-3, -1)),
-    (True, (3, 1)),
+    (True, (-3, -1, 3, 1)),
 )
 
 
@@ -376,7 +375,7 @@
     pieces = [below, mine, above, across, up, down]
     pieces += [
         lax.ppermute(piece, "core", SWAP)
-        for piece in (jnp.concatenate([below, mine, above, across]), up, down)
+        for piece in (jnp.concatenate([below, mine, above, across]), jnp.concatenate([up, down]))
     ]
     states = pl.pallas_call(
         assemble,

time: 57.6 us -> 57.9 us (level)
    ppermute x3 -> x2, waiting for transfers between devices: 0.99 us -> 1.16 us  [per_device(): lax.ppermute(piece, 'core', SWAP)]
    ppermute x3 -> x2, starting transfers between devices: 6.83 us -> 6.92 us  [per_device(): lax.ppermute(piece, 'core', SWAP)]
  transfers between devices with their start and end apart: 17 -> 16, of which waited for: 10 -> 10; matrix products, arithmetic and copies ran while one was open for 0% -> 0% of each run, Pallas kernels for 0% -> 0%
where the time goes in v8:
time: 57.9 us
  starting transfers between devices  30.3 us (52%)
  waiting for transfers between devices  19.3 us (33%)
  Pallas kernels  7.81 us (13%)
    ppermute x10, starting transfers between devices, shift(): return lax.ppermute(array, ('z', 'core'), pairs)  16.2 us
    ppermute x10, waiting for transfers between devices, shift(): return lax.ppermute(array, ('z', 'core'), pairs)  11.9 us
    ppermute x2, starting transfers between devices, per_device(): lax.ppermute(piece, 'core', SWAP)  6.92 us
    pallas_call x1, Pallas kernels, per_device(): pl.pallas_call(attend, out_shape=(jax.ShapeDtypeStruct((chips, flat, shar...  6.73 us
    ppermute x3, waiting for transfers between devices, per_device(): lax.ppermute(update, 'section', [(i, (i + by) % sections) for i in range(...  4.74 us
    ppermute x3, starting transfers between devices, per_device(): lax.ppermute(update, 'section', [(i, (i + by) % sections) for i in range(...  3.85 us
    ppermute x1, starting transfers between devices, per_device(): got = lax.ppermute(send, 'core', SWAP)  3.33 us
    ppermute x1, waiting for transfers between devices, per_device(): got = lax.ppermute(send, 'core', SWAP)  1.54 us
  transfers between devices with their start and end apart: 16, of which 10 were waited for; matrix products, arithmetic and copies ran while one was open for 0% of the time, Pallas kernels for 0%

profile of v8, /device:TPU:1, one launch (start us, length us, event | category | flops | bytes accessed | tf_op | source)
XLA Modules:
  0.0 57.9 jit_solution(6767735467111016767)
XLA Ops:
  0.0 6.7 %attend.1 = (bf16[8,64,512]{2,1,0:T(8,128)(2,1)S(1)}, f32[8,64,512]{2,1,0:T(8,128)S(1)}, bf16[64,512]{1,0:T(8,128)(2,1)S(1)}) custom-call(s32[1]{0:T(128)} %bitcast.core_ref, s32[1]{0:T(128)} %bitcast.1.chip_ref, s32[32]{0:T(128)} %length_hbm.1, s32[32]{0:T(128)} %position_hbm.1, f32[1,128]{1,0:T(1,128)} %constant.25.clone.rate_hbm, ...), custom_call_target="tpu_custom_call" | custom-call | tf_op jit(solution)/shard_map/attend/pallas_call | solution.py:294
  6.7 3.3 %collective-permute-start = (bf16[8,64,512]{2,1,0:T(8,128)(2,1)S(1)}, bf16[8,64,512]{2,1,0:T(8,128)(2,1)S(1)}, u32[]{:S(2)}, u32[]{:S(2)}) collective-permute-start(bf16[8,64,512]{2,1,0:T(8,128)(2,1)S(1)} %get-tuple-element.14), channel_id=1, source_target_pairs={{0,1},{1,0},{2,3},{3,2},{4,5},{5,4},{6,7},{7,6},{8,9},{9,8},{10,11... | collective-permute-start | bytes 1572872 | tf_op jit(solution)/shard_map/ppermute | solution.py:345
  10.1 1.5 %collective-permute-done = bf16[8,64,512]{2,1,0:T(8,128)(2,1)S(1)} collective-permute-done((bf16[8,64,512]{2,1,0:T(8,128)(2,1)S(1)}, bf16[8,64,512]{2,1,0:T(8,128)(2,1)S(1)}, u32[]{:S(2)}, u32[]{:S(2)}) %collective-permute-start) | collective-permute-done | bytes 524320 | tf_op jit(solution)/shard_map/ppermute | solution.py:345
  11.8 3.9 %collective-permute-start.1 = (bf16[2,64,512]{2,1,0:T(8,128)(2,1)S(1)}, bf16[2,64,512]{2,1,0:T(8,128)(2,1)S(1)}, u32[]{:S(2)}, u32[]{:S(2)}) collective-permute-start(bf16[2,64,512]{2,1,0:T(8,128)(2,1)S(1)} %get-tuple-element.16), channel_id=1, source_target_pairs={{0,2},{1,15},{2,4},{3,1},{4,6},{5,3},{6,8},{7,5},{8,10},{9,7},{10,... | collective-permute-start | bytes 393224 | tf_op jit(solution)/shard_map/ppermute | solution.py:292
  15.7 2.8 %collective-permute-start.3 = (bf16[1,64,512]{2,1,0:T(8,128)(2,1)S(1)}, bf16[1,64,512]{2,1,0:T(8,128)(2,1)S(1)}, u32[]{:S(2)}, u32[]{:S(2)}) collective-permute-start(bf16[1,64,512]{2,1,0:T(8,128)(2,1)S(1)} %add_convert_fusion.8), channel_id=1, source_target_pairs={{0,8},{1,9},{2,10},{3,11},{4,12},{5,13},{6,14},{7,15},{8,0},{9,1},... | collective-permute-start | bytes 196616 | tf_op jit(solution)/shard_map/ppermute | solution.py:292
  18.5 2.2 %collective-permute-done.2 = bf16[2,64,512]{2,1,0:T(8,128)(2,1)S(1)} collective-permute-done((bf16[2,64,512]{2,1,0:T(8,128)(2,1)S(1)}, bf16[2,64,512]{2,1,0:T(8,128)(2,1)S(1)}, u32[]{:S(2)}, u32[]{:S(2)}) %collective-permute-start.2) | collective-permute-done | bytes 131104 | tf_op jit(solution)/shard_map/ppermute | solution.py:292
  20.7 1.6 %collective-permute-start.4 = (bf16[64,512]{1,0:T(8,128)(2,1)S(1)}, bf16[64,512]{1,0:T(8,128)(2,1)S(1)}, u32[]{:S(2)}, u32[]{:S(2)}) collective-permute-start(bf16[64,512]{1,0:T(8,128)(2,1)S(1)} %get-tuple-element.21), channel_id=1, source_target_pairs={{0,4},{1,13},{2,6},{3,15},{4,8},{5,1},{6,10},{7,3},{8,12},{9,5},{1... | collective-permute-start | bytes 196616 | tf_op jit(solution)/shard_map/ppermute | solution.py:292
  22.4 0.8 %collective-permute-start.5 = (bf16[64,512]{1,0:T(8,128)(2,1)S(1)}, bf16[64,512]{1,0:T(8,128)(2,1)S(1)}, u32[]{:S(2)}, u32[]{:S(2)}) collective-permute-start(bf16[64,512]{1,0:T(8,128)(2,1)S(1)} %get-tuple-element.22), channel_id=1, source_target_pairs={{0,12},{1,5},{2,14},{3,7},{4,0},{5,9},{6,2},{7,11},{8,4},{9,13},{1... | collective-permute-start | bytes 196616 | tf_op jit(solution)/shard_map/ppermute | solution.py:292
  23.2 2.6 %collective-permute-done.4 = bf16[64,512]{1,0:T(8,128)(2,1)S(1)} collective-permute-done((bf16[64,512]{1,0:T(8,128)(2,1)S(1)}, bf16[64,512]{1,0:T(8,128)(2,1)S(1)}, u32[]{:S(2)}, u32[]{:S(2)}) %collective-permute-start.4) | collective-permute-done | bytes 65568 | tf_op jit(solution)/shard_map/ppermute | solution.py:292
  25.8 2.2 %collective-permute-done.5 = bf16[64,512]{1,0:T(8,128)(2,1)S(1)} collective-permute-done((bf16[64,512]{1,0:T(8,128)(2,1)S(1)}, bf16[64,512]{1,0:T(8,128)(2,1)S(1)}, u32[]{:S(2)}, u32[]{:S(2)}) %collective-permute-start.5) | collective-permute-done | bytes 65568 | tf_op jit(solution)/shard_map/ppermute | solution.py:292
  28.1 2.8 %collective-permute-start.6 = (bf16[64,512]{1,0:T(8,128)(2,1)S(1)}, bf16[64,512]{1,0:T(8,128)(2,1)S(1)}, u32[]{:S(2)}, u32[]{:S(2)}) collective-permute-start(bf16[64,512]{1,0:T(8,128)(2,1)S(1)} %fusion.1), channel_id=1, source_target_pairs={{0,48},{16,0},{32,16},{48,32},{1,49},{17,1},{33,17},{49,33},{2,50}... | collective-permute-start | bytes 196616 | tf_op jit(solution)/shard_map/ppermute | solution.py:361
  30.9 0.4 collective-permute-start.7
  31.2 0.7 %collective-permute-start.8 = (bf16[64,512]{1,0:T(8,128)(2,1)S(1)}, bf16[64,512]{1,0:T(8,128)(2,1)S(1)}, u32[]{:S(2)}, u32[]{:S(2)}) collective-permute-start(bf16[64,512]{1,0:T(8,128)(2,1)S(1)} %fusion.1), channel_id=1, source_target_pairs={{0,16},{16,32},{32,48},{48,0},{1,17},{17,33},{33,49},{49,1},{2,18}... | collective-permute-start | bytes 196616 | tf_op jit(solution)/shard_map/ppermute | solution.py:361
  32.2 3.4 %collective-permute-done.7 = bf16[64,512]{1,0:T(8,128)(2,1)S(1)} collective-permute-done((bf16[64,512]{1,0:T(8,128)(2,1)S(1)}, bf16[64,512]{1,0:T(8,128)(2,1)S(1)}, u32[]{:S(2)}, u32[]{:S(2)}) %collective-permute-start.7) | collective-permute-done | bytes 65568 | tf_op jit(solution)/shard_map/ppermute | solution.py:361
  35.6 1.1 %collective-permute-done.8 = bf16[64,512]{1,0:T(8,128)(2,1)S(1)} collective-permute-done((bf16[64,512]{1,0:T(8,128)(2,1)S(1)}, bf16[64,512]{1,0:T(8,128)(2,1)S(1)}, u32[]{:S(2)}, u32[]{:S(2)}) %collective-permute-start.8) | collective-permute-done | bytes 65568 | tf_op jit(solution)/shard_map/ppermute | solution.py:361
  36.8 3.6 %collective-permute-start.9 = (bf16[1,64,512]{2,1,0:T(8,128)(2,1)S(1)}, bf16[1,64,512]{2,1,0:T(8,128)(2,1)S(1)}, u32[]{:S(2)}, u32[]{:S(2)}) collective-permute-start(bf16[1,64,512]{2,1,0:T(8,128)(2,1)S(1)} %fusion.4.refs_1_), channel_id=1, source_target_pairs={{0,4},{1,13},{2,6},{3,15},{4,8},{5,1},{6,10},{7,3},{8,12},{9,5},{1... | collective-permute-start | bytes 196616 | tf_op jit(solution)/shard_map/ppermute | solution.py:292
  40.4 0.5 collective-permute-start.11
  40.9 1.8 %collective-permute-done.10.refs_2_ = bf16[1,64,512]{2,1,0:T(8,128)(2,1)S(1)} collective-permute-done((bf16[1,64,512]{2,1,0:T(8,128)(2,1)S(1)}, bf16[1,64,512]{2,1,0:T(8,128)(2,1)S(1)}, u32[]{:S(2)}, u32[]{:S(2)}) %collective-permute-start.10) | collective-permute-done | bytes 65568 | tf_op jit(solution)/shard_map/ppermute | solution.py:292
  42.7 2.9 %collective-permute-start.12 = (bf16[2,64,512]{2,1,0:T(8,128)(2,1)S(1)}, bf16[2,64,512]{2,1,0:T(8,128)(2,1)S(1)}, u32[]{:S(2)}, u32[]{:S(2)}) collective-permute-start(bf16[2,64,512]{2,1,0:T(8,128)(2,1)S(1)} %get-tuple-element.24), channel_id=1, source_target_pairs={{0,2},{1,15},{2,4},{3,1},{4,6},{5,3},{6,8},{7,5},{8,10},{9,7},{10,... | collective-permute-start | bytes 393224 | tf_op jit(solution)/shard_map/ppermute | solution.py:292
  45.6 3.0 %collective-permute-done.11.refs_3_ = bf16[1,64,512]{2,1,0:T(8,128)(2,1)S(1)} collective-permute-done((bf16[1,64,512]{2,1,0:T(8,128)(2,1)S(1)}, bf16[1,64,512]{2,1,0:T(8,128)(2,1)S(1)}, u32[]{:S(2)}, u32[]{:S(2)}) %collective-permute-start.11) | collective-permute-done | bytes 65568 | tf_op jit(solution)/shard_map/ppermute | solution.py:292
  48.7 3.4 %collective-permute-start.14 = (bf16[4,64,512]{2,1,0:T(8,128)(2,1)S(1)}, bf16[4,64,512]{2,1,0:T(8,128)(2,1)S(1)}, u32[]{:S(2)}, u32[]{:S(2)}) collective-permute-start(bf16[4,64,512]{2,1,0:T(8,128)(2,1)S(1)} %pad_maximum_fusion), channel_id=1, source_target_pairs={{0,1},{1,0},{2,3},{3,2},{4,5},{5,4},{6,7},{7,6},{8,9},{9,8},{10,11... | collective-permute-start | bytes 786440 | tf_op jit(solution)/shard_map/ppermute | solution.py:377
  52.1 3.5 %collective-permute-start.15 = (bf16[4,64,512]{2,1,0:T(8,128)(2,1)S(1)}, bf16[4,64,512]{2,1,0:T(8,128)(2,1)S(1)}, u32[]{:S(2)}, u32[]{:S(2)}) collective-permute-start(bf16[4,64,512]{2,1,0:T(8,128)(2,1)S(1)} %pad_maximum_fusion.1), channel_id=1, source_target_pairs={{0,1},{1,0},{2,3},{3,2},{4,5},{5,4},{6,7},{7,6},{8,9},{9,8},{10,11... | collective-permute-start | bytes 786440 | tf_op jit(solution)/shard_map/ppermute | solution.py:377
  55.6 1.2 %collective-permute-done.15.refs_7_ = bf16[4,64,512]{2,1,0:T(8,128)(2,1)S(1)} collective-permute-done((bf16[4,64,512]{2,1,0:T(8,128)(2,1)S(1)}, bf16[4,64,512]{2,1,0:T(8,128)(2,1)S(1)}, u32[]{:S(2)}, u32[]{:S(2)}) %collective-permute-start.15) | collective-permute-done | bytes 262176 | tf_op jit(solution)/shard_map/ppermute | solution.py:377
  56.8 1.1 %assemble.1 = bf16[64,8192]{1,0:T(8,128)(2,1)} custom-call(s32[1]{0:T(128)} %bitcast.core_ref, s32[1]{0:T(128)} %bitcast.1.chip_ref, bf16[1,64,512]{2,1,0:T(8,128)(2,1)S(1)} %collective-permute-done.9.refs_0_, bf16[1,64,512]{2,1,0:T(8,128)(2,1)S(1)} %fusion.4.refs_1_, bf16[1,64,512]{2,1,0:T(8,128)(2,1)S(1)} %collective-permute-done.10.refs_2_, ...), custom_call_target="tpu_custom_call" | custom-call | tf_op jit(solution)/shard_map/assemble/pallas_call | solution.py:380
  (19 shorter events, 0.7 us)
Async XLA Ops:
  6.7 4.9 %collective-permute-start = (bf16[8,64,512]{2,1,0:T(8,128)(2,1)S(1)}, bf16[8,64,512]{2,1,0:T(8,128)(2,1)S(1)}, u32[]{:S(2)}, u32[]{:S(2)}) collective-permute-start(bf16[8,64,512]{2,1,0:T(8,128)(2,1)S(1)} %get-tuple-element.14), channel_id=1, source_target_pairs={{0,1},{1,0},{2,3},{3,2},{4,5},{5,4},{6,7},{7,6},{8,9},{9,8},{10,11... | collective-permute-start | bytes 1572872 | tf_op jit(solution)/shard_map/ppermute | solution.py:345
  11.8 6.7 %collective-permute-start.1 = (bf16[2,64,512]{2,1,0:T(8,128)(2,1)S(1)}, bf16[2,64,512]{2,1,0:T(8,128)(2,1)S(1)}, u32[]{:S(2)}, u32[]{:S(2)}) collective-permute-start(bf16[2,64,512]{2,1,0:T(8,128)(2,1)S(1)} %get-tuple-element.16), channel_id=1, source_target_pairs={{0,2},{1,15},{2,4},{3,1},{4,6},{5,3},{6,8},{7,5},{8,10},{9,7},{10,... | collective-permute-start | bytes 393224 | tf_op jit(solution)/shard_map/ppermute | solution.py:292
  15.7 5.0 %collective-permute-start.2 = (bf16[2,64,512]{2,1,0:T(8,128)(2,1)S(1)}, bf16[2,64,512]{2,1,0:T(8,128)(2,1)S(1)}, u32[]{:S(2)}, u32[]{:S(2)}) collective-permute-start(bf16[2,64,512]{2,1,0:T(8,128)(2,1)S(1)} %get-tuple-element.17), channel_id=1, source_target_pairs={{0,14},{1,3},{2,0},{3,5},{4,2},{5,7},{6,4},{7,9},{8,6},{9,11},{10,... | collective-permute-start | bytes 393224 | tf_op jit(solution)/shard_map/ppermute | solution.py:292
  15.7 7.5 %collective-permute-start.3 = (bf16[1,64,512]{2,1,0:T(8,128)(2,1)S(1)}, bf16[1,64,512]{2,1,0:T(8,128)(2,1)S(1)}, u32[]{:S(2)}, u32[]{:S(2)}) collective-permute-start(bf16[1,64,512]{2,1,0:T(8,128)(2,1)S(1)} %add_convert_fusion.8), channel_id=1, source_target_pairs={{0,8},{1,9},{2,10},{3,11},{4,12},{5,13},{6,14},{7,15},{8,0},{9,1},... | collective-permute-start | bytes 196616 | tf_op jit(solution)/shard_map/ppermute | solution.py:292
  20.7 5.1 %collective-permute-start.4 = (bf16[64,512]{1,0:T(8,128)(2,1)S(1)}, bf16[64,512]{1,0:T(8,128)(2,1)S(1)}, u32[]{:S(2)}, u32[]{:S(2)}) collective-permute-start(bf16[64,512]{1,0:T(8,128)(2,1)S(1)} %get-tuple-element.21), channel_id=1, source_target_pairs={{0,4},{1,13},{2,6},{3,15},{4,8},{5,1},{6,10},{7,3},{8,12},{9,5},{1... | collective-permute-start | bytes 196616 | tf_op jit(solution)/shard_map/ppermute | solution.py:292
  22.4 5.7 %collective-permute-start.5 = (bf16[64,512]{1,0:T(8,128)(2,1)S(1)}, bf16[64,512]{1,0:T(8,128)(2,1)S(1)}, u32[]{:S(2)}, u32[]{:S(2)}) collective-permute-start(bf16[64,512]{1,0:T(8,128)(2,1)S(1)} %get-tuple-element.22), channel_id=1, source_target_pairs={{0,12},{1,5},{2,14},{3,7},{4,0},{5,9},{6,2},{7,11},{8,4},{9,13},{1... | collective-permute-start | bytes 196616 | tf_op jit(solution)/shard_map/ppermute | solution.py:292
  28.1 4.1 %collective-permute-start.6 = (bf16[64,512]{1,0:T(8,128)(2,1)S(1)}, bf16[64,512]{1,0:T(8,128)(2,1)S(1)}, u32[]{:S(2)}, u32[]{:S(2)}) collective-permute-start(bf16[64,512]{1,0:T(8,128)(2,1)S(1)} %fusion.1), channel_id=1, source_target_pairs={{0,48},{16,0},{32,16},{48,32},{1,49},{17,1},{33,17},{49,33},{2,50}... | collective-permute-start | bytes 196616 | tf_op jit(solution)/shard_map/ppermute | solution.py:361
  30.9 4.7 %collective-permute-start.7 = (bf16[64,512]{1,0:T(8,128)(2,1)S(1)}, bf16[64,512]{1,0:T(8,128)(2,1)S(1)}, u32[]{:S(2)}, u32[]{:S(2)}) collective-permute-start(bf16[64,512]{1,0:T(8,128)(2,1)S(1)} %fusion.1), channel_id=1, source_target_pairs={{0,32},{16,48},{32,0},{48,16},{1,33},{17,49},{33,1},{49,17},{2,34}... | collective-permute-start | bytes 196616 | tf_op jit(solution)/shard_map/ppermute | solution.py:361
  31.2 5.4 %collective-permute-start.8 = (bf16[64,512]{1,0:T(8,128)(2,1)S(1)}, bf16[64,512]{1,0:T(8,128)(2,1)S(1)}, u32[]{:S(2)}, u32[]{:S(2)}) collective-permute-start(bf16[64,512]{1,0:T(8,128)(2,1)S(1)} %fusion.1), channel_id=1, source_target_pairs={{0,16},{16,32},{32,48},{48,0},{1,17},{17,33},{33,49},{49,1},{2,18}... | collective-permute-start | bytes 196616 | tf_op jit(solution)/shard_map/ppermute | solution.py:361
  36.7 5.9 %collective-permute-start.10 = (bf16[1,64,512]{2,1,0:T(8,128)(2,1)S(1)}, bf16[1,64,512]{2,1,0:T(8,128)(2,1)S(1)}, u32[]{:S(2)}, u32[]{:S(2)}) collective-permute-start(bf16[1,64,512]{2,1,0:T(8,128)(2,1)S(1)} %fusion.4.refs_1_), channel_id=1, source_target_pairs={{0,12},{1,5},{2,14},{3,7},{4,0},{5,9},{6,2},{7,11},{8,4},{9,13},{1... | collective-permute-start | bytes 196616 | tf_op jit(solution)/shard_map/ppermute | solution.py:292
  36.8 5.8 %collective-permute-start.9 = (bf16[1,64,512]{2,1,0:T(8,128)(2,1)S(1)}, bf16[1,64,512]{2,1,0:T(8,128)(2,1)S(1)}, u32[]{:S(2)}, u32[]{:S(2)}) collective-permute-start(bf16[1,64,512]{2,1,0:T(8,128)(2,1)S(1)} %fusion.4.refs_1_), channel_id=1, source_target_pairs={{0,4},{1,13},{2,6},{3,15},{4,8},{5,1},{6,10},{7,3},{8,12},{9,5},{1... | collective-permute-start | bytes 196616 | tf_op jit(solution)/shard_map/ppermute | solution.py:292
  40.4 8.2 %collective-permute-start.11 = (bf16[1,64,512]{2,1,0:T(8,128)(2,1)S(1)}, bf16[1,64,512]{2,1,0:T(8,128)(2,1)S(1)}, u32[]{:S(2)}, u32[]{:S(2)}) collective-permute-start(bf16[1,64,512]{2,1,0:T(8,128)(2,1)S(1)} %fusion.4.refs_1_), channel_id=1, source_target_pairs={{0,8},{1,9},{2,10},{3,11},{4,12},{5,13},{6,14},{7,15},{8,0},{9,1},... | collective-permute-start | bytes 196616 | tf_op jit(solution)/shard_map/ppermute | solution.py:292
  42.7 9.3 %collective-permute-start.12 = (bf16[2,64,512]{2,1,0:T(8,128)(2,1)S(1)}, bf16[2,64,512]{2,1,0:T(8,128)(2,1)S(1)}, u32[]{:S(2)}, u32[]{:S(2)}) collective-permute-start(bf16[2,64,512]{2,1,0:T(8,128)(2,1)S(1)} %get-tuple-element.24), channel_id=1, source_target_pairs={{0,2},{1,15},{2,4},{3,1},{4,6},{5,3},{6,8},{7,5},{8,10},{9,7},{10,... | collective-permute-start | bytes 393224 | tf_op jit(solution)/shard_map/ppermute | solution.py:292
  45.6 6.4 %collective-permute-start.13 = (bf16[2,64,512]{2,1,0:T(8,128)(2,1)S(1)}, bf16[2,64,512]{2,1,0:T(8,128)(2,1)S(1)}, u32[]{:S(2)}, u32[]{:S(2)}) collective-permute-start(bf16[2,64,512]{2,1,0:T(8,128)(2,1)S(1)} %get-tuple-element.23), channel_id=1, source_target_pairs={{0,14},{1,3},{2,0},{3,5},{4,2},{5,7},{6,4},{7,9},{8,6},{9,11},{10,... | collective-permute-start | bytes 393224 | tf_op jit(solution)/shard_map/ppermute | solution.py:292
  48.7 7.0 %collective-permute-start.14 = (bf16[4,64,512]{2,1,0:T(8,128)(2,1)S(1)}, bf16[4,64,512]{2,1,0:T(8,128)(2,1)S(1)}, u32[]{:S(2)}, u32[]{:S(2)}) collective-permute-start(bf16[4,64,512]{2,1,0:T(8,128)(2,1)S(1)} %pad_maximum_fusion), channel_id=1, source_target_pairs={{0,1},{1,0},{2,3},{3,2},{4,5},{5,4},{6,7},{7,6},{8,9},{9,8},{10,11... | collective-permute-start | bytes 786440 | tf_op jit(solution)/shard_map/ppermute | solution.py:377
  52.1 4.7 %collective-permute-start.15 = (bf16[4,64,512]{2,1,0:T(8,128)(2,1)S(1)}, bf16[4,64,512]{2,1,0:T(8,128)(2,1)S(1)}, u32[]{:S(2)}, u32[]{:S(2)}) collective-permute-start(bf16[4,64,512]{2,1,0:T(8,128)(2,1)S(1)} %pad_maximum_fusion.1), channel_id=1, source_target_pairs={{0,1},{1,0},{2,3},{3,2},{4,5},{5,4},{6,7},{7,6},{8,9},{9,8},{10,11... | collective-permute-start | bytes 786440 | tf_op jit(solution)/shard_map/ppermute | solution.py:377
